TPU v7x, 32 devices: a whole 2x2x4 slice. The times are simulated.
32 devices in a mesh: section: 4 (over y, x), dp: 8 (over z, core).
Axes of the slice: x: 2, y: 2, z: 4, core: 2. Of those that a mesh axis runs over, the one named last changes fastest.
Arguments:
- pixels: bfloat16 [16, 1536, 1536], P('dp'), may hold values from -6 to 6
- token_order: int32 [16, 1536], P('dp'), may hold values from 0 to 1535, each once within a row
- visible: int32 [16], P('dp'), may hold values from 192 to 576, as said below
- wide_weight: float32 [1024, 8576], P('dp'), may hold values from -0.1875 to 0.1875
- tall_weight: float32 [5632, 1024], P('dp'), may hold values from -0.09375 to 0.09375
- pred_weight: float32 [384, 4096], P('dp'), may hold values from -0.3125 to 0.3125
- pred_down: float32 [1536, 384], P('dp'), may hold values from -0.15625 to 0.15625
- enc_gains: float32 [1024, 3], P('dp'), may hold values from 0.15 to 5
- pred_gains: float32 [384, 4], P('dp'), may hold values from -3 to 5
- wide_first: float32 [1024, 8576], P('dp'), may hold values from -7.6293945e-06 to 7.6293945e-06
- tall_first: float32 [5632, 1024], P('dp'), may hold values from -7.6293945e-06 to 7.6293945e-06
- pred_first: float32 [384, 4096], P('dp'), may hold values from -7.6293945e-06 to 7.6293945e-06
- pred_down_first: float32 [1536, 384], P('dp'), may hold values from -7.6293945e-06 to 7.6293945e-06
- enc_gains_first: float32 [1024, 3], P('dp'), may hold values from -3.0517578e-05 to 3.0517578e-05
- pred_gains_first: float32 [384, 4], P('dp'), may hold values from -3.0517578e-05 to 3.0517578e-05
- wide_second: float32 [1024, 8576], P('dp'), may hold values from 1.4955474e-13 to 5.9821896e-13
- tall_second: float32 [5632, 1024], P('dp'), may hold values from 1.4955474e-13 to 5.9821896e-13
- pred_second: float32 [384, 4096], P('dp'), may hold values from 1.4955474e-13 to 5.9821896e-13
- pred_down_second: float32 [1536, 384], P('dp'), may hold values from 1.4955474e-13 to 5.9821896e-13
- enc_gains_second: float32 [1024, 3], P('dp'), may hold values from 2.3928758e-12 to 9.571503e-12
- pred_gains_second: float32 [384, 4], P('dp'), may hold values from 2.3928758e-12 to 9.571503e-12
- teacher_wide: float32 [1024, 8192], P('dp'), may hold values from -0.1875 to 0.1875
- teacher_tall: float32 [5632, 1024], P('dp'), may hold values from -0.09375 to 0.09375
- teacher_gains: float32 [1024, 3], P('dp'), may hold values from 0.15 to 5
Outputs:
- loss_sum: float32 [], replicated
- target_count: float32 [], replicated
- grad_norm: float32 [], replicated
- wide_new: float32 [1024, 8576], P('dp')
- tall_new: float32 [5632, 1024], P('dp')
- pred_new: float32 [384, 4096], P('dp')
- pred_down_new: float32 [1536, 384], P('dp')
- enc_gains_new: float32 [1024, 3], P('dp')
- pred_gains_new: float32 [384, 4], P('dp')
- wide_first_new: float32 [1024, 8576], P('dp')
- tall_first_new: float32 [5632, 1024], P('dp')
- pred_first_new: float32 [384, 4096], P('dp')
- pred_down_first_new: float32 [1536, 384], P('dp')
- enc_gains_first_new: float32 [1024, 3], P('dp')
- pred_gains_first_new: float32 [384, 4], P('dp')
- wide_second_new: float32 [1024, 8576], P('dp')
- tall_second_new: float32 [5632, 1024], P('dp')
- pred_second_new: float32 [384, 4096], P('dp')
- pred_down_second_new: float32 [1536, 384], P('dp')
- enc_gains_second_new: float32 [1024, 3], P('dp')
- pred_gains_second_new: float32 [384, 4], P('dp')
- wide_copy: bfloat16 [1024, 8576], P('dp')
- tall_copy: bfloat16 [5632, 1024], P('dp')
- pred_copy: bfloat16 [384, 4096], P('dp')
- pred_down_copy: bfloat16 [1536, 384], P('dp')
- enc_gains_copy: bfloat16 [1024, 3], P('dp')
- pred_gains_copy: bfloat16 [384, 4], P('dp')
- teacher_wide_new: float32 [1024, 8192], P('dp')
- teacher_tall_new: float32 [5632, 1024], P('dp')
- teacher_gains_new: float32 [1024, 3], P('dp')
Inputs may be any that keep to these rules, and one draw needn't show every extreme that they name: Some clip has exactly 576 visible tokens and some clip exactly 192.
All inputs are finite; a program needn't handle non-finite values.
Results may differ from a plain program's by a relative error of at most 0.005.
The roundings to bfloat16 on the way count: a program that leaves them out, or rounds other values in their place, can miss the bound.
Values may be sent and summed in bfloat16 or wider, within the bound.
A program may use at most 640 MiB of HBM per device.

v0:
```python
import math

import jax
import jax.numpy as jnp
from jax import lax
from jax.sharding import PartitionSpec as P

D = 1024
HE = 16
FF = 4096
PD = 384
PH = 12
PF = 1536
PATCH = 1536
L = 1536
MICRO = 2
STEP = 10
VIS = 576


BETA_ONE = 0.9
BETA_TWO = 0.999
EPSILON = 1e-08
RATE = 0.02
GAIN_RATE = 0.5
DECAY = 0.05
CLIP_AT = 0.05
KEEP_RATE = 0.8
NEGATIVE = -1e30


def shortened(x):
    return jax.tree.map(lambda a: a.astype(jnp.bfloat16) if a.dtype == jnp.float32 else a, x)


def passed_along(block, axis, distance):
    devices = range(lax.axis_size(axis))
    route = [(i - distance, i) for i in devices if i - distance in devices]
    return lax.ppermute(block, axis, route)


def normed(stream):
    centred = stream - jnp.mean(stream, axis=-1, keepdims=True)
    return centred * lax.rsqrt(jnp.mean(centred * centred, axis=-1, keepdims=True) + 1e-06)


def scaled(stream, gain_vec):
    return normed(stream) * gain_vec


def position_table(positions, feature_width):
    frequency = jnp.exp(
        jnp.arange(feature_width // 2, dtype=jnp.float32)
        * (-2.0 * math.log(10000.0) / feature_width)
    )
    angles = positions.astype(jnp.float32)[:, None] * frequency[None, :]
    return jnp.concatenate([jnp.sin(angles), jnp.cos(angles)], axis=1)


def matmul(left, right):
    return jnp.dot(left, right, preferred_element_type=jnp.float32)


def inner_rows(left, right):
    return lax.dot_general(
        left, right, (((0,), (0,)), ((), ())), preferred_element_type=jnp.float32
    )


def outer_rows(left, right):
    return lax.dot_general(
        left, right, (((1,), (1,)), ((), ())), preferred_element_type=jnp.float32
    )


def gelu_exact(raised):
    return jax.nn.gelu(raised, approximate=False)


def query_blocks(row_count):
    block_rows = 512 if row_count % 512 == 0 else row_count
    return [(offset, block_rows) for offset in range(0, row_count, block_rows)]


def scores(queries, key_heads, key_keep):
    logits = jnp.einsum(
        "qhd,khd->hqk", queries, key_heads, preferred_element_type=jnp.float32
    ) * queries.shape[2] ** (-0.5)
    if key_keep is None:
        return logits
    return jnp.where(key_keep[None, None, :], logits, NEGATIVE)


def split_heads(packed, num_heads):
    row_count = packed.shape[0]
    feature_width = packed.shape[1] // 3
    head_size = feature_width // num_heads
    return [
        packed[:, member * feature_width : (member + 1) * feature_width].reshape(
            row_count, num_heads, head_size
        )
        for member in range(3)
    ]


def attend_fwd(stream, gain_vec, w_in, w_out, num_heads, key_keep):
    normal_in = scaled(stream, gain_vec).astype(jnp.bfloat16)
    packed = matmul(normal_in, w_in).astype(jnp.bfloat16)
    queries, key_heads, value_heads = split_heads(packed, num_heads)
    outputs = []
    log_totals = []
    for offset, block_rows in query_blocks(stream.shape[0]):
        logits = scores(queries[offset : offset + block_rows], key_heads, key_keep)
        row_max = jnp.max(logits, axis=-1, keepdims=True)
        exp_scores = jnp.exp(logits - row_max)
        row_total = jnp.sum(exp_scores, axis=-1, keepdims=True)
        attn_probs = (exp_scores / row_total).astype(jnp.bfloat16)
        outputs.append(
            jnp.einsum("hqk,khd->qhd", attn_probs, value_heads, preferred_element_type=jnp.float32)
        )
        log_totals.append(row_max + jnp.log(row_total))
    merged = jnp.concatenate(outputs, axis=0).reshape(stream.shape[0], -1).astype(jnp.bfloat16)
    return (stream + matmul(merged, w_out), (normal_in, packed, merged, log_totals))


def attend_back(stream, gain_vec, w_in, w_out, num_heads, key_keep, stored, grad_out):
    normal_in, packed, merged, log_totals = stored
    queries, key_heads, value_heads = split_heads(packed, num_heads)
    scaling = queries.shape[2] ** (-0.5)
    branch_grad = grad_out.astype(jnp.bfloat16)
    grad_wout = inner_rows(merged, branch_grad)
    grad_merged = outer_rows(branch_grad, w_out).astype(jnp.bfloat16).reshape(queries.shape)
    grad_queries = []
    grad_keys = jnp.zeros(key_heads.shape, jnp.float32)
    grad_values = jnp.zeros(value_heads.shape, jnp.float32)
    for (offset, block_rows), log_total in zip(query_blocks(stream.shape[0]), log_totals):
        block_queries = queries[offset : offset + block_rows]
        block_grad = grad_merged[offset : offset + block_rows]
        attn_probs = jnp.exp(scores(block_queries, key_heads, key_keep) - log_total)
        grad_probs = jnp.einsum(
            "qhd,khd->hqk", block_grad, value_heads, preferred_element_type=jnp.float32
        )
        grad_logits = (
            attn_probs * (grad_probs - jnp.sum(grad_probs * attn_probs, axis=-1, keepdims=True))
        ).astype(jnp.bfloat16)
        grad_queries.append(
            jnp.einsum("hqk,khd->qhd", grad_logits, key_heads, preferred_element_type=jnp.float32)
            * scaling
        )
        grad_keys = (
            grad_keys
            + jnp.einsum(
                "hqk,qhd->khd", grad_logits, block_queries, preferred_element_type=jnp.float32
            )
            * scaling
        )
        grad_values = grad_values + jnp.einsum(
            "hqk,qhd->khd",
            attn_probs.astype(jnp.bfloat16),
            block_grad,
            preferred_element_type=jnp.float32,
        )
    row_count = stream.shape[0]
    grad_packed = jnp.concatenate(
        [
            jnp.concatenate(grad_queries, axis=0).reshape(row_count, -1),
            grad_keys.reshape(row_count, -1),
            grad_values.reshape(row_count, -1),
        ],
        axis=1,
    ).astype(jnp.bfloat16)
    grad_win = inner_rows(normal_in, grad_packed)
    grad_normal = outer_rows(grad_packed, w_in).astype(jnp.bfloat16).astype(jnp.float32)
    discarded_value, backward_fn = jax.vjp(scaled, stream, gain_vec)
    grad_stream, grad_gain = backward_fn(grad_normal)
    return (grad_out + grad_stream, grad_win, grad_wout, grad_gain)


def feed_fwd(stream, gain_vec, w_up, w_down):
    normal_in = scaled(stream, gain_vec).astype(jnp.bfloat16)
    raised = matmul(normal_in, w_up)
    hidden = gelu_exact(raised).astype(jnp.bfloat16)
    return (stream + matmul(hidden, w_down), (normal_in, raised, hidden))


def feed_back(stream, gain_vec, w_up, w_down, stored, grad_out):
    normal_in, raised, hidden = stored
    branch_grad = grad_out.astype(jnp.bfloat16)
    grad_wdown = inner_rows(hidden, branch_grad)
    grad_hidden = outer_rows(branch_grad, w_down).astype(jnp.bfloat16).astype(jnp.float32)
    discarded_value, backward_fn = jax.vjp(gelu_exact, raised)
    grad_raised = backward_fn(grad_hidden)[0].astype(jnp.bfloat16)
    grad_wup = inner_rows(normal_in, grad_raised)
    grad_normal = outer_rows(grad_raised, w_up).astype(jnp.bfloat16).astype(jnp.float32)
    discarded_value, backward_fn = jax.vjp(scaled, stream, gain_vec)
    grad_stream, grad_gain = backward_fn(grad_normal)
    return (grad_out + grad_stream, grad_wup, grad_wdown, grad_gain)


def adamw_step(weight, grad_now, first, second, decay, rate):
    first = BETA_ONE * first + (1.0 - BETA_ONE) * grad_now
    second = BETA_TWO * second + (1.0 - BETA_TWO) * grad_now * grad_now
    ratio = first / (1.0 - BETA_ONE**STEP) / (jnp.sqrt(second / (1.0 - BETA_TWO**STEP)) + EPSILON)
    return (weight - rate * (ratio + decay * weight), first, second)


def local(
    pixels,
    token_order,
    visible,
    wide_weight,
    tall_weight,
    pred_weight,
    pred_down,
    enc_gains,
    pred_gains,
    wide_first,
    tall_first,
    pred_first,
    pred_down_first,
    enc_gains_first,
    pred_gains_first,
    wide_second,
    tall_second,
    pred_second,
    pred_down_second,
    enc_gains_second,
    pred_gains_second,
    teacher_wide,
    teacher_tall,
    teacher_gains,
):
    masters = (wide_weight, tall_weight, pred_weight, pred_down, enc_gains, pred_gains)
    copies = tuple((member.astype(jnp.bfloat16) for member in masters))
    teach_bf = (
        teacher_wide.astype(jnp.bfloat16),
        teacher_tall.astype(jnp.bfloat16),
        teacher_gains.astype(jnp.bfloat16),
    )
    section_idx = lax.axis_index("section")
    section_count = lax.axis_size("section")
    gathered = (
        lax.all_gather(copies[0], "dp", axis=0, tiled=True),
        lax.all_gather(copies[1], "dp", axis=0, tiled=True),
        lax.all_gather(copies[2], "dp", axis=0, tiled=True),
        lax.all_gather(copies[3], "dp", axis=0, tiled=True),
        lax.all_gather(copies[4], "dp", axis=0, tiled=True),
        lax.all_gather(copies[5], "dp", axis=0, tiled=True),
        lax.all_gather(teach_bf[0], "dp", axis=0, tiled=True),
        lax.all_gather(teach_bf[1], "dp", axis=0, tiled=True),
        lax.all_gather(teach_bf[2], "dp", axis=0, tiled=True),
    )
    w_wide, w_tall, w_pred, w_down, enc_copy, pred_copy, teach_wide, teach_tall, teach_copy = (
        gathered
    )
    enc_gain = enc_copy.astype(jnp.float32)
    pred_gain = pred_copy.astype(jnp.float32)
    teach_gain = teach_copy.astype(jnp.float32)
    target_here = jnp.sum(L - visible).astype(jnp.float32)
    target_total = lax.psum(target_here, "dp")
    positions = lax.iota(jnp.int32, L)
    empty_enc = jnp.zeros((VIS, D), jnp.bfloat16)
    empty_teach = jnp.zeros((L, D), jnp.bfloat16)
    empty_pred = jnp.zeros((L, PD), jnp.bfloat16)
    enc_attn = (w_wide[:, : 3 * D], w_wide[:, 3 * D : 4 * D])
    enc_feed = (w_wide[:, 4 * D : 4 * D + FF], w_tall[PATCH:])
    pred_attn = (w_pred[:, : 3 * PD], w_pred[:, 3 * PD : 4 * PD])
    pred_feed = (w_pred[:, 4 * PD : 4 * PD + PF], w_down)
    pred_head = w_pred[:, 4 * PD + PF :]
    pred_embed = w_wide[:, 4 * D + FF :]

    def embed(microbatch_index):
        row_ids = token_order[microbatch_index, :VIS]
        chosen = pixels[microbatch_index][row_ids]
        stream = matmul(chosen, w_tall[:PATCH]) + position_table(row_ids, D)
        return (chosen, stream, positions[:VIS] < visible[microbatch_index])

    def predictor_in(microbatch_index, encoded):
        projected = matmul(encoded, pred_embed)
        filled = jnp.concatenate([projected, jnp.zeros((L - VIS, PD), jnp.float32)], axis=0)
        context = (positions < visible[microbatch_index])[:, None]
        stream = jnp.where(context, filled, pred_gain[:, 3][None, :]) + position_table(
            token_order[microbatch_index], PD
        )
        return (context, stream)

    def teach_first(microbatch_index):
        teach_stream = matmul(pixels[microbatch_index], teach_tall[:PATCH]) + position_table(
            positions, D
        )
        teach_stream, discarded_value = attend_fwd(
            teach_stream,
            teach_gain[:, 0],
            teach_wide[:, : 3 * D],
            teach_wide[:, 3 * D : 4 * D],
            HE,
            None,
        )
        return teach_stream.astype(jnp.bfloat16)

    def teach_second(microbatch_index, teach_in):
        teach_stream, discarded_value = feed_fwd(
            teach_in.astype(jnp.float32),
            teach_gain[:, 1],
            teach_wide[:, 4 * D :],
            teach_tall[PATCH:],
        )
        return normed(scaled(teach_stream, teach_gain[:, 2]))[token_order[microbatch_index]].astype(
            jnp.bfloat16
        )

    def student_first(microbatch_index):
        chosen, stream, key_keep = embed(microbatch_index)
        stream, discarded_value = attend_fwd(
            stream, enc_gain[:, 0], enc_attn[0], enc_attn[1], HE, key_keep
        )
        return stream.astype(jnp.bfloat16)

    def student_second(attended):
        stream, discarded_value = feed_fwd(
            attended.astype(jnp.float32), enc_gain[:, 1], enc_feed[0], enc_feed[1]
        )
        return scaled(stream, enc_gain[:, 2]).astype(jnp.bfloat16)

    def student_third(microbatch_index, encoded):
        context, stream = predictor_in(microbatch_index, encoded)
        stream, discarded_value = attend_fwd(
            stream, pred_gain[:, 0], pred_attn[0], pred_attn[1], PH, None
        )
        return stream.astype(jnp.bfloat16)

    def backward_first(microbatch_index, grad_in, grad_sums, loss_part, retained_values):
        chosen, stream, key_keep = embed(microbatch_index)
        updated, stored = attend_fwd(stream, enc_gain[:, 0], enc_attn[0], enc_attn[1], HE, key_keep)
        grad_stream, grad_win, grad_wout, grad_gain = attend_back(
            stream,
            enc_gain[:, 0],
            enc_attn[0],
            enc_attn[1],
            HE,
            key_keep,
            stored,
            grad_in[0].astype(jnp.float32),
        )
        grad_patch = inner_rows(chosen, grad_stream.astype(jnp.bfloat16))
        sums = list(grad_sums)
        sums[0] = sums[0].at[:, : 3 * D].add(grad_win).at[:, 3 * D : 4 * D].add(grad_wout)
        sums[1] = sums[1].at[:PATCH].add(grad_patch)
        sums[4] = sums[4].at[:, 0].add(grad_gain)
        return ((empty_enc, empty_pred), tuple(sums), loss_part)

    def backward_second(microbatch_index, grad_in, grad_sums, loss_part, retained_values):
        stream = retained_values[0].astype(jnp.float32)
        updated, stored = feed_fwd(stream, enc_gain[:, 1], enc_feed[0], enc_feed[1])
        discarded_value, backward_fn = jax.vjp(scaled, updated, enc_gain[:, 2])
        grad_updated, grad_final_gain = backward_fn(grad_in[0].astype(jnp.float32))
        grad_stream, grad_wup, grad_wdown, grad_gain = feed_back(
            stream, enc_gain[:, 1], enc_feed[0], enc_feed[1], stored, grad_updated
        )
        sums = list(grad_sums)
        sums[0] = sums[0].at[:, 4 * D : 4 * D + FF].add(grad_wup)
        sums[1] = sums[1].at[PATCH:].add(grad_wdown)
        sums[4] = sums[4].at[:, 1].add(grad_gain).at[:, 2].add(grad_final_gain)
        return ((grad_stream.astype(jnp.bfloat16), empty_pred), tuple(sums), loss_part)

    def backward_third(microbatch_index, grad_in, grad_sums, loss_part, retained_values):
        encoded = retained_values[0]
        context, stream = predictor_in(microbatch_index, encoded)
        updated, stored = attend_fwd(stream, pred_gain[:, 0], pred_attn[0], pred_attn[1], PH, None)
        grad_stream, grad_win, grad_wout, grad_gain = attend_back(
            stream,
            pred_gain[:, 0],
            pred_attn[0],
            pred_attn[1],
            PH,
            None,
            stored,
            grad_in[1].astype(jnp.float32),
        )
        grad_token = jnp.sum(jnp.where(context, 0.0, grad_stream), axis=0)
        grad_projected = jnp.where(context, grad_stream, 0.0)[:VIS].astype(jnp.bfloat16)
        grad_embed = inner_rows(encoded, grad_projected)
        grad_encoded = outer_rows(grad_projected, pred_embed).astype(jnp.bfloat16)
        sums = list(grad_sums)
        sums[0] = sums[0].at[:, 4 * D + FF :].add(grad_embed)
        sums[2] = sums[2].at[:, : 3 * PD].add(grad_win).at[:, 3 * PD : 4 * PD].add(grad_wout)
        sums[5] = sums[5].at[:, 0].add(grad_gain).at[:, 3].add(grad_token)
        return ((grad_encoded, empty_pred), tuple(sums), loss_part)

    def backward_fourth(microbatch_index, grad_in, grad_sums, loss_part, retained_values):
        target_rows = retained_values[1].astype(jnp.float32)
        stream = retained_values[2].astype(jnp.float32)
        updated, stored = feed_fwd(stream, pred_gain[:, 1], pred_feed[0], pred_feed[1])
        final = scaled(updated, pred_gain[:, 2]).astype(jnp.bfloat16)
        guess = matmul(final, pred_head)
        residual = guess - target_rows
        smooth_err = jnp.sqrt(residual * residual + 1.0)
        target_mask = (positions >= visible[microbatch_index])[:, None]
        loss_part = loss_part + jnp.sum(jnp.where(target_mask, smooth_err - 1.0, 0.0))
        grad_guess = (jnp.where(target_mask, residual / smooth_err, 0.0) / target_total).astype(
            jnp.bfloat16
        )
        grad_head = inner_rows(final, grad_guess)
        grad_final = outer_rows(grad_guess, pred_head).astype(jnp.bfloat16).astype(jnp.float32)
        discarded_value, backward_fn = jax.vjp(scaled, updated, pred_gain[:, 2])
        grad_updated, grad_final_gain = backward_fn(grad_final)
        grad_stream, grad_wup, grad_wdown, grad_gain = feed_back(
            stream, pred_gain[:, 1], pred_feed[0], pred_feed[1], stored, grad_updated
        )
        sums = list(grad_sums)
        sums[2] = (
            sums[2].at[:, 4 * PD : 4 * PD + PF].add(grad_wup).at[:, 4 * PD + PF :].add(grad_head)
        )
        sums[3] = sums[3] + grad_wdown
        sums[5] = sums[5].at[:, 1].add(grad_gain).at[:, 2].add(grad_final_gain)
        return ((empty_enc, grad_stream.astype(jnp.bfloat16)), tuple(sums), loss_part)

    def backward_rest(microbatch_index, grad_in, grad_sums, loss_part, retained_values):
        return ((empty_enc, empty_pred), grad_sums, loss_part)

    sums_start = tuple(
        (
            jnp.zeros(member.shape, jnp.float32)
            for member in (w_wide, w_tall, w_pred, w_down, enc_copy, pred_copy)
        )
    )
    loss_start = jnp.zeros((), jnp.float32)

    def forward_first(microbatch_index, incoming_activation):
        return (student_first(microbatch_index), teach_first(microbatch_index), empty_pred)

    def forward_second(microbatch_index, incoming_activation):
        return (
            student_second(incoming_activation[0]),
            teach_second(microbatch_index, incoming_activation[1]),
            empty_pred,
        )

    def forward_third(microbatch_index, incoming_activation):
        return (
            empty_enc,
            incoming_activation[1],
            student_third(microbatch_index, incoming_activation[0]),
        )

    def forward_rest(microbatch_index, incoming_activation):
        return (empty_enc, empty_teach, empty_pred)

    def forward_tick(clock_tick, carried_through):
        incoming_activation, saved_activations = carried_through
        microbatch_index = clock_tick - section_idx
        active = (microbatch_index >= 0) & (microbatch_index < MICRO)
        microbatch_index = jnp.clip(microbatch_index, 0, MICRO - 1)
        saved_activations = tuple(
            (
                holding_slots.at[microbatch_index].set(
                    jnp.where(active, received_activation, holding_slots[microbatch_index])
                )
                for holding_slots, received_activation in zip(
                    saved_activations, incoming_activation
                )
            )
        )
        branch_idx = jnp.where(active, section_idx, 4)
        first_out, second_out, third_out = lax.switch(
            branch_idx,
            [forward_first, forward_second, forward_third, forward_rest, forward_rest],
            microbatch_index,
            incoming_activation,
        )
        incoming_activation = (
            passed_along(shortened(first_out), "section", 1).astype(first_out.dtype),
            passed_along(shortened(second_out), "section", 1).astype(second_out.dtype),
            passed_along(shortened(third_out), "section", 1).astype(third_out.dtype),
        )
        return (incoming_activation, saved_activations)

    stash_start = (
        jnp.zeros((MICRO, VIS, D), jnp.bfloat16),
        jnp.zeros((MICRO, L, D), jnp.bfloat16),
        jnp.zeros((MICRO, L, PD), jnp.bfloat16),
    )
    discarded_value, saved_activations = lax.fori_loop(
        0,
        MICRO + section_count - 1,
        forward_tick,
        ((empty_enc, empty_teach, empty_pred), stash_start),
    )

    def backward_tick(clock_tick, carried_through):
        grad_in, grad_sums, loss_part = carried_through
        microbatch_index = clock_tick - (section_count - 1 - section_idx)
        active = (microbatch_index >= 0) & (microbatch_index < MICRO)
        microbatch_index = jnp.clip(microbatch_index, 0, MICRO - 1)
        branch_idx = jnp.where(active, section_idx, 4)
        retained_values = tuple(
            (holding_slots[microbatch_index] for holding_slots in saved_activations)
        )
        grad_out, grad_sums, loss_part = lax.switch(
            branch_idx,
            [backward_first, backward_second, backward_third, backward_fourth, backward_rest],
            microbatch_index,
            grad_in,
            grad_sums,
            loss_part,
            retained_values,
        )
        grad_in = passed_along((shortened(grad_out[0]), shortened(grad_out[1])), "section", -1)
        return (grad_in, grad_sums, loss_part)

    discarded_value, grad_sums, loss_part = lax.fori_loop(
        0,
        MICRO + section_count - 1,
        backward_tick,
        ((empty_enc, empty_pred), sums_start, loss_start),
    )
    grad_wide, grad_tall, grad_pred, grad_down, grad_enc, grad_predg = grad_sums
    shares = (
        lax.psum_scatter(grad_wide, "dp", scatter_dimension=0, tiled=True),
        lax.psum_scatter(grad_tall, "dp", scatter_dimension=0, tiled=True),
        lax.psum_scatter(grad_pred, "dp", scatter_dimension=0, tiled=True),
        lax.psum_scatter(grad_down, "dp", scatter_dimension=0, tiled=True),
        lax.psum_scatter(grad_enc, "dp", scatter_dimension=0, tiled=True),
        lax.psum_scatter(grad_predg, "dp", scatter_dimension=0, tiled=True),
    )
    shares = lax.psum((shares[0], shares[1], shares[2], shares[3], shares[4], shares[5]), "section")
    square = sum((jnp.sum(member * member) for member in shares)) / section_count
    loss_sum, square_total = lax.psum((loss_part, square), ("section", "dp"))
    grad_norm = jnp.sqrt(square_total)
    factor = jnp.minimum(1.0, CLIP_AT / (grad_norm + 1e-06))
    firsts = (
        wide_first,
        tall_first,
        pred_first,
        pred_down_first,
        enc_gains_first,
        pred_gains_first,
    )
    seconds = (
        wide_second,
        tall_second,
        pred_second,
        pred_down_second,
        enc_gains_second,
        pred_gains_second,
    )
    decays = (DECAY, DECAY, DECAY, DECAY, 0.0, 0.0)
    rates = (RATE, RATE, RATE, RATE, GAIN_RATE, GAIN_RATE)
    results = [
        adamw_step(
            masters[group_idx],
            shares[group_idx] * factor,
            firsts[group_idx],
            seconds[group_idx],
            decays[group_idx],
            rates[group_idx],
        )
        for group_idx in range(6)
    ]
    news = [entry[0] for entry in results]
    teacher_wide_new = KEEP_RATE * teacher_wide + (1.0 - KEEP_RATE) * news[0][:, : 4 * D + FF]
    teacher_tall_new = KEEP_RATE * teacher_tall + (1.0 - KEEP_RATE) * news[1]
    teacher_gains_new = KEEP_RATE * teacher_gains + (1.0 - KEEP_RATE) * news[4]
    return (
        loss_sum,
        target_total,
        grad_norm,
        news[0],
        news[1],
        news[2],
        news[3],
        news[4],
        news[5],
        results[0][1],
        results[1][1],
        results[2][1],
        results[3][1],
        results[4][1],
        results[5][1],
        results[0][2],
        results[1][2],
        results[2][2],
        results[3][2],
        results[4][2],
        results[5][2],
        news[0].astype(jnp.bfloat16),
        news[1].astype(jnp.bfloat16),
        news[2].astype(jnp.bfloat16),
        news[3].astype(jnp.bfloat16),
        news[4].astype(jnp.bfloat16),
        news[5].astype(jnp.bfloat16),
        teacher_wide_new,
        teacher_tall_new,
        teacher_gains_new,
    )


def solution(mesh):
    return jax.shard_map(
        local,
        mesh=mesh,
        in_specs=(
            P("dp", None, None),
            P("dp", None),
            P("dp"),
            P("dp", None),
            P("dp", None),
            P("dp", None),
            P("dp", None),
            P("dp", None),
            P("dp", None),
            P("dp", None),
            P("dp", None),
            P("dp", None),
            P("dp", None),
            P("dp", None),
            P("dp", None),
            P("dp", None),
            P("dp", None),
            P("dp", None),
            P("dp", None),
            P("dp", None),
            P("dp", None),
            P("dp", None),
            P("dp", None),
            P("dp", None),
        ),
        out_specs=(
            P(),
            P(),
            P(),
            P("dp", None),
            P("dp", None),
            P("dp", None),
            P("dp", None),
            P("dp", None),
            P("dp", None),
            P("dp", None),
            P("dp", None),
            P("dp", None),
            P("dp", None),
            P("dp", None),
            P("dp", None),
            P("dp", None),
            P("dp", None),
            P("dp", None),
            P("dp", None),
            P("dp", None),
            P("dp", None),
            P("dp", None),
            P("dp", None),
            P("dp", None),
            P("dp", None),
            P("dp", None),
            P("dp", None),
            P("dp", None),
            P("dp", None),
            P("dp", None),
        ),
        check_vma=False,
    )
```

profile of v0, /device:TPU:0, one launch (start us, length us, event | category | flops | bytes accessed | tf_op | source)
XLA Modules:
  0.0 5165.5 jit_solution(16268187126298306257)
XLA Ops:
  82.0 78.9 %all-gather.8.cloned.1.call-done = bf16[5632,1024]{1,0:T(8,128)(2,1)} async-done(((bf16[704,1024]{1,0:T(8,128)(2,1)}), bf16[5632,1024]{1,0:T(8,128)(2,1)}) %all-gather.8.cloned.1.call-update) | async-done | bytes 11534352 | tf_op jit(solution)/shard_map/all_gather | solution.py:244
  168.5 150.5 %all-gather.10.cloned.1.call-done = bf16[1024,8576]{1,0:T(8,128)(2,1)} async-done(((bf16[128,8576]{1,0:T(8,128)(2,1)}), bf16[1024,8576]{1,0:T(8,128)(2,1)}) %all-gather.10.cloned.1.call-update) | async-done | bytes 17563664 | tf_op jit(solution)/shard_map/all_gather | solution.py:243
  342.0 109.9 %all-gather.12.cloned.1.call-done = bf16[5632,1024]{1,0:T(8,128)(2,1)} async-done(((bf16[704,1024]{1,0:T(8,128)(2,1)}), bf16[5632,1024]{1,0:T(8,128)(2,1)}) %all-gather.12.cloned.1.call-update) | async-done | bytes 11534352 | tf_op jit(solution)/shard_map/all_gather | solution.py:250
  451.9 151.5 %all-gather.14.cloned.1.call-done = bf16[1024,8192]{1,0:T(8,128)(2,1)} async-done(((bf16[128,8192]{1,0:T(8,128)(2,1)}), bf16[1024,8192]{1,0:T(8,128)(2,1)}) %all-gather.14.cloned.1.call-update) | async-done | bytes 16777232 | tf_op jit(solution)/shard_map/all_gather | solution.py:249
  614.5 1595.1 %while.77 = (s32[]{:T(128)}, bf16[576,1024]{1,0:T(8,128)(2,1)}, bf16[1536,1024]{1,0:T(8,128)(2,1)}, bf16[1536,384]{1,0:T(8,128)(2,1)}, bf16[2,576,1024]{2,1,0:T(...) while((s32[]{:T(128)}, bf16[576,1024]{1,0:T(8,128)(2,1)}, ...), condition=%wide.region_37.38_spmd.clone.clone, body=%wide.region_0.37_spmd.clone.clone.sunk | while | flops 36065591296 | bytes 770988928 | solution.py:483
  615.0 295.9 %conditional.8 = (bf16[576,1024]{1,0:T(8,128)(2,1)}, bf16[1536,1024]{1,0:T(8,128)(2,1)}, bf16[1536,384]{1,0:T(8,128)(2,1)}) conditional(s32[]{:T(128)} %clamp.27, (s32[]{:T(128)}, bf16[2,1536,1536]{2,1,0:T(8,128)(2,1)}, s32[2,1536]{1,0:T(2,128)}, bf16[5632,1024]{1,0:T(8,128)(2,1)}, f32[1024,3]{0,1:T(4,128)}, ...), branch_computations={%region_1.13_spmd, %region_14.24_spmd, %region_25.33_spmd, %region... | conditional | flops 36060086272 | bytes 657733760 | solution.py:465
  935.2 96.1 %collective-permute-done.2 = bf16[1536,384]{1,0:T(8,128)(2,1)} collective-permute-done((bf16[1536,384]{1,0:T(8,128)(2,1)}, bf16[1536,384]{1,0:T(8,128)(2,1)}, u32[]{:S(2)}, u32[]{:S(2)}) %collective-permute-start.2) | collective-permute-done | bytes 1179680 | tf_op jit(solution)/shard_map/while/body/eval_jaxpr/ppermute | solution.py:39
  1040.2 296.0 %conditional.8 = (bf16[576,1024]{1,0:T(8,128)(2,1)}, bf16[1536,1024]{1,0:T(8,128)(2,1)}, bf16[1536,384]{1,0:T(8,128)(2,1)}) conditional(s32[]{:T(128)} %clamp.27, (s32[]{:T(128)}, bf16[2,1536,1536]{2,1,0:T(8,128)(2,1)}, s32[2,1536]{1,0:T(2,128)}, bf16[5632,1024]{1,0:T(8,128)(2,1)}, f32[1024,3]{0,1:T(4,128)}, ...), branch_computations={%region_1.13_spmd, %region_14.24_spmd, %region_25.33_spmd, %region... | conditional | flops 36060086272 | bytes 657733760 | solution.py:465
  1360.5 95.6 %collective-permute-done.2 = bf16[1536,384]{1,0:T(8,128)(2,1)} collective-permute-done((bf16[1536,384]{1,0:T(8,128)(2,1)}, bf16[1536,384]{1,0:T(8,128)(2,1)}, u32[]{:S(2)}, u32[]{:S(2)}) %collective-permute-start.2) | collective-permute-done | bytes 1179680 | tf_op jit(solution)/shard_map/while/body/eval_jaxpr/ppermute | solution.py:39
  1490.8 167.1 %collective-permute-start.1 = (bf16[1536,1024]{1,0:T(8,128)(2,1)}, bf16[1536,1024]{1,0:T(8,128)(2,1)}, u32[]{:S(2)}, u32[]{:S(2)}) collective-permute-start(bf16[1536,1024]{1,0:T(8,128)(2,1)} %get-tuple-element.3124), channel_id=1, source_target_pairs={{0,8},{8,16},{16,24},{1,9},{9,17},{17,25},{2,10},{10,18},{18,26},{... | collective-permute-start | bytes 9437192 | tf_op jit(solution)/shard_map/while/body/eval_jaxpr/ppermute | solution.py:39
  1679.0 94.7 %collective-permute-done.2 = bf16[1536,384]{1,0:T(8,128)(2,1)} collective-permute-done((bf16[1536,384]{1,0:T(8,128)(2,1)}, bf16[1536,384]{1,0:T(8,128)(2,1)}, u32[]{:S(2)}, u32[]{:S(2)}) %collective-permute-start.2) | collective-permute-done | bytes 1179680 | tf_op jit(solution)/shard_map/while/body/eval_jaxpr/ppermute | solution.py:39
  1814.3 117.4 %collective-permute-start = (bf16[576,1024]{1,0:T(8,128)(2,1)}, bf16[576,1024]{1,0:T(8,128)(2,1)}, u32[]{:S(2)}, u32[]{:S(2)}) collective-permute-start(bf16[576,1024]{1,0:T(8,128)(2,1)} %get-tuple-element.3123), channel_id=1, source_target_pairs={{0,8},{8,16},{16,24},{1,9},{9,17},{17,25},{2,10},{10,18},{18,26},{... | collective-permute-start | bytes 3538952 | tf_op jit(solution)/shard_map/while/body/eval_jaxpr/ppermute | solution.py:39
  2014.2 69.5 %collective-permute-start.1 = (bf16[1536,1024]{1,0:T(8,128)(2,1)}, bf16[1536,1024]{1,0:T(8,128)(2,1)}, u32[]{:S(2)}, u32[]{:S(2)}) collective-permute-start(bf16[1536,1024]{1,0:T(8,128)(2,1)} %get-tuple-element.3124), channel_id=1, source_target_pairs={{0,8},{8,16},{16,24},{1,9},{9,17},{17,25},{2,10},{10,18},{18,26},{... | collective-permute-start | bytes 9437192 | tf_op jit(solution)/shard_map/while/body/eval_jaxpr/ppermute | solution.py:39
  2107.6 90.4 %collective-permute-done.2 = bf16[1536,384]{1,0:T(8,128)(2,1)} collective-permute-done((bf16[1536,384]{1,0:T(8,128)(2,1)}, bf16[1536,384]{1,0:T(8,128)(2,1)}, u32[]{:S(2)}, u32[]{:S(2)}) %collective-permute-start.2) | collective-permute-done | bytes 1179680 | tf_op jit(solution)/shard_map/while/body/eval_jaxpr/ppermute | solution.py:39
  2239.1 1922.9 %while.78 = (s32[]{:T(128)}, bf16[576,1024]{1,0:T(8,128)(2,1)S(1)}, bf16[1536,384]{0,1:T(8,128)(2,1)}, f32[1024,8576]{1,0:T(8,128)}, f32[5632,1024]{1,0:T(8,128)...) while((s32[]{:T(128)}, bf16[576,1024]{1,0:T(8,128)(2,1)S(1)}, ...), condition=%wide.region_101.102_spmd.clone.clone, body=%wide.region_40.101_spmd.clone.clone.sunk | while | flops 29237780480 | bytes 1467037056 | solution.py:511
  2241.7 43.2 conditional.9
  2476.1 746.8 %collective-permute-done.3 = bf16[576,1024]{1,0:T(8,128)(2,1)S(1)} collective-permute-done((bf16[576,1024]{1,0:T(8,128)(2,1)}, bf16[576,1024]{1,0:T(8,128)(2,1)S(1)}, u32[]{:S(2)}, u32[]{:S(2)}) %collective-permute-start.3) | collective-permute-done | bytes 1179680 | tf_op jit(solution)/shard_map/while/body/eval_jaxpr/ppermute | solution.py:39
  3246.2 227.1 %conditional.9 = (bf16[576,1024]{1,0:T(8,128)(2,1)}, bf16[1536,384]{0,1:T(8,128)(2,1)}, f32[1024,8576]{1,0:T(8,128)}, f32[5632,1024]{1,0:T(8,128)}, f32[384,4096...) conditional(s32[]{:T(128)} %clamp.28, ...), branch_computations={%region_41.52_spmd, %region_53.65_spmd, %region_66.84_spmd, %regio... | conditional | flops 29237780480 | bytes 1450514944 | solution.py:499
  3475.9 380.0 %collective-permute-done.3 = bf16[576,1024]{1,0:T(8,128)(2,1)S(1)} collective-permute-done((bf16[576,1024]{1,0:T(8,128)(2,1)}, bf16[576,1024]{1,0:T(8,128)(2,1)S(1)}, u32[]{:S(2)}, u32[]{:S(2)}) %collective-permute-start.3) | collective-permute-done | bytes 1179680 | tf_op jit(solution)/shard_map/while/body/eval_jaxpr/ppermute | solution.py:39
  3878.3 227.1 %conditional.9 = (bf16[576,1024]{1,0:T(8,128)(2,1)}, bf16[1536,384]{0,1:T(8,128)(2,1)}, f32[1024,8576]{1,0:T(8,128)}, f32[5632,1024]{1,0:T(8,128)}, f32[384,4096...) conditional(s32[]{:T(128)} %clamp.28, ...), branch_computations={%region_41.52_spmd, %region_53.65_spmd, %region_66.84_spmd, %regio... | conditional | flops 29237780480 | bytes 1450514944 | solution.py:499
  4194.9 71.4 %reduce-scatter.15.cloned.1.call-done = f32[48,4096]{1,0:T(8,128)} async-done(((f32[384,4096]{1,0:T(8,128)}), f32[48,4096]{1,0:T(8,128)}) %reduce-scatter.15.cloned.1.call-update) | async-done | bytes 786448 | tf_op jit(solution)/shard_map/reduce_scatter | solution.py:521
  4266.2 228.2 %reduce-scatter.13.cloned.1.call-done = f32[704,1024]{1,0:T(8,128)} async-done(((f32[5632,1024]{1,0:T(8,128)}), f32[704,1024]{1,0:T(8,128)}) %reduce-scatter.13.cloned.1.call-update) | async-done | bytes 2883600 | tf_op jit(solution)/shard_map/reduce_scatter | solution.py:520
  4494.4 340.9 %reduce-scatter.11.cloned.1.call-done = f32[128,8576]{1,0:T(8,128)} async-done(((f32[1024,8576]{1,0:T(8,128)}), f32[128,8576]{1,0:T(8,128)}) %reduce-scatter.11.cloned.1.call-update) | async-done | bytes 4390928 | tf_op jit(solution)/shard_map/reduce_scatter | solution.py:519
  4910.9 163.4 %all-reduce.7.cloned.1.call-done = (f32[128,8576]{1,0:T(8,128)}, f32[704,1024]{1,0:T(8,128)}, f32[48,4096]{1,0:T(8,128)}, f32[192,384]{1,0:T(8,128)}) async-done(((f32[128,8576]{1,0:T(8,128)}, f32[704,1024]{1,0:T(8,128)}, f32[48,4096]{1,0:T(8,128)}, f32[192,384]{1,0:T(8,128)}), (f32[128,8576]{1,0:T(8,128)}, f32[704,1024]{1,0:T(8,128)}, f32[48,4096]{1,0:T(8,128)}, ...) | async-done | bytes 8355856 | tf_op jit(solution)/shard_map/psum | solution.py:526
  (663 shorter events, 1842.6 us)
Async XLA Ops:
  9.2 151.7 %all-gather.8.cloned.1.call-start = ((), (), s32[]{:S(2)}) async-start(), calls=%async_computation.6 | async-start | bytes 12976128 | tf_op jit(solution)/shard_map/all_gather | solution.py:244
  12.4 306.6 %all-gather.10.cloned.1.call-start = ((), (), s32[]{:S(2)}) async-start(), calls=%async_computation.7 | async-start | bytes 19759104 | tf_op jit(solution)/shard_map/all_gather | solution.py:243
  16.5 325.5 %all-gather.18.cloned.1.call-start = ((), (), s32[]{:S(2)}) async-start(), calls=%async_computation.11 | async-start | bytes 1327104 | tf_op jit(solution)/shard_map/all_gather | solution.py:246
  17.3 434.7 %all-gather.12.cloned.1.call-start = ((), (), s32[]{:S(2)}) async-start(), calls=%async_computation.8 | async-start | bytes 12976128 | tf_op jit(solution)/shard_map/all_gather | solution.py:250
  18.7 584.7 %all-gather.14.cloned.1.call-start = ((), (), s32[]{:S(2)}) async-start(), calls=%async_computation.9 | async-start | bytes 18874368 | tf_op jit(solution)/shard_map/all_gather | solution.py:249
  22.8 4172.1 %reduce-scatter.17.cloned.1.call-start = ((), (), s32[]{:S(2)}) async-start(), calls=%async_computation.15 | async-start | bytes 2654208 | tf_op jit(solution)/shard_map/reduce_scatter | solution.py:522
  910.9 125.2 %collective-permute-start.1 = (bf16[1536,1024]{1,0:T(8,128)(2,1)}, bf16[1536,1024]{1,0:T(8,128)(2,1)}, u32[]{:S(2)}, u32[]{:S(2)}) collective-permute-start(bf16[1536,1024]{1,0:T(8,128)(2,1)} %get-tuple-element.3124), channel_id=1, source_target_pairs={{0,8},{8,16},{16,24},{1,9},{9,17},{17,25},{2,10},{10,18},{18,26},{... | collective-permute-start | bytes 9437192 | tf_op jit(solution)/shard_map/while/body/eval_jaxpr/ppermute | solution.py:39
  914.0 119.7 %collective-permute-start = (bf16[576,1024]{1,0:T(8,128)(2,1)}, bf16[576,1024]{1,0:T(8,128)(2,1)}, u32[]{:S(2)}, u32[]{:S(2)}) collective-permute-start(bf16[576,1024]{1,0:T(8,128)(2,1)} %get-tuple-element.3123), channel_id=1, source_target_pairs={{0,8},{8,16},{16,24},{1,9},{9,17},{17,25},{2,10},{10,18},{18,26},{... | collective-permute-start | bytes 3538952 | tf_op jit(solution)/shard_map/while/body/eval_jaxpr/ppermute | solution.py:39
  1336.2 124.7 %collective-permute-start.1 = (bf16[1536,1024]{1,0:T(8,128)(2,1)}, bf16[1536,1024]{1,0:T(8,128)(2,1)}, u32[]{:S(2)}, u32[]{:S(2)}) collective-permute-start(bf16[1536,1024]{1,0:T(8,128)(2,1)} %get-tuple-element.3124), channel_id=1, source_target_pairs={{0,8},{8,16},{16,24},{1,9},{9,17},{17,25},{2,10},{10,18},{18,26},{... | collective-permute-start | bytes 9437192 | tf_op jit(solution)/shard_map/while/body/eval_jaxpr/ppermute | solution.py:39
  1339.3 119.2 %collective-permute-start = (bf16[576,1024]{1,0:T(8,128)(2,1)}, bf16[576,1024]{1,0:T(8,128)(2,1)}, u32[]{:S(2)}, u32[]{:S(2)}) collective-permute-start(bf16[576,1024]{1,0:T(8,128)(2,1)} %get-tuple-element.3123), channel_id=1, source_target_pairs={{0,8},{8,16},{16,24},{1,9},{9,17},{17,25},{2,10},{10,18},{18,26},{... | collective-permute-start | bytes 3538952 | tf_op jit(solution)/shard_map/while/body/eval_jaxpr/ppermute | solution.py:39
  1490.8 287.8 %collective-permute-start.1 = (bf16[1536,1024]{1,0:T(8,128)(2,1)}, bf16[1536,1024]{1,0:T(8,128)(2,1)}, u32[]{:S(2)}, u32[]{:S(2)}) collective-permute-start(bf16[1536,1024]{1,0:T(8,128)(2,1)} %get-tuple-element.3124), channel_id=1, source_target_pairs={{0,8},{8,16},{16,24},{1,9},{9,17},{17,25},{2,10},{10,18},{18,26},{... | collective-permute-start | bytes 9437192 | tf_op jit(solution)/shard_map/while/body/eval_jaxpr/ppermute | solution.py:39
  1657.9 118.3 %collective-permute-start = (bf16[576,1024]{1,0:T(8,128)(2,1)}, bf16[576,1024]{1,0:T(8,128)(2,1)}, u32[]{:S(2)}, u32[]{:S(2)}) collective-permute-start(bf16[576,1024]{1,0:T(8,128)(2,1)} %get-tuple-element.3123), channel_id=1, source_target_pairs={{0,8},{8,16},{16,24},{1,9},{9,17},{17,25},{2,10},{10,18},{18,26},{... | collective-permute-start | bytes 3538952 | tf_op jit(solution)/shard_map/while/body/eval_jaxpr/ppermute | solution.py:39
  1808.1 176.6 %collective-permute-start.1 = (bf16[1536,1024]{1,0:T(8,128)(2,1)}, bf16[1536,1024]{1,0:T(8,128)(2,1)}, u32[]{:S(2)}, u32[]{:S(2)}) collective-permute-start(bf16[1536,1024]{1,0:T(8,128)(2,1)} %get-tuple-element.3124), channel_id=1, source_target_pairs={{0,8},{8,16},{16,24},{1,9},{9,17},{17,25},{2,10},{10,18},{18,26},{... | collective-permute-start | bytes 9437192 | tf_op jit(solution)/shard_map/while/body/eval_jaxpr/ppermute | solution.py:39
  1814.3 168.0 %collective-permute-start = (bf16[576,1024]{1,0:T(8,128)(2,1)}, bf16[576,1024]{1,0:T(8,128)(2,1)}, u32[]{:S(2)}, u32[]{:S(2)}) collective-permute-start(bf16[576,1024]{1,0:T(8,128)(2,1)} %get-tuple-element.3123), channel_id=1, source_target_pairs={{0,8},{8,16},{16,24},{1,9},{9,17},{17,25},{2,10},{10,18},{18,26},{... | collective-permute-start | bytes 3538952 | tf_op jit(solution)/shard_map/while/body/eval_jaxpr/ppermute | solution.py:39
  2014.2 188.6 %collective-permute-start.1 = (bf16[1536,1024]{1,0:T(8,128)(2,1)}, bf16[1536,1024]{1,0:T(8,128)(2,1)}, u32[]{:S(2)}, u32[]{:S(2)}) collective-permute-start(bf16[1536,1024]{1,0:T(8,128)(2,1)} %get-tuple-element.3124), channel_id=1, source_target_pairs={{0,8},{8,16},{16,24},{1,9},{9,17},{17,25},{2,10},{10,18},{18,26},{... | collective-permute-start | bytes 9437192 | tf_op jit(solution)/shard_map/while/body/eval_jaxpr/ppermute | solution.py:39
  2473.5 749.4 %collective-permute-start.3 = (bf16[576,1024]{1,0:T(8,128)(2,1)}, bf16[576,1024]{1,0:T(8,128)(2,1)S(1)}, u32[]{:S(2)}, u32[]{:S(2)}) collective-permute-start(bf16[576,1024]{1,0:T(8,128)(2,1)} %get-tuple-element.3158), channel_id=1, source_target_pairs={{8,0},{16,8},{24,16},{9,1},{17,9},{25,17},{10,2},{18,10},{26,18},{... | collective-permute-start | bytes 3538952 | tf_op jit(solution)/shard_map/while/body/eval_jaxpr/ppermute | solution.py:39
  2474.8 768.3 %collective-permute-start.4 = (bf16[1536,384]{0,1:T(8,128)(2,1)}, bf16[1536,384]{0,1:T(8,128)(2,1)S(1)}, u32[]{:S(2)}, u32[]{:S(2)}) collective-permute-start(bf16[1536,384]{0,1:T(8,128)(2,1)} %get-tuple-element.3159), channel_id=1, source_target_pairs={{8,0},{16,8},{24,16},{9,1},{17,9},{25,17},{10,2},{18,10},{26,18},{... | collective-permute-start | bytes 3538952 | tf_op jit(solution)/shard_map/while/body/eval_jaxpr/ppermute | solution.py:39
  3473.3 382.6 %collective-permute-start.3 = (bf16[576,1024]{1,0:T(8,128)(2,1)}, bf16[576,1024]{1,0:T(8,128)(2,1)S(1)}, u32[]{:S(2)}, u32[]{:S(2)}) collective-permute-start(bf16[576,1024]{1,0:T(8,128)(2,1)} %get-tuple-element.3158), channel_id=1, source_target_pairs={{8,0},{16,8},{24,16},{9,1},{17,9},{25,17},{10,2},{18,10},{26,18},{... | collective-permute-start | bytes 3538952 | tf_op jit(solution)/shard_map/while/body/eval_jaxpr/ppermute | solution.py:39
  3474.6 400.6 %collective-permute-start.4 = (bf16[1536,384]{0,1:T(8,128)(2,1)}, bf16[1536,384]{0,1:T(8,128)(2,1)S(1)}, u32[]{:S(2)}, u32[]{:S(2)}) collective-permute-start(bf16[1536,384]{0,1:T(8,128)(2,1)} %get-tuple-element.3159), channel_id=1, source_target_pairs={{8,0},{16,8},{24,16},{9,1},{17,9},{25,17},{10,2},{18,10},{26,18},{... | collective-permute-start | bytes 3538952 | tf_op jit(solution)/shard_map/while/body/eval_jaxpr/ppermute | solution.py:39
  4162.9 331.6 %reduce-scatter.13.cloned.1.call-start = ((), (), s32[]{:S(2)}) async-start(), calls=%async_computation.13 | async-start | bytes 25952256 | tf_op jit(solution)/shard_map/reduce_scatter | solution.py:520
  4163.6 671.8 %reduce-scatter.11.cloned.1.call-start = ((), (), s32[]{:S(2)}) async-start(), calls=%async_computation.12 | async-start | bytes 39518208 | tf_op jit(solution)/shard_map/reduce_scatter | solution.py:519
  4164.2 702.8 %reduce-scatter.21.cloned.1.call-start = ((), (), s32[]{:S(2)}) async-start(), calls=%async_computation.17 | async-start | bytes 221184
  4165.2 733.6 %reduce-scatter.19.cloned.1.call-start = ((), (), s32[]{:S(2)}) async-start(), calls=%async_computation.16 | async-start | bytes 589824
  4167.0 907.2 %all-reduce.7.cloned.1.call-start = ((), (), s32[]{:S(2)}) async-start(), calls=%async_computation.18 | async-start | bytes 16711680 | tf_op jit(solution)/shard_map/psum | solution.py:526
  (136 other events, 3072.2 us)
Sparse Core Ops, SparseCore 0:
  10.3 41.3 all-gather.15
  53.8 106.9 all-gather.7
  163.1 155.8 all-gather.9
  321.1 20.8 all-gather.17
  344.1 107.8 all-gather.11
  454.0 149.3 all-gather.13
  4162.2 32.5 reduce-scatter.16
  4197.2 69.0 reduce-scatter.14
  4268.6 225.8 reduce-scatter.12
  4496.7 338.6 reduce-scatter.10
  4838.3 28.6 reduce-scatter.20
  4869.7 29.0 reduce-scatter.18
  4903.3 170.8 all-reduce.6
where the time goes:
time: 5180 us; the launch traced here: 5170 us
  waiting for transfers between devices  3110 us (60%)
  matrix products  637 us (12%)
  starting transfers between devices  404 us (8%)
  local copies, waits for them, and re-layouts  355 us (7%)
  loops' own time  302 us (6%)
  other arithmetic  239 us (5%)
  blocking collectives  97 us (2%)
    ppermute x25, waiting for transfers between devices, passed_along(): return lax.ppermute(block, axis, route)  1720 us
    ppermute x25, starting transfers between devices, passed_along(): return lax.ppermute(block, axis, route)  403 us
    reduce_scatter x1, waiting for transfers between devices, local(): lax.psum_scatter(grad_wide, 'dp', scatter_dimension=0, tiled=True)  341 us
    reduce_scatter x1, waiting for transfers between devices, local(): lax.psum_scatter(grad_tall, 'dp', scatter_dimension=0, tiled=True)  228 us
    another operation x5, loops' own time, backward_tick(): lax.switch(branch_idx, [backward_first, backward_second, backward_third,...  166 us
    psum x1, waiting for transfers between devices, local(): lax.psum((shares[0], shares[1], shares[2], shares[3], shares[4], shares[5...  163 us
    dot_general x10, matrix products, attend_fwd(): jnp.einsum('hqk,khd->qhd', attn_probs, value_heads, preferred_element_typ...  162 us
    sub x8, matrix products, attend_fwd(): exp_scores = jnp.exp(logits - row_max)  154 us
  transfers between devices with their start and end apart: 38, of which 27 were waited for; matrix products, arithmetic and copies ran while one was open for 3% of the time, Pallas kernels for 0%

commit v1 on v0

v1 whole, which is shorter than its diff:
```python
import functools
import math

import jax
import jax.numpy as jnp
from jax import lax
from jax.experimental import pallas as pl
from jax.experimental.pallas import tpu as pltpu
from jax.sharding import PartitionSpec as P

D = 1024
HE = 16
FF = 4096
PD = 384
PH = 12
PF = 1536
PATCH = 1536
L = 1536
STEP = 10
VIS = 576
VIS_LO = 192
HALF = L // 2
SEEN = VIS // 2
SKIP = VIS_LO // 2
LANES = 128
VMEM_LIMIT = 50 * 1024 * 1024


BETA_ONE = 0.9
BETA_TWO = 0.999
EPSILON = 1e-08
RATE = 0.02
GAIN_RATE = 0.5
DECAY = 0.05
CLIP_AT = 0.05
KEEP_RATE = 0.8
NEGATIVE = -1e30


def shortened(x):
    return jax.tree.map(lambda a: a.astype(jnp.bfloat16) if a.dtype == jnp.float32 else a, x)


def normed(stream):
    centred = stream - jnp.mean(stream, axis=-1, keepdims=True)
    return centred * lax.rsqrt(jnp.mean(centred * centred, axis=-1, keepdims=True) + 1e-06)


def scaled(stream, gain_vec):
    return normed(stream) * gain_vec


def position_table(positions, feature_width):
    frequency = jnp.exp(
        jnp.arange(feature_width // 2, dtype=jnp.float32)
        * (-2.0 * math.log(10000.0) / feature_width)
    )
    angles = positions.astype(jnp.float32)[:, None] * frequency[None, :]
    return jnp.concatenate([jnp.sin(angles), jnp.cos(angles)], axis=1)


def matmul(left, right):
    return jnp.dot(left, right, preferred_element_type=jnp.float32)


def inner_rows(left, right):
    return lax.dot_general(
        left, right, (((0,), (0,)), ((), ())), preferred_element_type=jnp.float32
    )


def outer_rows(left, right):
    return lax.dot_general(
        left, right, (((1,), (1,)), ((), ())), preferred_element_type=jnp.float32
    )


def gelu_exact(raised):
    return jax.nn.gelu(raised, approximate=False)


def head_scores(queries, key_heads, kept):
    logits = outer_rows(queries, key_heads)
    if kept is None:
        return logits
    key_ids = lax.broadcasted_iota(jnp.int32, logits.shape, 1)
    return jnp.where(key_ids < kept, logits, NEGATIVE)


def attend_kernel(head_size, masked, kept_ref, q_ref, k0_ref, v0_ref, k1_ref, v1_ref, o_ref, l_ref):
    exponent = head_size ** (-0.5) * math.log2(math.e)
    lane_head = lax.broadcasted_iota(jnp.int32, (1, LANES), 1) // head_size
    kept = (kept_ref[0], kept_ref[1]) if masked else (None, None)
    queries = q_ref[...]
    merged = jnp.zeros(o_ref.shape, jnp.float32)
    log_totals = jnp.zeros(o_ref.shape, jnp.float32)
    for head in range(LANES // head_size):
        chosen = lane_head == head
        head_queries = jnp.where(chosen, queries, jnp.zeros_like(queries))
        near = head_scores(head_queries, k0_ref[...], kept[0])
        far = head_scores(head_queries, k1_ref[...], kept[1])
        row_max = exponent * jnp.maximum(
            jnp.max(near, axis=1, keepdims=True), jnp.max(far, axis=1, keepdims=True)
        )
        near = jnp.exp2(near * exponent - row_max)
        far = jnp.exp2(far * exponent - row_max)
        row_total = jnp.sum(near, axis=1, keepdims=True) + jnp.sum(far, axis=1, keepdims=True)
        outcome = matmul(near.astype(jnp.bfloat16), v0_ref[...]) + matmul(
            far.astype(jnp.bfloat16), v1_ref[...]
        )
        merged = jnp.where(chosen, outcome / row_total, merged)
        log_totals = jnp.where(chosen, row_max + jnp.log2(row_total), log_totals)
    o_ref[...] = merged.astype(o_ref.dtype)
    l_ref[...] = log_totals


def attend_rows(queries, kv_near, kv_far, kept, num_heads, block_rows):
    row_count, width = queries.shape
    keys = kv_near.shape[0]
    groups = width // LANES
    masked = kept is not None
    if not masked:
        kept = jnp.zeros((2,), jnp.int32)
    row_spec = pl.BlockSpec((block_rows, LANES), lambda g, b, kept: (b, g))
    k_spec = pl.BlockSpec((keys, LANES), lambda g, b, kept: (0, g))
    v_spec = pl.BlockSpec((keys, LANES), lambda g, b, kept: (0, g + groups))
    return pl.pallas_call(
        functools.partial(attend_kernel, width // num_heads, masked),
        grid_spec=pltpu.PrefetchScalarGridSpec(
            num_scalar_prefetch=1,
            grid=(groups, row_count // block_rows),
            in_specs=[row_spec, k_spec, v_spec, k_spec, v_spec],
            out_specs=[row_spec, row_spec],
        ),
        out_shape=[
            jax.ShapeDtypeStruct((row_count, width), jnp.bfloat16),
            jax.ShapeDtypeStruct((row_count, width), jnp.float32),
        ],
        compiler_params=pltpu.CompilerParams(vmem_limit_bytes=VMEM_LIMIT),
        cost_estimate=pl.CostEstimate(
            flops=8 * row_count * keys * width,
            bytes_accessed=8 * (row_count + keys) * width,
            transcendentals=2 * row_count * keys * num_heads,
        ),
    )(kept, queries, kv_near, kv_near, kv_far, kv_far)


def attend_back_kernel(
    head_size, masked, kept_ref, q_ref, g_ref, l_ref, k0_ref, v0_ref, k1_ref, v1_ref,
    dq_ref, dk0_ref, dv0_ref, dk1_ref, dv1_ref,
):
    scaling = head_size ** (-0.5)
    exponent = scaling * math.log2(math.e)
    lane_head = lax.broadcasted_iota(jnp.int32, (1, LANES), 1) // head_size
    kept = (kept_ref[0], kept_ref[1]) if masked else (None, None)

    @pl.when(pl.program_id(1) == 0)
    def _():
        for ref in (dk0_ref, dv0_ref, dk1_ref, dv1_ref):
            ref[...] = jnp.zeros_like(ref)

    queries, grads, log_totals = q_ref[...], g_ref[...], l_ref[...]
    grad_queries = jnp.zeros(dq_ref.shape, jnp.float32)
    for head in range(LANES // head_size):
        chosen = lane_head == head
        head_queries = jnp.where(chosen, queries, jnp.zeros_like(queries))
        head_grads = jnp.where(chosen, grads, jnp.zeros_like(grads))
        log_total = log_totals[:, head * head_size : head * head_size + 1]
        probs, steps, totals = [], [], 0.0
        for k_ref, v_ref, count in ((k0_ref, v0_ref, kept[0]), (k1_ref, v1_ref, kept[1])):
            attn = jnp.exp2(head_scores(head_queries, k_ref[...], count) * exponent - log_total)
            step = outer_rows(head_grads, v_ref[...]) * attn
            totals = totals + jnp.sum(step, axis=1, keepdims=True)
            probs.append(attn)
            steps.append(step)
        outcome = 0.0
        for attn, step, k_ref, dk_ref, dv_ref in zip(
            probs, steps, (k0_ref, k1_ref), (dk0_ref, dk1_ref), (dv0_ref, dv1_ref)
        ):
            grad_logits = (step - attn * totals).astype(jnp.bfloat16)
            dv_ref[...] += inner_rows(attn.astype(jnp.bfloat16), head_grads)
            dk_ref[...] += inner_rows(grad_logits, head_queries) * scaling
            outcome = outcome + matmul(grad_logits, k_ref[...])
        grad_queries = jnp.where(chosen, outcome * scaling, grad_queries)
    dq_ref[...] = grad_queries.astype(dq_ref.dtype)


def attend_rows_back(queries, grads, log_totals, kv_near, kv_far, kept, num_heads, block_rows):
    row_count, width = queries.shape
    keys = kv_near.shape[0]
    groups = width // LANES
    masked = kept is not None
    if not masked:
        kept = jnp.zeros((2,), jnp.int32)
    row_spec = pl.BlockSpec((block_rows, LANES), lambda g, b, kept: (b, g))
    k_spec = pl.BlockSpec((keys, LANES), lambda g, b, kept: (0, g))
    v_spec = pl.BlockSpec((keys, LANES), lambda g, b, kept: (0, g + groups))
    key_shape = jax.ShapeDtypeStruct((keys, width), jnp.float32)
    return pl.pallas_call(
        functools.partial(attend_back_kernel, width // num_heads, masked),
        grid_spec=pltpu.PrefetchScalarGridSpec(
            num_scalar_prefetch=1,
            grid=(groups, row_count // block_rows),
            in_specs=[row_spec, row_spec, row_spec, k_spec, v_spec, k_spec, v_spec],
            out_specs=[row_spec, k_spec, k_spec, k_spec, k_spec],
        ),
        out_shape=[jax.ShapeDtypeStruct((row_count, width), jnp.bfloat16)] + [key_shape] * 4,
        compiler_params=pltpu.CompilerParams(vmem_limit_bytes=VMEM_LIMIT),
        cost_estimate=pl.CostEstimate(
            flops=20 * row_count * keys * width,
            bytes_accessed=8 * (row_count + 4 * keys) * width,
            transcendentals=2 * row_count * keys * num_heads,
        ),
    )(kept, queries, grads, log_totals, kv_near, kv_near, kv_far, kv_far)


def padded_rows(block, before, after):
    return jnp.pad(block, ((before, after), (0, 0)))


def scaled_back(stream, gain_vec, grad_out):
    discarded_value, backward_fn = jax.vjp(scaled, stream, gain_vec)
    return backward_fn(grad_out)


def feed_fwd(stream, gain_vec, w_up, w_down):
    normal_in = scaled(stream, gain_vec).astype(jnp.bfloat16)
    raised = matmul(normal_in, w_up)
    hidden = gelu_exact(raised).astype(jnp.bfloat16)
    return (stream + matmul(hidden, w_down), (normal_in, raised, hidden))


def feed_back(stream, gain_vec, w_up, w_down, stored, grad_out):
    normal_in, raised, hidden = stored
    branch_grad = grad_out.astype(jnp.bfloat16)
    grad_wdown = inner_rows(hidden, branch_grad)
    grad_hidden = outer_rows(branch_grad, w_down).astype(jnp.bfloat16).astype(jnp.float32)
    discarded_value, backward_fn = jax.vjp(gelu_exact, raised)
    grad_raised = backward_fn(grad_hidden)[0].astype(jnp.bfloat16)
    grad_wup = inner_rows(normal_in, grad_raised)
    grad_normal = outer_rows(grad_raised, w_up).astype(jnp.bfloat16).astype(jnp.float32)
    grad_stream, grad_gain = scaled_back(stream, gain_vec, grad_normal)
    return (grad_out + grad_stream, grad_wup, grad_wdown, grad_gain)


def swapped(block):
    devices = range(lax.axis_size("dp"))
    return lax.ppermute(block, "dp", [(i, i ^ 1) for i in devices])


def attend_fwd(stream, gain_vec, w_in, w_out, num_heads, kept, skip, block_rows):
    width = stream.shape[1]
    normal_in = scaled(stream, gain_vec).astype(jnp.bfloat16)
    kv_near = matmul(normal_in, w_in[:, width:]).astype(jnp.bfloat16)
    kv_far = swapped(kv_near)
    queries = matmul(normal_in[skip:], w_in[:, :width]).astype(jnp.bfloat16)
    merged, log_totals = attend_rows(queries, kv_near, kv_far, kept, num_heads, block_rows)
    outcome = stream[skip:] + matmul(merged, w_out)
    return (outcome, (normal_in, queries, kv_near, kv_far, merged, log_totals))


def attend_back(stream, gain_vec, w_in, w_out, num_heads, kept, skip, block_rows, stored, grad_out):
    normal_in, queries, kv_near, kv_far, merged, log_totals = stored
    branch_grad = grad_out.astype(jnp.bfloat16)
    grad_wout = inner_rows(merged, branch_grad)
    grad_merged = outer_rows(branch_grad, w_out).astype(jnp.bfloat16)
    dq, dk_near, dv_near, dk_far, dv_far = attend_rows_back(
        queries, grad_merged, log_totals, kv_near, kv_far, kept, num_heads, block_rows
    )
    dk = (dk_near + swapped(dk_far)).astype(jnp.bfloat16)
    dv = (dv_near + swapped(dv_far)).astype(jnp.bfloat16)
    grad_packed = jnp.concatenate([padded_rows(dq, skip, 0), dk, dv], axis=1)
    grad_win = inner_rows(normal_in, grad_packed)
    grad_normal = outer_rows(grad_packed, w_in).astype(jnp.bfloat16).astype(jnp.float32)
    grad_stream, grad_gain = scaled_back(stream, gain_vec, grad_normal)
    return (padded_rows(grad_out, skip, 0) + grad_stream, grad_win, grad_wout, grad_gain)


MESH = pl.DeviceIdType.MESH


def gather_kernel(count, zn, *refs):
    ins, outs = refs[:count], refs[count : 2 * count]
    local_sem, z_send, z_recv, p_send, p_recv = refs[2 * count :]
    section, place = lax.axis_index("section"), lax.axis_index("dp")
    z, core = place // 2, place % 2
    near = {"section": section + 1 - 2 * (section % 2)}
    far = {"section": (section + 2) % 4}
    mate = {"dp": place + 1 - 2 * core}
    ahead = {"dp": place + 2}
    behind = {"dp": place - 2}

    barrier = pltpu.get_barrier_semaphore()
    line = [{"dp": (z + j) % zn * 2 + core} for j in range(1, zn)]
    for other in [near, far, mate] + line:
        pl.semaphore_signal(barrier, inc=1, device_id=other, device_id_type=MESH)
    pl.semaphore_wait(barrier, 3 + len(line))

    def block(ref, a, owner_z, quarter=None, rows=None, owner_core=core):
        size = ins[a].shape[0]
        start, length = (0, size) if rows is None else rows
        offset = pl.multiple_of((owner_z * 2 + owner_core) * size + start, 16)
        if quarter is None:
            return ref.at[pl.ds(offset, length), :]
        width = ins[a].shape[1] // 4
        return ref.at[pl.ds(offset, length), pl.ds(pl.multiple_of(quarter * width, 128), width)]

    def own_quarter(a):
        width = ins[a].shape[1] // 4
        return ins[a].at[:, pl.ds(pl.multiple_of(section * width, 128), width)]

    def copy(src, dst, sends, recvs, index, device):
        return pltpu.make_async_remote_copy(
            src_ref=src,
            dst_ref=dst,
            send_sem=sends.at[index],
            recv_sem=recvs.at[index],
            device_id=device,
            device_id_type=MESH,
        )

    def along(a, step, upward):
        device = ahead if upward else behind
        source_z = z - (step - 1) if upward else z + (step - 1)
        src = own_quarter(a) if step == 1 else block(outs[a], a, source_z, section)
        index = (a * (zn - 1) + step - 1) * 2 + (0 if upward else 1)
        return copy(src, block(outs[a], a, source_z, section), z_send, z_recv, index, device)

    def sends_along(step, upward):
        if upward:
            return (z - (step - 1) >= 0) & (z < zn - 1)
        return (z + (step - 1) <= zn - 1) & (z > 0)

    def first_half(a):
        size = ins[a].shape[0]
        return (0, (size + 31) // 32 * 16)

    def second_half(a):
        size = ins[a].shape[0]
        start = (size + 31) // 32 * 16
        return (start, size - start)

    def in_plane(a, step, upward, kind):
        owner_z = z - step if upward else z + step
        index = ((a * (zn - 1) + step - 1) * 2 + (0 if upward else 1)) * 5 + kind
        x_quarter, y_quarter = near["section"], far["section"]
        part = [
            lambda: block(outs[a], a, owner_z, section),
            lambda: block(outs[a], a, owner_z, section),
            lambda: block(outs[a], a, owner_z, x_quarter, first_half(a)),
            lambda: block(outs[a], a, owner_z, y_quarter, second_half(a)),
            lambda: block(outs[a], a, owner_z),
        ][kind]()
        return copy(part, part, p_send, p_recv, index, (near, far, far, near, mate)[kind])

    own = []
    for a in range(count):
        for upward in (True, False):

            @pl.when(sends_along(1, upward))
            def _(a=a, upward=upward):
                along(a, 1, upward).start()

    for a in range(count):
        keep = pltpu.make_async_copy(ins[a], block(outs[a], a, z), local_sem.at[a])
        keep.start()
        base = count * (zn - 1) * 10
        give = copy(ins[a], block(outs[a], a, z), p_send, p_recv, base + a, mate)
        give.start()
        own.append((keep, give))

    items = [
        (a, step, upward)
        for step in range(1, zn)
        for a in range(count)
        for upward in (True, False)
    ]

    def arrives(step, upward):
        return z - step >= 0 if upward else z + step <= zn - 1

    def received(a, step, upward):
        @pl.when(arrives(step, upward))
        def _():
            along(a, step, upward).wait_recv()
            in_plane(a, step, upward, 0).start()
            in_plane(a, step, upward, 1).start()

        if step < zn - 1:

            @pl.when(arrives(step, upward) & sends_along(step + 1, upward))
            def _():
                along(a, step + 1, upward).start()

    def passed_on(a, step, upward):
        @pl.when(arrives(step, upward))
        def _():
            in_plane(a, step, upward, 0).wait_recv()
            in_plane(a, step, upward, 2).start()
            in_plane(a, step, upward, 1).wait_recv()
            in_plane(a, step, upward, 3).start()

    def completed(a, step, upward):
        @pl.when(arrives(step, upward))
        def _():
            in_plane(a, step, upward, 2).wait_recv()
            in_plane(a, step, upward, 3).wait_recv()
            in_plane(a, step, upward, 4).start()

    lag = 4
    for i in range(len(items) + 2 * lag):
        if i < len(items):
            received(*items[i])
        if 0 <= i - lag < len(items):
            passed_on(*items[i - lag])
        if 0 <= i - 2 * lag < len(items):
            completed(*items[i - 2 * lag])

    for keep, give in own:
        keep.wait()
        give.wait()
    for a, step, upward in items:

        @pl.when(sends_along(step, upward))
        def _(a=a, step=step, upward=upward):
            along(a, step, upward).wait_send()

        @pl.when(arrives(step, upward))
        def _(a=a, step=step, upward=upward):
            for kind in range(5):
                in_plane(a, step, upward, kind).wait_send()
            in_plane(a, step, upward, 4).wait_recv()


def gather_blocks(blocks):
    count = len(blocks)
    dp_size = lax.axis_size("dp")
    zn = dp_size // 2
    return pl.pallas_call(
        functools.partial(gather_kernel, count, zn),
        in_specs=[pl.BlockSpec(memory_space=pl.ANY)] * count,
        out_specs=[pl.BlockSpec(memory_space=pl.ANY)] * count,
        out_shape=[
            jax.ShapeDtypeStruct((member.shape[0] * dp_size, member.shape[1]), member.dtype)
            for member in blocks
        ],
        scratch_shapes=[
            pltpu.SemaphoreType.DMA((count,)),
            pltpu.SemaphoreType.DMA((count * (zn - 1) * 2,)),
            pltpu.SemaphoreType.DMA((count * (zn - 1) * 2,)),
            pltpu.SemaphoreType.DMA((count * ((zn - 1) * 10 + 1),)),
            pltpu.SemaphoreType.DMA((count * ((zn - 1) * 10 + 1),)),
        ],
        compiler_params=pltpu.CompilerParams(collective_id=0, has_side_effects=True),
    )(*blocks)


def upper_rows(size):
    return (size + 31) // 32 * 16


def add_blocks(rows, targets):
    def step(i, carried_through):
        at = pl.ds(pl.multiple_of(i * 16, 16), 16)
        for out, terms in targets:
            out[at, :] = sum(term[at, :].astype(jnp.float32) for term in terms).astype(out.dtype)
        return carried_through

    lax.fori_loop(0, rows // 16, step, 0)


def reduce_kernel(count, zn, *refs):
    ins, refs = refs[: count + 1], refs[count + 1 :]
    outs, refs = refs[: count + 1], refs[count + 1 :]
    whole, refs = refs[:count], refs[count:]
    near_one, refs = refs[:count], refs[count:]
    far_one, refs = refs[:count], refs[count:]
    far_two, refs = refs[:count], refs[count:]
    near_two, refs = refs[:count], refs[count:]
    along, refs = refs[:count], refs[count:]
    loaded, refs = refs[:count], refs[count:]
    held, refs = refs[:count], refs[count:]
    done, refs = refs[:count], refs[count:]
    total_ref, side_ref, line_ref, load_sem, move_send, move_recv, side_send, side_recv, line_send, line_recv = refs
    tally, out_total = ins[count], outs[count]
    tally_rows = out_total.shape[0]

    section, place = lax.axis_index("section"), lax.axis_index("dp")
    z, core = place // 2, place % 2
    x_quarter = section + 1 - 2 * (section % 2)
    y_quarter = (section + 2) % 4
    xy_quarter = (x_quarter + 2) % 4
    near, far = {"section": x_quarter}, {"section": y_quarter}
    mate = {"dp": place + 1 - 2 * core}
    sizes = [out.shape[0] for out in outs[:count]]
    widths = [out.shape[1] // 4 for out in outs[:count]]

    barrier = pltpu.get_barrier_semaphore()
    line = [{"dp": (z + j) % zn * 2 + core} for j in range(1, zn)]
    for other in [near, far, mate] + line:
        pl.semaphore_signal(barrier, inc=1, device_id=other, device_id_type=MESH)
    pl.semaphore_wait(barrier, 3 + len(line))

    def rows_at(a, slot, start=0, length=None):
        return pl.ds(pl.multiple_of(slot * sizes[a] + start, 16), sizes[a] if length is None else length)

    def quarter_at(a, quarter):
        return pl.ds(pl.multiple_of(quarter * widths[a], 128), widths[a])

    def upper(a):
        return upper_rows(sizes[a])

    def lower(a):
        return sizes[a] - upper_rows(sizes[a])

    def sent(src, dst, kind, a, slot, device):
        index = (kind * count + a) * (zn + 1) + slot
        return pltpu.make_async_remote_copy(
            src_ref=src,
            dst_ref=dst,
            send_sem=move_send.at[index],
            recv_sem=move_recv.at[index],
            device_id=device,
            device_id_type=MESH,
        )

    def load(a, owner_z):
        source = pl.ds(pl.multiple_of((owner_z * 2 + core) * sizes[a], 16), sizes[a])
        return pltpu.make_async_copy(
            ins[a].at[source, :], loaded[a], load_sem.at[a]
        )

    def give(a, owner_z):
        source = pl.ds(pl.multiple_of((owner_z * 2 + 1 - core) * sizes[a], 16), sizes[a])
        return sent(ins[a].at[source, :], whole[a].at[rows_at(a, owner_z), :], 0, a, owner_z, mate)

    def first_near(a, owner_z, which):
        quarter = (x_quarter, xy_quarter)[which]
        return sent(
            whole[a].at[rows_at(a, owner_z, 0, upper(a)), quarter_at(a, quarter)],
            near_one[a].at[pl.ds(pl.multiple_of((owner_z * 2 + which) * upper(a), 16), upper(a)), :],
            1 + which, a, owner_z, near,
        )

    def first_far(a, owner_z, which):
        quarter = (y_quarter, xy_quarter)[which]
        return sent(
            whole[a].at[rows_at(a, owner_z, upper(a), lower(a)), quarter_at(a, quarter)],
            far_one[a].at[pl.ds(pl.multiple_of((owner_z * 2 + which) * lower(a), 16), lower(a)), :],
            3 + which, a, owner_z, far,
        )

    def second_far(a, owner_z):
        return sent(
            whole[a].at[rows_at(a, owner_z, 0, upper(a)), quarter_at(a, y_quarter)],
            far_two[a].at[pl.ds(pl.multiple_of(owner_z * upper(a), 16), upper(a)), :],
            5, a, owner_z, far,
        )

    def second_near(a, owner_z):
        return sent(
            whole[a].at[rows_at(a, owner_z, upper(a), lower(a)), quarter_at(a, x_quarter)],
            near_two[a].at[pl.ds(pl.multiple_of(owner_z * lower(a), 16), lower(a)), :],
            6, a, owner_z, near,
        )

    def onward(a, owner_z, upward, last):
        slot = zn if last and not upward else owner_z
        return sent(
            held[a].at[rows_at(a, owner_z), :],
            along[a].at[rows_at(a, slot), :],
            7, a, slot, {"dp": place + 2 if upward else place - 2},
        )

    def finished(a, kind):
        quarter = (section, section, x_quarter, y_quarter)[kind]
        columns = quarter_at(a, quarter)
        part = (
            pl.ds(0, sizes[a]), pl.ds(0, sizes[a]), pl.ds(0, upper(a)), pl.ds(upper(a), lower(a))
        )[kind]
        src = done[a] if kind < 2 else outs[a].at[part, columns]
        return sent(src, outs[a].at[part, columns], 8 + kind, a, 0, (near, far, far, near)[kind])

    def keep(a):
        return pltpu.make_async_copy(
            done[a], outs[a].at[:, quarter_at(a, section)], load_sem.at[a]
        )

    legs = [(k, upward) for k in range(zn - 1, 0, -1) for upward in (True, False)] + [(0, True)]
    items = [(a, leg) for leg in range(len(legs)) for a in range(count)]

    def owner_of(leg):
        k, upward = legs[leg]
        return z + k if upward else z - k

    def is_live(leg):
        k, upward = legs[leg]
        return (z + k <= zn - 1) if upward else (z - k >= 0)

    def started(a, leg):
        @pl.when(is_live(leg))
        def _():
            give(a, owner_of(leg)).start()

    def load_started(a, leg):
        @pl.when(is_live(leg))
        def _():
            load(a, owner_of(leg)).start()

    def paired(a, leg):
        @pl.when(is_live(leg))
        def _():
            owner_z = owner_of(leg)
            load(a, owner_z).wait()
            give(a, owner_z).wait_recv()
            target = whole[a].at[rows_at(a, owner_z), :]
            add_blocks(sizes[a], [(target, (target, loaded[a]))])
            for which in (1, 0):
                first_near(a, owner_z, which).start()
                first_far(a, owner_z, which).start()

        if leg + 1 < len(legs):
            load_started(a, leg + 1)

    def from_near(a, owner_z, which):
        start = pl.multiple_of((owner_z * 2 + which) * upper(a), 16)
        return near_one[a].at[pl.ds(start, upper(a)), :]

    def from_far(a, owner_z, which):
        start = pl.multiple_of((owner_z * 2 + which) * lower(a), 16)
        return far_one[a].at[pl.ds(start, lower(a)), :]

    def halved(a, leg):
        @pl.when(is_live(leg))
        def _():
            owner_z = owner_of(leg)
            first_near(a, owner_z, 1).wait_recv()
            target = whole[a].at[rows_at(a, owner_z, 0, upper(a)), quarter_at(a, y_quarter)]
            add_blocks(upper(a), [(target, (target, from_near(a, owner_z, 1)))])
            second_far(a, owner_z).start()
            first_far(a, owner_z, 1).wait_recv()
            target = whole[a].at[
                rows_at(a, owner_z, upper(a), lower(a)), quarter_at(a, x_quarter)
            ]
            add_blocks(lower(a), [(target, (target, from_far(a, owner_z, 1)))])
            second_near(a, owner_z).start()

    def quartered(a, leg):
        k, upward = legs[leg]

        @pl.when(is_live(leg))
        def _():
            owner_z = owner_of(leg)
            own = quarter_at(a, section)
            first_near(a, owner_z, 0).wait_recv()
            second_far(a, owner_z).wait_recv()
            add_blocks(
                upper(a),
                [
                    (
                        held[a].at[rows_at(a, owner_z, 0, upper(a)), :],
                        (
                            whole[a].at[rows_at(a, owner_z, 0, upper(a)), own],
                            from_near(a, owner_z, 0),
                            far_two[a].at[
                                pl.ds(pl.multiple_of(owner_z * upper(a), 16), upper(a)), :
                            ],
                        ),
                    )
                ],
            )
            first_far(a, owner_z, 0).wait_recv()
            second_near(a, owner_z).wait_recv()
            add_blocks(
                lower(a),
                [
                    (
                        held[a].at[rows_at(a, owner_z, upper(a), lower(a)), :],
                        (
                            whole[a].at[rows_at(a, owner_z, upper(a), lower(a)), own],
                            from_far(a, owner_z, 0),
                            near_two[a].at[
                                pl.ds(pl.multiple_of(owner_z * lower(a), 16), lower(a)), :
                            ],
                        ),
                    )
                ],
            )
            target = held[a].at[rows_at(a, owner_z), :]

            def join(upward_from, slot):
                onward(a, owner_z, upward_from, slot is not owner_z or k == 0).wait_recv()
                add_blocks(sizes[a], [(target, (target, along[a].at[rows_at(a, slot), :]))])

            if k > 0:

                @pl.when(z > 0 if upward else z < zn - 1)
                def _():
                    join(upward, owner_z)

                onward(a, owner_z, upward, k == 1).start()
            else:

                @pl.when(z > 0)
                def _():
                    join(True, owner_z)

                @pl.when(z < zn - 1)
                def _():
                    join(False, zn)

                def settle(i, carried_through):
                    at = pl.ds(pl.multiple_of(i * 16, 16), 16)
                    values = target[at, :]
                    done[a][at, :] = values.astype(done[a].dtype)
                    squares = values * values
                    squares = squares[:8] + squares[8:]
                    carried = total_ref[0:8, :]
                    for column in range(0, widths[a], 128):
                        carried = carried + squares[:, column : column + 128]
                    total_ref[0:8, :] = carried
                    return carried_through

                lax.fori_loop(0, sizes[a] // 16, settle, 0)
                keep(a).start()
                finished(a, 0).start()
                finished(a, 1).start()

    total_ref[0:8, :] = jnp.zeros((8, 128), jnp.float32)
    tally_copy = pltpu.make_async_copy(tally, total_ref.at[8:, :], load_sem.at[count])
    tally_copy.start()
    for a, leg in items[:count]:
        load_started(a, leg)
    for a, leg in items:
        started(a, leg)
    lag = 4
    for i in range(len(items) + 2 * lag):
        if i < len(items):
            paired(*items[i])
        if 0 <= i - lag < len(items):
            halved(*items[i - lag])
        if 0 <= i - 2 * lag < len(items):
            quartered(*items[i - 2 * lag])

    tally_copy.wait()

    def exchanged(stage, device):
        return pltpu.make_async_remote_copy(
            src_ref=total_ref,
            dst_ref=side_ref.at[pl.ds(stage * tally_rows, tally_rows), :],
            send_sem=side_send.at[stage],
            recv_sem=side_recv.at[stage],
            device_id=device,
            device_id_type=MESH,
        )

    for stage, device in enumerate((mate, near, far)):
        swap = exchanged(stage, device)
        swap.start()
        swap.wait()
        total_ref[...] += side_ref[stage * tally_rows : (stage + 1) * tally_rows, :]

    def told(from_z, to_z, j):
        index = from_z * zn + to_z
        return pltpu.make_async_remote_copy(
            src_ref=total_ref,
            dst_ref=line_ref.at[pl.ds(pl.multiple_of(from_z * tally_rows, 8), tally_rows), :],
            send_sem=line_send.at[index],
            recv_sem=line_recv.at[index],
            device_id={"dp": to_z * 2 + core},
            device_id_type=MESH,
        )

    for j in range(1, zn):
        told(z, (z + j) % zn, j).start()
    line_ref[pl.ds(pl.multiple_of(z * tally_rows, 8), tally_rows), :] = total_ref[...]
    for j in range(1, zn):
        told((z + j) % zn, z, j).wait_recv()
    grand = line_ref[0:tally_rows, :]
    for j in range(1, zn):
        grand = grand + line_ref[j * tally_rows : (j + 1) * tally_rows, :]
    for j in range(1, zn):
        told(z, (z + j) % zn, j).wait_send()
    total_ref[...] = grand
    show = pltpu.make_async_copy(total_ref, out_total, load_sem.at[count])
    show.start()

    for a in range(count):
        finished(a, 0).wait_recv()
        finished(a, 2).start()
        finished(a, 1).wait_recv()
        finished(a, 3).start()
    for a in range(count):
        keep(a).wait()
        finished(a, 2).wait_recv()
        finished(a, 3).wait_recv()
        for kind in range(4):
            finished(a, kind).wait_send()
    for a, leg in items:
        k, upward = legs[leg]

        @pl.when(is_live(leg))
        def _(a=a, leg=leg, k=k, upward=upward):
            owner_z = owner_of(leg)
            give(a, owner_z).wait_send()
            for which in (0, 1):
                first_near(a, owner_z, which).wait_send()
                first_far(a, owner_z, which).wait_send()
            second_near(a, owner_z).wait_send()
            second_far(a, owner_z).wait_send()
            if k > 0:
                onward(a, owner_z, upward, k == 1).wait_send()

    show.wait()


def reduce_blocks(blocks, tally, result_types):
    count = len(blocks)
    dp_size = lax.axis_size("dp")
    zn = dp_size // 2
    tally_rows = 8 + tally.shape[0]
    shapes = [(member.shape[0] // dp_size, member.shape[1]) for member in blocks]
    vmem = lambda rows, columns, dtype=jnp.bfloat16: pltpu.VMEM((rows, columns), dtype)
    anywhere = pl.BlockSpec(memory_space=pl.ANY)
    moves = 12 * count * (zn + 1)
    return pl.pallas_call(
        functools.partial(reduce_kernel, count, zn),
        in_specs=[anywhere] * (count + 1),
        out_specs=[anywhere] * (count + 1),
        out_shape=[jax.ShapeDtypeStruct(shape, kind) for shape, kind in zip(shapes, result_types)]
        + [jax.ShapeDtypeStruct((tally_rows, 128), jnp.float32)],
        scratch_shapes=[vmem(zn * r, w) for r, w in shapes]
        + [vmem(zn * 2 * upper_rows(r), w // 4) for r, w in shapes]
        + [vmem(zn * 2 * (r - upper_rows(r)), w // 4) for r, w in shapes]
        + [vmem(zn * upper_rows(r), w // 4) for r, w in shapes]
        + [vmem(zn * (r - upper_rows(r)), w // 4) for r, w in shapes]
        + [vmem((zn + 1) * r, w // 4, jnp.float32) for r, w in shapes]
        + [vmem(r, w) for r, w in shapes]
        + [vmem(zn * r, w // 4, jnp.float32) for r, w in shapes]
        + [vmem(r, w // 4, kind) for (r, w), kind in zip(shapes, result_types)]
        + [
            vmem(tally_rows, 128, jnp.float32),
            vmem(3 * tally_rows, 128, jnp.float32),
            vmem(zn * tally_rows, 128, jnp.float32),
            pltpu.SemaphoreType.DMA((count + 1,)),
            pltpu.SemaphoreType.DMA((moves,)),
            pltpu.SemaphoreType.DMA((moves,)),
            pltpu.SemaphoreType.DMA((3,)),
            pltpu.SemaphoreType.DMA((3,)),
            pltpu.SemaphoreType.DMA((zn * zn,)),
            pltpu.SemaphoreType.DMA((zn * zn,)),
        ],
        compiler_params=pltpu.CompilerParams(
            collective_id=1, has_side_effects=True, vmem_limit_bytes=58 * 1024 * 1024
        ),
    )(*blocks, tally)


def adamw_step(weight, grad_now, first, second, decay, rate):
    first = BETA_ONE * first + (1.0 - BETA_ONE) * grad_now
    second = BETA_TWO * second + (1.0 - BETA_TWO) * grad_now * grad_now
    ratio = first / (1.0 - BETA_ONE**STEP) / (jnp.sqrt(second / (1.0 - BETA_TWO**STEP)) + EPSILON)
    return (weight - rate * (ratio + decay * weight), first, second)


def local(
    pixels,
    token_order,
    visible,
    wide_weight,
    tall_weight,
    pred_weight,
    pred_down,
    enc_gains,
    pred_gains,
    wide_first,
    tall_first,
    pred_first,
    pred_down_first,
    enc_gains_first,
    pred_gains_first,
    wide_second,
    tall_second,
    pred_second,
    pred_down_second,
    enc_gains_second,
    pred_gains_second,
    teacher_wide,
    teacher_tall,
    teacher_gains,
):
    masters = (wide_weight, tall_weight, pred_weight, pred_down, enc_gains, pred_gains)
    section_idx = lax.axis_index("section")
    section_count = lax.axis_size("section")
    core = lax.axis_index("dp") % 2
    clips_here = pixels.shape[0]
    assert section_count == 2 * clips_here

    owner = section_idx // clips_here
    clip = section_idx % clips_here
    holds = core == owner
    counts_own = lax.dynamic_index_in_dim(visible, clip, 0)
    order_own = lax.dynamic_index_in_dim(token_order, clip, 0, keepdims=False)
    clip_facts = jnp.concatenate([order_own, counts_own])
    clip_facts = jnp.where(holds, clip_facts, swapped(clip_facts))
    seen = clip_facts[L]
    order_pairs = clip_facts[:L].reshape(HALF, 2)
    order = jnp.where(core == 0, order_pairs[:, 0], order_pairs[:, 1])
    pairs_own = order_own.reshape(HALF, 2)
    order_here = jnp.where(core == 0, pairs_own[:, 0], pairs_own[:, 1])
    order_there = jnp.where(core == 0, pairs_own[:, 1], pairs_own[:, 0])
    pixel_rows = pixels.reshape(clips_here * L, PATCH)
    for_here = pixel_rows[order_here + clip * L]
    for_there = pixel_rows[order_there + clip * L]
    chosen = jnp.where(holds, for_here, swapped(for_there))
    seen_near = (seen - core + 1) // 2
    seen_far = (seen + core) // 2
    kept = jnp.stack([seen_near, seen_far])
    visible_high, visible_low = visible // LANES, visible % LANES
    dp_size = lax.axis_size("dp")
    row_count = wide_weight.shape[0]
    small = jnp.concatenate(
        [
            wide_weight[:, 4 * D + FF :],
            enc_gains,
            teacher_gains,
            jnp.pad(pred_gains, ((0, row_count - pred_gains.shape[0]), (0, 0))),
            jnp.zeros((row_count, LANES - 10 - 2 * clips_here), jnp.float32),
            jnp.broadcast_to(
                jnp.concatenate([visible_high, visible_low]).astype(jnp.float32)[None, :],
                (row_count, 2 * clips_here),
            ),
        ],
        axis=1,
    )
    blocks = (
        teacher_wide,
        teacher_tall,
        wide_weight[:, : 4 * D + FF],
        tall_weight,
        pred_weight.reshape(-1, D),
        small,
        jnp.pad(pred_down, ((0, 0), (0, LANES))),
    )
    teach_wide, teach_tall, w_wide, w_tall, w_pred, w_small, w_down = gather_blocks(
        tuple(member.astype(jnp.bfloat16) for member in blocks)
    )
    w_pred = w_pred.reshape(PD, -1)
    w_down = w_down[:, :PD]
    pred_embed = w_small[:, :PD]
    enc_copy = w_small[:, PD : PD + 3]
    teach_copy = w_small[:, PD + 3 : PD + 6]
    pred_copy = w_small[:, PD + 6 : PD + 10].reshape(dp_size, row_count, 4)
    pred_copy = pred_copy[:, : pred_gains.shape[0]].reshape(PD, 4)
    counts = w_small[::row_count, PD + LANES - 2 * clips_here :].astype(jnp.float32)
    counts = counts[:, :clips_here] * LANES + counts[:, clips_here:]
    target_total = jnp.sum(L - counts)
    enc_gain = enc_copy.astype(jnp.float32)
    pred_gain = pred_copy.astype(jnp.float32)
    teach_gain = teach_copy.astype(jnp.float32)
    enc_attn = (w_wide[:, : 3 * D], w_wide[:, 3 * D : 4 * D])
    enc_feed = (w_wide[:, 4 * D : 4 * D + FF], w_tall[PATCH:])
    pred_attn = (w_pred[:, : 3 * PD], w_pred[:, 3 * PD : 4 * PD])
    pred_feed = (w_pred[:, 4 * PD : 4 * PD + PF], w_down)
    pred_head = w_pred[:, 4 * PD + PF :]

    table = position_table(order, D)
    pred_table = position_table(order, PD)
    row_ids = lax.iota(jnp.int32, HALF)
    context = (row_ids < seen_near)[:, None]

    teach_stream = matmul(chosen, teach_tall[:PATCH]) + table
    teach_stream, discarded_value = attend_fwd(
        teach_stream, teach_gain[:, 0], teach_wide[:, : 3 * D], teach_wide[:, 3 * D : 4 * D],
        HE, None, SKIP, 336,
    )
    teach_stream = teach_stream.astype(jnp.bfloat16).astype(jnp.float32)
    teach_stream, discarded_value = feed_fwd(
        teach_stream, teach_gain[:, 1], teach_wide[:, 4 * D :], teach_tall[PATCH:]
    )
    goal = normed(scaled(teach_stream, teach_gain[:, 2])).astype(jnp.bfloat16).astype(jnp.float32)

    enc_chosen = chosen[:SEEN]
    stream_a = matmul(enc_chosen, w_tall[:PATCH]) + table[:SEEN]
    stream_b, stored_a = attend_fwd(
        stream_a, enc_gain[:, 0], enc_attn[0], enc_attn[1], HE, kept, 0, SEEN
    )
    stream_b = stream_b.astype(jnp.bfloat16).astype(jnp.float32)
    stream_c, stored_b = feed_fwd(stream_b, enc_gain[:, 1], enc_feed[0], enc_feed[1])
    encoded = scaled(stream_c, enc_gain[:, 2]).astype(jnp.bfloat16)

    projected = padded_rows(matmul(encoded, pred_embed), 0, HALF - SEEN)
    stream_d = jnp.where(context, projected, pred_gain[:, 3][None, :]) + pred_table
    stream_e, stored_d = attend_fwd(
        stream_d, pred_gain[:, 0], pred_attn[0], pred_attn[1], PH, None, SKIP, 336
    )
    stream_e = stream_e.astype(jnp.bfloat16).astype(jnp.float32)
    stream_f, stored_e = feed_fwd(stream_e, pred_gain[:, 1], pred_feed[0], pred_feed[1])
    final = scaled(stream_f, pred_gain[:, 2]).astype(jnp.bfloat16)
    residual = matmul(final, pred_head) - goal
    smooth_err = jnp.sqrt(residual * residual + 1.0)
    target_mask = jnp.logical_not(context[SKIP:])
    loss_part = jnp.sum(jnp.where(target_mask, smooth_err - 1.0, 0.0))
    grad_guess = (jnp.where(target_mask, residual / smooth_err, 0.0) / target_total).astype(
        jnp.bfloat16
    )

    grad_head = inner_rows(final, grad_guess)
    grad_final = outer_rows(grad_guess, pred_head).astype(jnp.bfloat16).astype(jnp.float32)
    grad_stream, grad_pg2 = scaled_back(stream_f, pred_gain[:, 2], grad_final)
    grad_stream, grad_pup, grad_down, grad_pg1 = feed_back(
        stream_e, pred_gain[:, 1], pred_feed[0], pred_feed[1], stored_e, grad_stream
    )
    grad_stream = grad_stream.astype(jnp.bfloat16).astype(jnp.float32)
    grad_stream, grad_pin, grad_pout, grad_pg0 = attend_back(
        stream_d, pred_gain[:, 0], pred_attn[0], pred_attn[1], PH, None, SKIP, 336, stored_d, grad_stream
    )
    grad_token = jnp.sum(jnp.where(context, 0.0, grad_stream), axis=0)
    grad_projected = jnp.where(context, grad_stream, 0.0)[:SEEN].astype(jnp.bfloat16)
    grad_embed = inner_rows(encoded, grad_projected)
    grad_encoded = outer_rows(grad_projected, pred_embed).astype(jnp.bfloat16).astype(jnp.float32)
    grad_stream, grad_eg2 = scaled_back(stream_c, enc_gain[:, 2], grad_encoded)
    grad_stream, grad_eup, grad_edown, grad_eg1 = feed_back(
        stream_b, enc_gain[:, 1], enc_feed[0], enc_feed[1], stored_b, grad_stream
    )
    grad_stream = grad_stream.astype(jnp.bfloat16).astype(jnp.float32)
    grad_stream, grad_ein, grad_eout, grad_eg0 = attend_back(
        stream_a, enc_gain[:, 0], enc_attn[0], enc_attn[1], HE, kept, 0, SEEN, stored_a, grad_stream
    )
    grad_patch = inner_rows(enc_chosen, grad_stream.astype(jnp.bfloat16))

    gain_grads = jnp.concatenate(
        [
            jnp.stack([grad_eg0, grad_eg1, grad_eg2], axis=1).reshape(-1, LANES),
            jnp.stack([grad_pg0, grad_pg1, grad_pg2, grad_token], axis=1).reshape(-1, LANES),
        ],
        axis=0,
    )
    gain_rows = 3 * D // LANES
    loss_tile = jnp.zeros((8, LANES), jnp.float32).at[0, 0].set(loss_part)
    tally = jnp.concatenate(
        [loss_tile, gain_grads, jnp.zeros((4, LANES), jnp.float32)], axis=0
    )
    blocks = shortened(
        (
            grad_ein,
            grad_eout,
            grad_eup,
            jnp.pad(grad_embed, ((0, 0), (0, LANES))),
            jnp.concatenate(shortened([grad_patch, grad_edown]), axis=0),
            jnp.concatenate(shortened([grad_pin, grad_pout, grad_pup, grad_head]), axis=1).reshape(-1, D),
            jnp.pad(grad_down, ((0, 0), (0, LANES))),
        )
    )
    *summed, tally = reduce_blocks(
        blocks, tally, [jnp.bfloat16] * 5 + [jnp.float32] * 2
    )
    wide_parts = [summed[0], summed[1], summed[2], summed[3][:, :PD]]
    place = lax.axis_index("dp")
    gains_all = tally[16 : 16 + gain_rows].reshape(D, 3)
    pred_gains_all = tally[16 + gain_rows : 16 + gain_rows + 4 * PD // LANES].reshape(PD, 4)
    shares = (
        jnp.concatenate(wide_parts, axis=1).astype(jnp.float32),
        summed[4].astype(jnp.float32),
        summed[5].reshape(pred_weight.shape).astype(jnp.float32),
        summed[6][:, :PD].astype(jnp.float32),
        lax.dynamic_slice_in_dim(gains_all, place * enc_gains.shape[0], enc_gains.shape[0], 0),
        lax.dynamic_slice_in_dim(pred_gains_all, place * pred_gains.shape[0], pred_gains.shape[0], 0),
    )
    loss_sum = tally[8, 0]
    square_total = jnp.sum(tally[:8]) + jnp.sum(jnp.square(tally[16:]))
    grad_norm = jnp.sqrt(square_total)
    factor = jnp.minimum(1.0, CLIP_AT / (grad_norm + 1e-06))
    firsts = (
        wide_first,
        tall_first,
        pred_first,
        pred_down_first,
        enc_gains_first,
        pred_gains_first,
    )
    seconds = (
        wide_second,
        tall_second,
        pred_second,
        pred_down_second,
        enc_gains_second,
        pred_gains_second,
    )
    decays = (DECAY, DECAY, DECAY, DECAY, 0.0, 0.0)
    rates = (RATE, RATE, RATE, RATE, GAIN_RATE, GAIN_RATE)
    results = [
        adamw_step(
            masters[group_idx],
            shares[group_idx] * factor,
            firsts[group_idx],
            seconds[group_idx],
            decays[group_idx],
            rates[group_idx],
        )
        for group_idx in range(6)
    ]
    news = [entry[0] for entry in results]
    teacher_wide_new = KEEP_RATE * teacher_wide + (1.0 - KEEP_RATE) * news[0][:, : 4 * D + FF]
    teacher_tall_new = KEEP_RATE * teacher_tall + (1.0 - KEEP_RATE) * news[1]
    teacher_gains_new = KEEP_RATE * teacher_gains + (1.0 - KEEP_RATE) * news[4]
    return (
        loss_sum,
        target_total,
        grad_norm,
        news[0],
        news[1],
        news[2],
        news[3],
        news[4],
        news[5],
        results[0][1],
        results[1][1],
        results[2][1],
        results[3][1],
        results[4][1],
        results[5][1],
        results[0][2],
        results[1][2],
        results[2][2],
        results[3][2],
        results[4][2],
        results[5][2],
        news[0].astype(jnp.bfloat16),
        news[1].astype(jnp.bfloat16),
        news[2].astype(jnp.bfloat16),
        news[3].astype(jnp.bfloat16),
        news[4].astype(jnp.bfloat16),
        news[5].astype(jnp.bfloat16),
        teacher_wide_new,
        teacher_tall_new,
        teacher_gains_new,
    )


def solution(mesh):
    return jax.shard_map(
        local,
        mesh=mesh,
        in_specs=(
            P("dp", None, None),
            P("dp", None),
            P("dp"),
            P("dp", None),
            P("dp", None),
            P("dp", None),
            P("dp", None),
            P("dp", None),
            P("dp", None),
            P("dp", None),
            P("dp", None),
            P("dp", None),
            P("dp", None),
            P("dp", None),
            P("dp", None),
            P("dp", None),
            P("dp", None),
            P("dp", None),
            P("dp", None),
            P("dp", None),
            P("dp", None),
            P("dp", None),
            P("dp", None),
            P("dp", None),
        ),
        out_specs=(
            P(),
            P(),
            P(),
            P("dp", None),
            P("dp", None),
            P("dp", None),
            P("dp", None),
            P("dp", None),
            P("dp", None),
            P("dp", None),
            P("dp", None),
            P("dp", None),
            P("dp", None),
            P("dp", None),
            P("dp", None),
            P("dp", None),
            P("dp", None),
            P("dp", None),
            P("dp", None),
            P("dp", None),
            P("dp", None),
            P("dp", None),
            P("dp", None),
            P("dp", None),
            P("dp", None),
            P("dp", None),
            P("dp", None),
            P("dp", None),
            P("dp", None),
            P("dp", None),
        ),
        check_vma=False,
    )
```

time: 5180 us -> 979 us (0.19)
  waiting for transfers between devices: 3110 us -> 0.02 us
  Pallas kernels: 0 us -> 614 us
  matrix products: 637 us -> 187 us
  starting transfers between devices: 404 us -> 3.47 us
  loops' own time: 302 us -> 0 us
  local copies, waits for them, and re-layouts: 355 us -> 66.4 us
  other arithmetic: 239 us -> 92.4 us
  blocking collectives: 97 us -> 0 us
    ppermute x25 -> x9, waiting for transfers between devices: 1720 us -> 0.02 us  [swapped(): return lax.ppermute(block, 'dp', [(i, i ^ 1) for i in devices])]
    reduce_scatter x4 -> x0, waiting for transfers between devices: 668 us -> none  [the longest x1 341 us: local(): lax.psum_scatter(grad_wide, 'dp', scatter_dimension=0, tiled=True)]
    pallas_call x0 -> x7, Pallas kernels: none -> 614 us  [the longest x1 247 us: gather_blocks(): pl.pallas_call(functools.partial(gather_kernel, count, zn), in_specs=[pl....]
    all_gather x6 -> x0, waiting for transfers between devices: 495 us -> none  [the longest x1 151 us: local(): lax.all_gather(teach_bf[0], 'dp', axis=0, tiled=True)]
    ppermute x25 -> x9, starting transfers between devices: 403 us -> 3.47 us  [swapped(): return lax.ppermute(block, 'dp', [(i, i ^ 1) for i in devices])]
    another operation x12 -> x0, loops' own time: 302 us -> none  [the longest x5 166 us: backward_tick(): lax.switch(branch_idx, [backward_first, backward_second, backward_third,...]
    dot_general x20 -> x0, matrix products: 287 us -> none  [the longest x10 162 us: attend_fwd(): jnp.einsum('hqk,khd->qhd', attn_probs, value_heads, preferred_element_typ...]
    psum x1 -> x0, waiting for transfers between devices: 163 us -> none  [local(): lax.psum((shares[0], shares[1], shares[2], shares[3], shares[4], shares[5...]
  transfers between devices with their start and end apart: 38 -> 9, of which waited for: 27 -> 0; matrix products, arithmetic and copies ran while one was open for 3% -> 12% of each run, Pallas kernels for 0% -> 28%
where the time goes in v1:
time: 979 us; the launch traced here: 971 us
  Pallas kernels  614 us (63%)
  matrix products  187 us (19%)
  other arithmetic  92.4 us (9%)
  local copies, waits for them, and re-layouts  66.4 us (7%)
    pallas_call x1, Pallas kernels, gather_blocks(): pl.pallas_call(functools.partial(gather_kernel, count, zn), in_specs=[pl....  247 us
    pallas_call x1, Pallas kernels, reduce_blocks(): pl.pallas_call(functools.partial(reduce_kernel, count, zn), in_specs=[any...  231 us
    dot_general x19, matrix products, matmul(): return jnp.dot(left, right, preferred_element_type=jnp.float32)  116 us
    pallas_call x3, Pallas kernels, attend_rows(): pl.pallas_call(functools.partial(attend_kernel, width // num_heads, maske...  70 us
    pallas_call x2, Pallas kernels, attend_rows_back(): pl.pallas_call(functools.partial(attend_back_kernel, width // num_heads,...  65.4 us
    dot_general x11, matrix products, inner_rows(): lax.dot_general(left, right, (((0,), (0,)), ((), ())), preferred_element_...  38.3 us
    dot_general x10, matrix products, outer_rows(): lax.dot_general(left, right, (((1,), (1,)), ((), ())), preferred_element_...  32.4 us
  transfers between devices with their start and end apart: 9, of which 0 were waited for; matrix products, arithmetic and copies ran while one was open for 12% of the time, Pallas kernels for 28%

profile of v1, /device:TPU:0, one launch (start us, length us, event | category | flops | bytes accessed | tf_op | source)
XLA Modules:
  0.0 970.6 jit_solution(14546032407578501211)
XLA Ops:
  2.2 10.8 %gather_fusion.1 = bf16[768,1536]{1,0:T(8,128)(2,1)} fusion(bf16[3072,1536]{1,0:T(8,128)(2,1)} %bitcast.40, s32[1024]{0:T(1024)S(1)} %pad_clamp_fusion), kind=kCustom, calls=%fused_computation.1 | custom fusion | bytes 4721664 | tf_op jit(solution)/shard_map/gather | solution.py:914
  29.8 247.5 %shard_map.463 = (bf16[1024,8192]{1,0:T(8,128)(2,1)}, bf16[5632,1024]{1,0:T(8,128)(2,1)}, bf16[1024,8192]{1,0:T(8,128)(2,1)}, bf16[5632,1024]{1,0:T(8,128)(2,1)}...) custom-call(bf16[128,8192]{1,0:T(8,128)(2,1)} %convert_element_type.283.refs_0_, ...), custom_call_target="tpu_custom_call" | custom-call | tf_op jit(solution)/shard_map/pallas_call | solution.py:439
  283.6 10.0 %gather_fusion = bf16[768,1536]{1,0:T(8,128)(2,1)S(1)} fusion(bf16[3072,1536]{1,0:T(8,128)(2,1)} %bitcast.41, s32[1024]{0:T(1024)S(1)} %pad_clamp_fusion.1), kind=kCustom, calls=%fused_computation | custom fusion | bytes 4721664 | tf_op jit(solution)/shard_map/gather | solution.py:913
  293.7 6.2 reshape.393
  333.0 10.8 %shard_map.464 = (bf16[288,1024]{1,0:T(8,128)(2,1)S(1)}, f32[288,1024]{1,0:T(8,128)S(1)}) custom-call(s32[2]{0:T(128)S(1)} %pad_add_fusion.1.kept_ref, bf16[288,1024]{1,0:T(8,128)(2,1)S(1)} %fusion.177.q_ref, bf16[288,2048]{1,0:T(8,128)(2,1)S(1)} %fusion.107.k0_ref.v0_ref, bf16[288,2048]{1,0:T(8,128)(2,1)S(1)} %fusion.107.k0_ref.v0_ref, ...), custom_call_target="tpu_custom_call" | custom-call | flops 679477248 | bytes 4718592 | tf_op jit(solution)/shard_map/pallas_call | solution.py:127
  347.5 16.2 %multiply_convert_fusion = (bf16[288,4096]{1,0:T(8,128)(2,1)S(1)}, f32[288,4096]{1,0:T(8,128)}, f32[288,4096]{1,0:T(8,128)}) fusion(bf16[1024,8192]{1,0:T(8,128)(2,1)} %get-tuple-element.74, bf16[288,1024]{1,0:T(8,128)(2,1)S(1)} %get-tuple-element.205, f32[1024]{0:T(1024)S(1)} %get-tuple-element.232, f32[288]{0:T(512)S(1)} %fusion.244, ...), kind=kOutput, calls=%fused_computation.84 | convolution fusion | flops 2494070784 | bytes 20781312 | tf_op jit(solution)/shard_map/dot_general | solution.py:63
  370.9 7.3 fusion.92.k0_ref.v0_ref
  384.3 21.8 %shard_map.465 = (bf16[672,384]{1,0:T(8,128)(2,1)S(1)}, f32[672,384]{1,0:T(8,128)S(1)}) custom-call(s32[2]{0:T(128)S(1)} %broadcast.593.kept_ref, bf16[672,384]{1,0:T(8,128)(2,1)S(1)} %convolution_convert_fusion.16.q_ref, bf16[768,768]{1,0:T(8,128)(2,1)S(1)} %convolution_convert_fusion.9.k0_ref.v0_ref, ...), custom_call_target="tpu_custom_call" | custom-call | flops 1585446912 | bytes 4423680 | tf_op jit(solution)/shard_map/pallas_call | solution.py:127
  408.3 12.9 %multiply_convert_fusion.1 = (bf16[672,1536]{1,0:T(8,128)(2,1)S(1)}, f32[672,1536]{1,0:T(8,128)}, f32[672,1536]{1,0:T(8,128)}) fusion(bf16[384,4096]{1,0:T(8,128)(2,1)} %reshape.393, bf16[672,384]{1,0:T(8,128)(2,1)S(1)} %get-tuple-element.210, f32[384]{0:T(512)S(1)} %get-tuple-element.153, f32[672]{0:T(1024)S(1)} %fusion.239, ...), kind=kOutput, calls=%fused_computation.117 | convolution fusion | flops 861106176 | bytes 12024576 | tf_op jit(solution)/shard_map/dot_general | solution.py:63
  422.9 37.4 %shard_map.466 = (bf16[672,1024]{1,0:T(8,128)(2,1)S(1)}, f32[672,1024]{1,0:T(8,128)}) custom-call(s32[2]{0:T(128)S(1)} %broadcast.593.kept_ref, bf16[672,1024]{1,0:T(8,128)(2,1)S(1)} %fusion.137.q_ref, bf16[768,2048]{1,0:T(8,128)(2,1)} %fusion.92.k0_ref.v0_ref, bf16[768,2048]{1,0:T(8,128)(2,1)} %fusion.92.k0_ref.v0_ref, ...), custom_call_target="tpu_custom_call" | custom-call | flops 4227858432 | bytes 11796480 | tf_op jit(solution)/shard_map/pallas_call | solution.py:127
  464.3 33.1 %fusion.123.clone.5 = bf16[672,4096]{1,0:T(8,128)(2,1)} fusion(bf16[1024,8192]{1,0:T(8,128)(2,1)} %get-tuple-element.80, bf16[672,1024]{1,0:T(8,128)(2,1)S(1)} %get-tuple-element.217, f32[1024]{0:T(1024)S(1)} %copy-done.117, f32[672]{0:T(1024)S(1)} %add_rsqrt_fusion.2, f32[672]{0:T(1024)S(1)} %broadcast_multiply_fusion.3), kind=kOutput, calls=%fused_computation.6.clone.clone.clone.clone.clone.clone.2 | convolution fusion | flops 5819498496 | bytes 15279360 | tf_op jit(solution)/shard_map/dot_general | solution.py:63
  497.5 8.5 fusion.313
  523.7 47.1 %shard_map.467 = (bf16[672,384]{1,0:T(8,128)(2,1)S(1)}, f32[768,384]{1,0:T(8,128)S(1)}, f32[768,384]{1,0:T(8,128)}, f32[768,384]{1,0:T(8,128)}, f32[768,384]{1,0:T(8,128)}) custom-call(s32[2]{0:T(128)S(1)} %broadcast.593.kept_ref, bf16[672,384]{1,0:T(8,128)(2,1)S(1)} %copy-done.14, bf16[672,384]{1,0:T(8,128)(2,1)S(1)} %convolution_convert_fusion.14.g_ref, ...), custom_call_target="tpu_custom_call" | custom-call | flops 3963617280 | bytes 11501568 | tf_op jit(solution)/shard_map/pallas_call | solution.py:199
  593.5 8.9 fusion.62
  602.4 6.2 fusion.198
  608.6 7.1 convolution_convert_fusion.1.refs_2_
  620.2 18.3 %shard_map.468 = (bf16[288,1024]{1,0:T(8,128)(2,1)S(1)}, f32[288,1024]{1,0:T(8,128)S(1)}, f32[288,1024]{1,0:T(8,128)}, f32[288,1024]{1,0:T(8,128)}, f32[288,1024]{1,0:T(8,128)}) custom-call(s32[2]{0:T(128)S(1)} %copy-done.9, bf16[288,1024]{1,0:T(8,128)(2,1)S(1)} %copy-done.4, bf16[288,1024]{1,0:T(8,128)(2,1)S(1)} %fusion.174.g_ref, f32[288,1024]{1,0:T(8,128)} %copy-done.5, ...), custom_call_target="tpu_custom_call" | custom-call | flops 1698693120 | bytes 11796480 | tf_op jit(solution)/shard_map/pallas_call | solution.py:199
  643.1 6.0 reshape.394.refs_5_
  655.0 7.0 convolution_convert_fusion
  670.4 6.3 convolution_convert_fusion.2.refs_0_
  681.3 15.7 %pad_maximum_fusion.refs_4_ = bf16[5632,1024]{1,0:T(8,128)(2,1)} fusion(bf16[4096,1024]{1,0:T(8,128)(2,1)} %convolution_convert_fusion, bf16[1536,1024]{1,0:T(8,128)(2,1)S(1)} %convolution_convert_fusion.3), kind=kLoop, calls=%fused_computation.3 | loop fusion | flops 23068672 | bytes 23068672 | tf_op jit(solution)/shard_map/concatenate | solution.py:1050
  698.4 231.4 %shard_map.469 = (bf16[128,3072]{1,0:T(8,128)(2,1)}, bf16[128,1024]{1,0:T(8,128)(2,1)}, bf16[128,4096]{1,0:T(8,128)(2,1)}, bf16[128,512]{1,0:T(8,128)(2,1)}, bf1...) custom-call(bf16[1024,3072]{1,0:T(8,128)(2,1)} %convolution_convert_fusion.2.refs_0_, ...), custom_call_target="tpu_custom_call" | custom-call | tf_op jit(solution)/shard_map/pallas_call | solution.py:826
  943.0 7.3 multiply_add_fusion.1
  953.4 7.9 fusion.302
  (497 shorter events, 171.8 us)
Async XLA Ops:
  13.0 300.3 %collective-permute-start = (bf16[768,1536]{1,0:T(8,128)(2,1)}, bf16[768,1536]{1,0:T(8,128)(2,1)}, u32[]{:S(2)}, u32[]{:S(2)}) collective-permute-start(bf16[768,1536]{1,0:T(8,128)(2,1)} %gather_fusion.1), channel_id=1, source_target_pairs={{0,1},{1,0},{2,3},{3,2},{4,5},{5,4},{6,7},{7,6},{8,9},{9,8},{10,11... | collective-permute-start | bytes 7077896 | tf_op jit(solution)/shard_map/ppermute | solution.py:248
  14.7 285.8 %collective-permute-start.1 = (s32[1537]{0:T(1024)S(1)}, s32[1537]{0:T(1024)S(1)}, u32[]{:S(2)}, u32[]{:S(2)}) collective-permute-start(s32[1537]{0:T(1024)S(1)} %pad_add_fusion), channel_id=1, source_target_pairs={{0,1},{1,0},{2,3},{3,2},{4,5},{5,4},{6,7},{7,6},{8,9},{9,8},{10,11... | collective-permute-start | bytes 18452 | tf_op jit(solution)/shard_map/ppermute | solution.py:248
  280.9 87.5 %copy-start.81 = (f32[384]{0:T(512)}, f32[384]{0:T(512)S(1)}, u32[]{:S(2)}) copy-start(f32[384]{0:T(512)S(1)} %get-tuple-element.154) | copy-start | bytes 4612
  283.6 39.4 %copy-start.66 = (f32[1024]{0:T(1024)}, f32[1024]{0:T(1024)S(1)}, u32[]{:S(2)}) copy-start(f32[1024]{0:T(1024)S(1)} %get-tuple-element.231) | copy-start | bytes 12292
  283.6 63.8 %copy-start.68 = (f32[1024]{0:T(1024)}, f32[1024]{0:T(1024)S(1)}, u32[]{:S(2)}) copy-start(f32[1024]{0:T(1024)S(1)} %get-tuple-element.232) | copy-start | bytes 12292
  283.6 83.3 %copy-start.96 = (f32[1024]{0:T(1024)}, f32[1024]{0:T(1024)S(1)}, u32[]{:S(2)}) copy-start(f32[1024]{0:T(1024)S(1)} %get-tuple-element.233) | copy-start | bytes 12292
  303.3 64.2 %copy-start.100 = (pred[768]{0:T(1024)(128)(4,1)}, pred[768]{0:T(1024)(128)(4,1)S(1)}, u32[]{:S(2)}) copy-start(pred[768]{0:T(1024)(128)(4,1)S(1)} %iota_compare_fusion.2) | copy-start | bytes 2308
  327.2 4.8 collective-permute-start.2
  368.1 38.1 %copy-start.15 = (f32[768,384]{1,0:T(8,128)}, f32[768,384]{1,0:T(8,128)S(1)}, u32[]{:S(2)}) copy-start(f32[768,384]{1,0:T(8,128)S(1)} %get-tuple-element.191) | copy-start | bytes 3538948
  370.8 12.3 %collective-permute-start.3 = (bf16[768,768]{1,0:T(8,128)(2,1)S(1)}, bf16[768,768]{1,0:T(8,128)(2,1)S(1)}, u32[]{:S(2)}, u32[]{:S(2)}) collective-permute-start(bf16[768,768]{1,0:T(8,128)(2,1)S(1)} %convolution_convert_fusion.9.k0_ref.v0_ref), channel_id=1, source_target_pairs={{0,1},{1,0},{2,3},{3,2},{4,5},{5,4},{6,7},{7,6},{8,9},{9,8},{10,11... | collective-permute-start | bytes 3538952 | tf_op jit(solution)/shard_map/ppermute | solution.py:248
  378.2 44.6 %collective-permute-start.4 = (bf16[768,2048]{1,0:T(8,128)(2,1)}, bf16[768,2048]{1,0:T(8,128)(2,1)}, u32[]{:S(2)}, u32[]{:S(2)}) collective-permute-start(bf16[768,2048]{1,0:T(8,128)(2,1)} %fusion.92.k0_ref.v0_ref), channel_id=1, source_target_pairs={{0,1},{1,0},{2,3},{3,2},{4,5},{5,4},{6,7},{7,6},{8,9},{9,8},{10,11... | collective-permute-start | bytes 9437192 | tf_op jit(solution)/shard_map/ppermute | solution.py:248
  422.5 92.5 %copy-start.32 = (f32[672,384]{1,0:T(8,128)}, f32[672,384]{1,0:T(8,128)S(1)}, u32[]{:S(2)}) copy-start(f32[672,384]{1,0:T(8,128)S(1)} %get-tuple-element.213) | copy-start | bytes 3096580
  460.3 37.1 %slice-start.6 = ((s8[11534336]{0:T(1024)(128)(4,1)}), s8[4194304]{0:T(1024)(128)(4,1)S(1)}, s32[]{:S(2)}) async-start(s8[11534336]{0:T(1024)(128)(4,1)} %bitcast.51), calls=%async_computation.6 | async-start | bytes 8388608
  464.3 33.1 %slice-start.7 = ((s8[11534336]{0:T(1024)(128)(4,1)}), s8[4194304]{0:T(1024)(128)(4,1)S(1)}, s32[]{:S(2)}) async-start(s8[11534336]{0:T(1024)(128)(4,1)} %bitcast.51), calls=%async_computation.7 | async-start | bytes 8388608
  464.3 33.1 %slice-start.8 = ((s8[11534336]{0:T(1024)(128)(4,1)}), s8[3145728]{0:T(1024)(128)(4,1)S(1)}, s32[]{:S(2)}) async-start(s8[11534336]{0:T(1024)(128)(4,1)} %bitcast.51), calls=%async_computation.8 | async-start | bytes 6291456
  523.7 48.9 %copy-start.131 = (bf16[672,1536]{1,0:T(8,128)(2,1)S(1)}, bf16[672,1536]{1,0:T(8,128)(2,1)}, u32[]{:S(2)}) copy-start(bf16[672,1536]{1,0:T(8,128)(2,1)} %copy-done.130) | copy-start | bytes 6193156
  570.8 11.2 %collective-permute-start.5 = (f32[768,384]{1,0:T(8,128)}, f32[768,384]{1,0:T(8,128)}, u32[]{:S(2)}, u32[]{:S(2)}) collective-permute-start(f32[768,384]{1,0:T(8,128)} %get-tuple-element.85), channel_id=1, source_target_pairs={{0,1},{1,0},{2,3},{3,2},{4,5},{5,4},{6,7},{7,6},{8,9},{9,8},{10,11... | collective-permute-start | bytes 3538952 | tf_op jit(solution)/shard_map/ppermute | solution.py:248
  571.3 12.3 %collective-permute-start.6 = (f32[768,384]{1,0:T(8,128)}, f32[768,384]{1,0:T(8,128)}, u32[]{:S(2)}, u32[]{:S(2)}) collective-permute-start(f32[768,384]{1,0:T(8,128)} %get-tuple-element.87), channel_id=1, source_target_pairs={{0,1},{1,0},{2,3},{3,2},{4,5},{5,4},{6,7},{7,6},{8,9},{9,8},{10,11... | collective-permute-start | bytes 3538952 | tf_op jit(solution)/shard_map/ppermute | solution.py:248
  638.5 23.6 %collective-permute-start.7 = (f32[288,1024]{1,0:T(8,128)}, f32[288,1024]{1,0:T(8,128)}, u32[]{:S(2)}, u32[]{:S(2)}) collective-permute-start(f32[288,1024]{1,0:T(8,128)} %get-tuple-element.91), channel_id=1, source_target_pairs={{0,1},{1,0},{2,3},{3,2},{4,5},{5,4},{6,7},{7,6},{8,9},{9,8},{10,11... | collective-permute-start | bytes 3538952 | tf_op jit(solution)/shard_map/ppermute | solution.py:248
  638.9 24.8 %collective-permute-start.8 = (f32[288,1024]{1,0:T(8,128)}, f32[288,1024]{1,0:T(8,128)}, u32[]{:S(2)}, u32[]{:S(2)}) collective-permute-start(f32[288,1024]{1,0:T(8,128)} %get-tuple-element.93), channel_id=1, source_target_pairs={{0,1},{1,0},{2,3},{3,2},{4,5},{5,4},{6,7},{7,6},{8,9},{9,8},{10,11... | collective-permute-start | bytes 3538952 | tf_op jit(solution)/shard_map/ppermute | solution.py:248
  698.4 238.9 %copy-start.105 = (f32[128,3]{0,1:T(4,128)S(1)}, f32[128,3]{0,1:T(4,128)}, u32[]{:S(2)}) copy-start(f32[128,3]{0,1:T(4,128)} %param.33) | copy-start | bytes 4612
  698.4 238.9 %copy-start.107 = (f32[128,3]{0,1:T(4,128)S(1)}, f32[128,3]{0,1:T(4,128)}, u32[]{:S(2)}) copy-start(f32[128,3]{0,1:T(4,128)} %param.49) | copy-start | bytes 4612
  698.4 238.9 %copy-start.120 = (f32[128,3]{0,1:T(4,128)S(1)}, f32[128,3]{0,1:T(4,128)}, u32[]{:S(2)}) copy-start(f32[128,3]{0,1:T(4,128)} %param.39) | copy-start | bytes 4612
  698.4 239.0 %copy-start.121 = (f32[128,3]{0,1:T(4,128)S(1)}, f32[128,3]{0,1:T(4,128)}, u32[]{:S(2)}) copy-start(f32[128,3]{0,1:T(4,128)} %param.45) | copy-start | bytes 4612
  (132 other events, 879.2 us)

commit v2 on v1

--- a/solution.py
+++ b/solution.py
@@ -73,10 +73,6 @@
     return lax.dot_general(
         left, right, (((1,), (1,)), ((), ())), preferred_element_type=jnp.float32
     )
-
-
-def gelu_exact(raised):
-    return jax.nn.gelu(raised, approximate=False)
 
 
 def head_scores(queries, key_heads, kept):
@@ -223,24 +219,36 @@
     return backward_fn(grad_out)
 
 
+def gelu_erf(raised):
+    return 0.5 * raised * (1.0 + lax.erf(raised * 0.5**0.5))
+
+
+def gelu_slope(raised):
+    bell = jnp.exp(-0.5 * raised * raised) * (2.0 * math.pi) ** (-0.5)
+    return 0.5 * (1.0 + lax.erf(raised * 0.5**0.5)) + raised * bell
+
+
 def feed_fwd(stream, gain_vec, w_up, w_down):
     normal_in = scaled(stream, gain_vec).astype(jnp.bfloat16)
     raised = matmul(normal_in, w_up)
-    hidden = gelu_exact(raised).astype(jnp.bfloat16)
+    hidden = gelu_erf(raised).astype(jnp.bfloat16)
     return (stream + matmul(hidden, w_down), (normal_in, raised, hidden))
 
 
 def feed_back(stream, gain_vec, w_up, w_down, stored, grad_out):
     normal_in, raised, hidden = stored
     branch_grad = grad_out.astype(jnp.bfloat16)
-    grad_wdown = inner_rows(hidden, branch_grad)
     grad_hidden = outer_rows(branch_grad, w_down).astype(jnp.bfloat16).astype(jnp.float32)
-    discarded_value, backward_fn = jax.vjp(gelu_exact, raised)
-    grad_raised = backward_fn(grad_hidden)[0].astype(jnp.bfloat16)
+    grad_raised = (grad_hidden * gelu_slope(raised)).astype(jnp.bfloat16)
     grad_wup = inner_rows(normal_in, grad_raised)
     grad_normal = outer_rows(grad_raised, w_up).astype(jnp.bfloat16).astype(jnp.float32)
     grad_stream, grad_gain = scaled_back(stream, gain_vec, grad_normal)
-    return (grad_out + grad_stream, grad_wup, grad_wdown, grad_gain)
+    return (grad_out + grad_stream, grad_wup, branch_grad, grad_gain)
+
+
+def picked_rows(table, row_ids):
+    choice = row_ids[:, None] == lax.iota(jnp.int32, table.shape[0])[None, :]
+    return matmul(choice.astype(table.dtype), table).astype(table.dtype)
 
 
 def swapped(block):
@@ -276,12 +284,47 @@
     return (padded_rows(grad_out, skip, 0) + grad_stream, grad_win, grad_wout, grad_gain)
 
 
+def tall_grad_kernel(first_blocks, x_ref, gx_ref, h_ref, gh_ref, out_ref):
+    @pl.when(pl.program_id(0) < first_blocks)
+    def _():
+        out_ref[...] = inner_rows(x_ref[...], gx_ref[...]).astype(out_ref.dtype)
+
+    @pl.when(pl.program_id(0) >= first_blocks)
+    def _():
+        out_ref[...] = inner_rows(h_ref[...], gh_ref[...]).astype(out_ref.dtype)
+
+
+def tall_grad(chosen, grad_stream, hidden, branch_grad):
+    rows, width = grad_stream.shape
+    block = 512
+    first_blocks, blocks = PATCH // block, (PATCH + FF) // block
+    return pl.pallas_call(
+        functools.partial(tall_grad_kernel, first_blocks),
+        grid=(blocks,),
+        in_specs=[
+            pl.BlockSpec((rows, block), lambda i: (0, jnp.minimum(i, first_blocks - 1))),
+            pl.BlockSpec((rows, width), lambda i: (0, 0)),
+            pl.BlockSpec((rows, block), lambda i: (0, jnp.maximum(i - first_blocks, 0))),
+            pl.BlockSpec((rows, width), lambda i: (0, 0)),
+        ],
+        out_specs=pl.BlockSpec((block, width), lambda i: (i, 0)),
+        out_shape=jax.ShapeDtypeStruct((PATCH + FF, width), jnp.bfloat16),
+        compiler_params=pltpu.CompilerParams(vmem_limit_bytes=VMEM_LIMIT),
+        cost_estimate=pl.CostEstimate(
+            flops=2 * rows * width * (PATCH + FF),
+            bytes_accessed=2 * (PATCH + FF) * (rows + width),
+            transcendentals=0,
+        ),
+    )(chosen, grad_stream, hidden, branch_grad)
+
+
 MESH = pl.DeviceIdType.MESH
 
 
 def gather_kernel(count, zn, *refs):
     ins, outs = refs[:count], refs[count : 2 * count]
-    local_sem, z_send, z_recv, p_send, p_recv = refs[2 * count :]
+    stages = refs[2 * count : 3 * count]
+    local_sem, z_send, z_recv, p_send, p_recv = refs[3 * count :]
     section, place = lax.axis_index("section"), lax.axis_index("dp")
     z, core = place // 2, place % 2
     near = {"section": section + 1 - 2 * (section % 2)}
@@ -354,7 +397,8 @@
         return copy(part, part, p_send, p_recv, index, (near, far, far, near, mate)[kind])
 
     own = []
-    for a in range(count):
+    ranked = sorted(range(count), key=lambda a: ins[a].shape[0] * ins[a].shape[1])
+    for a in ranked:
         for upward in (True, False):
 
             @pl.when(sends_along(1, upward))
@@ -362,17 +406,22 @@
                 along(a, 1, upward).start()
 
     for a in range(count):
-        keep = pltpu.make_async_copy(ins[a], block(outs[a], a, z), local_sem.at[a])
-        keep.start()
+        take = pltpu.make_async_copy(ins[a], stages[a], local_sem.at[a])
+        take.start()
         base = count * (zn - 1) * 10
         give = copy(ins[a], block(outs[a], a, z), p_send, p_recv, base + a, mate)
         give.start()
-        own.append((keep, give))
+        keep = pltpu.make_async_copy(stages[a], block(outs[a], a, z), local_sem.at[a])
+        own.append((take, keep, give))
+
+    for take, keep, give in own:
+        take.wait()
+        keep.start()
 
     items = [
         (a, step, upward)
         for step in range(1, zn)
-        for a in range(count)
+        for a in ranked
         for upward in (True, False)
     ]
 
@@ -416,7 +465,7 @@
         if 0 <= i - 2 * lag < len(items):
             completed(*items[i - 2 * lag])
 
-    for keep, give in own:
+    for take, keep, give in own:
         keep.wait()
         give.wait()
     for a, step, upward in items:
@@ -444,14 +493,17 @@
             jax.ShapeDtypeStruct((member.shape[0] * dp_size, member.shape[1]), member.dtype)
             for member in blocks
         ],
-        scratch_shapes=[
+        scratch_shapes=[pltpu.VMEM(member.shape, member.dtype) for member in blocks]
+        + [
             pltpu.SemaphoreType.DMA((count,)),
             pltpu.SemaphoreType.DMA((count * (zn - 1) * 2,)),
             pltpu.SemaphoreType.DMA((count * (zn - 1) * 2,)),
             pltpu.SemaphoreType.DMA((count * ((zn - 1) * 10 + 1),)),
             pltpu.SemaphoreType.DMA((count * ((zn - 1) * 10 + 1),)),
         ],
-        compiler_params=pltpu.CompilerParams(collective_id=0, has_side_effects=True),
+        compiler_params=pltpu.CompilerParams(
+            collective_id=0, has_side_effects=True, vmem_limit_bytes=VMEM_LIMIT
+        ),
     )(*blocks)
 
 
@@ -527,7 +579,7 @@
     def load(a, owner_z):
         source = pl.ds(pl.multiple_of((owner_z * 2 + core) * sizes[a], 16), sizes[a])
         return pltpu.make_async_copy(
-            ins[a].at[source, :], loaded[a], load_sem.at[a]
+            ins[a].at[source, :], loaded[a].at[rows_at(a, owner_z), :], load_sem.at[a * zn + owner_z]
         )
 
     def give(a, owner_z):
@@ -567,7 +619,7 @@
     def onward(a, owner_z, upward, last):
         slot = zn if last and not upward else owner_z
         return sent(
-            held[a].at[rows_at(a, owner_z), :],
+            whole[a].at[rows_at(a, owner_z), quarter_at(a, section)],
             along[a].at[rows_at(a, slot), :],
             7, a, slot, {"dp": place + 2 if upward else place - 2},
         )
@@ -583,7 +635,7 @@
 
     def keep(a):
         return pltpu.make_async_copy(
-            done[a], outs[a].at[:, quarter_at(a, section)], load_sem.at[a]
+            done[a], outs[a].at[:, quarter_at(a, section)], load_sem.at[a * zn]
         )
 
     legs = [(k, upward) for k in range(zn - 1, 0, -1) for upward in (True, False)] + [(0, True)]
@@ -606,6 +658,15 @@
         @pl.when(is_live(leg))
         def _():
             load(a, owner_of(leg)).start()
+
+    def parts(a, owner_z, is_upper, quarter):
+        size = (0, upper(a)) if is_upper else (upper(a), lower(a))
+        at = (rows_at(a, owner_z, *size), quarter_at(a, quarter))
+        return (whole[a].at[at], loaded[a].at[at])
+
+    def pair_up(a, owner_z, is_upper, quarter):
+        both = parts(a, owner_z, is_upper, quarter)
+        add_blocks(upper(a) if is_upper else lower(a), [(both[0], both)])
 
     def paired(a, leg):
         @pl.when(is_live(leg))
@@ -613,14 +674,14 @@
             owner_z = owner_of(leg)
             load(a, owner_z).wait()
             give(a, owner_z).wait_recv()
-            target = whole[a].at[rows_at(a, owner_z), :]
-            add_blocks(sizes[a], [(target, (target, loaded[a]))])
+            for quarter in (xy_quarter, x_quarter):
+                pair_up(a, owner_z, True, quarter)
+            for quarter in (xy_quarter, y_quarter):
+                pair_up(a, owner_z, False, quarter)
             for which in (1, 0):
                 first_near(a, owner_z, which).start()
                 first_far(a, owner_z, which).start()
 
-        if leg + 1 < len(legs):
-            load_started(a, leg + 1)
 
     def from_near(a, owner_z, which):
         start = pl.multiple_of((owner_z * 2 + which) * upper(a), 16)
@@ -635,14 +696,12 @@
         def _():
             owner_z = owner_of(leg)
             first_near(a, owner_z, 1).wait_recv()
-            target = whole[a].at[rows_at(a, owner_z, 0, upper(a)), quarter_at(a, y_quarter)]
-            add_blocks(upper(a), [(target, (target, from_near(a, owner_z, 1)))])
+            both = parts(a, owner_z, True, y_quarter)
+            add_blocks(upper(a), [(both[0], both + (from_near(a, owner_z, 1),))])
             second_far(a, owner_z).start()
             first_far(a, owner_z, 1).wait_recv()
-            target = whole[a].at[
-                rows_at(a, owner_z, upper(a), lower(a)), quarter_at(a, x_quarter)
-            ]
-            add_blocks(lower(a), [(target, (target, from_far(a, owner_z, 1)))])
+            both = parts(a, owner_z, False, x_quarter)
+            add_blocks(lower(a), [(both[0], both + (from_far(a, owner_z, 1),))])
             second_near(a, owner_z).start()
 
     def quartered(a, leg):
@@ -654,39 +713,19 @@
             own = quarter_at(a, section)
             first_near(a, owner_z, 0).wait_recv()
             second_far(a, owner_z).wait_recv()
-            add_blocks(
-                upper(a),
-                [
-                    (
-                        held[a].at[rows_at(a, owner_z, 0, upper(a)), :],
-                        (
-                            whole[a].at[rows_at(a, owner_z, 0, upper(a)), own],
-                            from_near(a, owner_z, 0),
-                            far_two[a].at[
-                                pl.ds(pl.multiple_of(owner_z * upper(a), 16), upper(a)), :
-                            ],
-                        ),
-                    )
-                ],
+            start = pl.multiple_of(owner_z * upper(a), 16)
+            terms = parts(a, owner_z, True, section) + (
+                from_near(a, owner_z, 0), far_two[a].at[pl.ds(start, upper(a)), :]
             )
+            add_blocks(upper(a), [(held[a].at[pl.ds(0, upper(a)), :], terms)])
             first_far(a, owner_z, 0).wait_recv()
             second_near(a, owner_z).wait_recv()
-            add_blocks(
-                lower(a),
-                [
-                    (
-                        held[a].at[rows_at(a, owner_z, upper(a), lower(a)), :],
-                        (
-                            whole[a].at[rows_at(a, owner_z, upper(a), lower(a)), own],
-                            from_far(a, owner_z, 0),
-                            near_two[a].at[
-                                pl.ds(pl.multiple_of(owner_z * lower(a), 16), lower(a)), :
-                            ],
-                        ),
-                    )
-                ],
+            start = pl.multiple_of(owner_z * lower(a), 16)
+            terms = parts(a, owner_z, False, section) + (
+                from_far(a, owner_z, 0), near_two[a].at[pl.ds(start, lower(a)), :]
             )
-            target = held[a].at[rows_at(a, owner_z), :]
+            add_blocks(lower(a), [(held[a].at[pl.ds(upper(a), lower(a)), :], terms)])
+            target = held[a]
 
             def join(upward_from, slot):
                 onward(a, owner_z, upward_from, slot is not owner_z or k == 0).wait_recv()
@@ -698,6 +737,7 @@
                 def _():
                     join(upward, owner_z)
 
+                add_blocks(sizes[a], [(whole[a].at[rows_at(a, owner_z), own], (target,))])
                 onward(a, owner_z, upward, k == 1).start()
             else:
 
@@ -727,13 +767,12 @@
                 finished(a, 1).start()
 
     total_ref[0:8, :] = jnp.zeros((8, 128), jnp.float32)
-    tally_copy = pltpu.make_async_copy(tally, total_ref.at[8:, :], load_sem.at[count])
+    tally_copy = pltpu.make_async_copy(tally, total_ref.at[8:, :], load_sem.at[count * zn])
     tally_copy.start()
-    for a, leg in items[:count]:
-        load_started(a, leg)
     for a, leg in items:
         started(a, leg)
-    lag = 4
+        load_started(a, leg)
+    lag = 5
     for i in range(len(items) + 2 * lag):
         if i < len(items):
             paired(*items[i])
@@ -782,7 +821,7 @@
     for j in range(1, zn):
         told(z, (z + j) % zn, j).wait_send()
     total_ref[...] = grand
-    show = pltpu.make_async_copy(total_ref, out_total, load_sem.at[count])
+    show = pltpu.make_async_copy(total_ref, out_total, load_sem.at[count * zn])
     show.start()
 
     for a in range(count):
@@ -834,15 +873,15 @@
         + [vmem(zn * 2 * (r - upper_rows(r)), w // 4) for r, w in shapes]
         + [vmem(zn * upper_rows(r), w // 4) for r, w in shapes]
         + [vmem(zn * (r - upper_rows(r)), w // 4) for r, w in shapes]
-        + [vmem((zn + 1) * r, w // 4, jnp.float32) for r, w in shapes]
-        + [vmem(r, w) for r, w in shapes]
-        + [vmem(zn * r, w // 4, jnp.float32) for r, w in shapes]
+        + [vmem((zn + 1) * r, w // 4) for r, w in shapes]
+        + [vmem(zn * r, w) for r, w in shapes]
+        + [vmem(r, w // 4, jnp.float32) for r, w in shapes]
         + [vmem(r, w // 4, kind) for (r, w), kind in zip(shapes, result_types)]
         + [
             vmem(tally_rows, 128, jnp.float32),
             vmem(3 * tally_rows, 128, jnp.float32),
             vmem(zn * tally_rows, 128, jnp.float32),
-            pltpu.SemaphoreType.DMA((count + 1,)),
+            pltpu.SemaphoreType.DMA((count * zn + 1,)),
             pltpu.SemaphoreType.DMA((moves,)),
             pltpu.SemaphoreType.DMA((moves,)),
             pltpu.SemaphoreType.DMA((3,)),
@@ -851,7 +890,7 @@
             pltpu.SemaphoreType.DMA((zn * zn,)),
         ],
         compiler_params=pltpu.CompilerParams(
-            collective_id=1, has_side_effects=True, vmem_limit_bytes=58 * 1024 * 1024
+            collective_id=1, has_side_effects=True, vmem_limit_bytes=60 * 1024 * 1024
         ),
     )(*blocks, tally)
 
@@ -909,9 +948,9 @@
     pairs_own = order_own.reshape(HALF, 2)
     order_here = jnp.where(core == 0, pairs_own[:, 0], pairs_own[:, 1])
     order_there = jnp.where(core == 0, pairs_own[:, 1], pairs_own[:, 0])
-    pixel_rows = pixels.reshape(clips_here * L, PATCH)
-    for_here = pixel_rows[order_here + clip * L]
-    for_there = pixel_rows[order_there + clip * L]
+    pixel_rows = lax.dynamic_index_in_dim(pixels, clip, 0, keepdims=False)
+    for_here = picked_rows(pixel_rows, order_here)
+    for_there = picked_rows(pixel_rows, order_there)
     chosen = jnp.where(holds, for_here, swapped(for_there))
     seen_near = (seen - core + 1) // 2
     seen_far = (seen + core) // 2
@@ -933,12 +972,14 @@
         ],
         axis=1,
     )
+    pred_block = pred_weight.shape if pred_weight.shape[0] % 16 == 0 else (-1, D)
+    pred_form = (PD, pred_weight.shape[1]) if pred_weight.shape[0] % 16 == 0 else (-1, D)
     blocks = (
         teacher_wide,
         teacher_tall,
         wide_weight[:, : 4 * D + FF],
         tall_weight,
-        pred_weight.reshape(-1, D),
+        pred_weight.reshape(pred_block),
         small,
         jnp.pad(pred_down, ((0, 0), (0, LANES))),
     )
@@ -1008,9 +1049,10 @@
     grad_head = inner_rows(final, grad_guess)
     grad_final = outer_rows(grad_guess, pred_head).astype(jnp.bfloat16).astype(jnp.float32)
     grad_stream, grad_pg2 = scaled_back(stream_f, pred_gain[:, 2], grad_final)
-    grad_stream, grad_pup, grad_down, grad_pg1 = feed_back(
+    grad_stream, grad_pup, branch_grad, grad_pg1 = feed_back(
         stream_e, pred_gain[:, 1], pred_feed[0], pred_feed[1], stored_e, grad_stream
     )
+    grad_down = inner_rows(stored_e[2], branch_grad)
     grad_stream = grad_stream.astype(jnp.bfloat16).astype(jnp.float32)
     grad_stream, grad_pin, grad_pout, grad_pg0 = attend_back(
         stream_d, pred_gain[:, 0], pred_attn[0], pred_attn[1], PH, None, SKIP, 336, stored_d, grad_stream
@@ -1020,14 +1062,16 @@
     grad_embed = inner_rows(encoded, grad_projected)
     grad_encoded = outer_rows(grad_projected, pred_embed).astype(jnp.bfloat16).astype(jnp.float32)
     grad_stream, grad_eg2 = scaled_back(stream_c, enc_gain[:, 2], grad_encoded)
-    grad_stream, grad_eup, grad_edown, grad_eg1 = feed_back(
+    grad_stream, grad_eup, branch_grad, grad_eg1 = feed_back(
         stream_b, enc_gain[:, 1], enc_feed[0], enc_feed[1], stored_b, grad_stream
     )
     grad_stream = grad_stream.astype(jnp.bfloat16).astype(jnp.float32)
     grad_stream, grad_ein, grad_eout, grad_eg0 = attend_back(
         stream_a, enc_gain[:, 0], enc_attn[0], enc_attn[1], HE, kept, 0, SEEN, stored_a, grad_stream
     )
-    grad_patch = inner_rows(enc_chosen, grad_stream.astype(jnp.bfloat16))
+    grad_tall = tall_grad(
+        chosen[:SEEN], grad_stream.astype(jnp.bfloat16), stored_b[2], branch_grad
+    )
 
     gain_grads = jnp.concatenate(
         [
@@ -1047,8 +1091,8 @@
             grad_eout,
             grad_eup,
             jnp.pad(grad_embed, ((0, 0), (0, LANES))),
-            jnp.concatenate(shortened([grad_patch, grad_edown]), axis=0),
-            jnp.concatenate(shortened([grad_pin, grad_pout, grad_pup, grad_head]), axis=1).reshape(-1, D),
+            grad_tall,
+            jnp.concatenate(shortened([grad_pin, grad_pout, grad_pup, grad_head]), axis=1).reshape(pred_form),
             jnp.pad(grad_down, ((0, 0), (0, LANES))),
         )
     )

time: 979 us -> 835 us (0.85)
  matrix products: 187 us -> 145 us
  Pallas kernels: 614 us -> 572 us
  local copies, waits for them, and re-layouts: 66.4 us -> 31.5 us
  other arithmetic: 92.4 us -> 71 us
    pallas_call x1, Pallas kernels: 247 us -> 215 us  [gather_blocks(): pl.pallas_call(functools.partial(gather_kernel, count, zn), in_specs=[pl....]
    dot_general x19 -> x20, matrix products: 116 us -> 90.9 us  [matmul(): return jnp.dot(left, right, preferred_element_type=jnp.float32)]
    pallas_call x1, Pallas kernels: 231 us -> 208 us  [reduce_blocks(): pl.pallas_call(functools.partial(reduce_kernel, count, zn), in_specs=[any...]
    gather x2 -> x0, local copies, waits for them, and re-layouts: 20.8 us -> none  [the longest x1 10.8 us: local(): for_there = pixel_rows[order_there + clip * L]]
    concatenate x1 -> x0, other arithmetic: 15.7 us -> none  [local(): jnp.concatenate(shortened([grad_patch, grad_edown]), axis=0)]
    pallas_call x0 -> x1, Pallas kernels: none -> 12.4 us  [tall_grad(): pl.pallas_call(functools.partial(tall_grad_kernel, first_blocks), grid=(b...]
    reshape x2 -> x0, local copies, waits for them, and re-layouts: 12.1 us -> none  [the longest x1 6.16 us: local(): w_pred = w_pred.reshape(PD, -1)]
    dot_general x11 -> x9, matrix products: 38.3 us -> 27.8 us  [inner_rows(): lax.dot_general(left, right, (((0,), (0,)), ((), ())), preferred_element_...]
  transfers between devices with their start and end apart: 9 -> 9, of which waited for: 0 -> 0; matrix products, arithmetic and copies ran while one was open for 12% -> 9% of each run, Pallas kernels for 28% -> 29%
where the time goes in v2:
time: 835 us; the launch traced here: 828 us
  Pallas kernels  572 us (69%)
  matrix products  145 us (17%)
  other arithmetic  71 us (9%)
  local copies, waits for them, and re-layouts  31.5 us (4%)
    pallas_call x1, Pallas kernels, gather_blocks(): pl.pallas_call(functools.partial(gather_kernel, count, zn), in_specs=[pl....  215 us
    pallas_call x1, Pallas kernels, reduce_blocks(): pl.pallas_call(functools.partial(reduce_kernel, count, zn), in_specs=[any...  208 us
    dot_general x20, matrix products, matmul(): return jnp.dot(left, right, preferred_element_type=jnp.float32)  90.9 us
    pallas_call x3, Pallas kernels, attend_rows(): pl.pallas_call(functools.partial(attend_kernel, width // num_heads, maske...  70.4 us
    pallas_call x2, Pallas kernels, attend_rows_back(): pl.pallas_call(functools.partial(attend_back_kernel, width // num_heads,...  65.4 us
    dot_general x9, matrix products, inner_rows(): lax.dot_general(left, right, (((0,), (0,)), ((), ())), preferred_element_...  27.8 us
    dot_general x10, matrix products, outer_rows(): lax.dot_general(left, right, (((1,), (1,)), ((), ())), preferred_element_...  25.8 us
  transfers between devices with their start and end apart: 9, of which 0 were waited for; matrix products, arithmetic and copies ran while one was open for 9% of the time, Pallas kernels for 29%

profile of v2, /device:TPU:0, one launch (start us, length us, event | category | flops | bytes accessed | tf_op | source)
XLA Modules:
  0.0 828.2 jit_solution(10717482425861983589)
XLA Ops:
  2.2 7.7 fusion.54
  14.0 3.9 convert_element_type.285.refs_0_
  21.4 215.2 %shard_map.463 = (bf16[1024,8192]{1,0:T(8,128)(2,1)}, bf16[5632,1024]{1,0:T(8,128)(2,1)}, bf16[1024,8192]{1,0:T(8,128)(2,1)}, bf16[5632,1024]{1,0:T(8,128)(2,1)}...) custom-call(bf16[128,8192]{1,0:T(8,128)(2,1)} %convert_element_type.285.refs_0_, ...), custom_call_target="tpu_custom_call" | custom-call | tf_op jit(solution)/shard_map/pallas_call | solution.py:488
  246.2 6.0 multiply_cosine_fusion
  252.2 6.6 fusion.67
  258.8 5.5 fusion.249
  268.0 3.8 fusion.75.k0_ref.v0_ref
  278.2 10.8 %shard_map.464 = (bf16[288,1024]{1,0:T(8,128)(2,1)S(1)}, f32[288,1024]{1,0:T(8,128)S(1)}) custom-call(s32[2]{0:T(128)S(1)} %pad_add_fusion.1.kept_ref, bf16[288,1024]{1,0:T(8,128)(2,1)S(1)} %fusion.145.q_ref, bf16[288,2048]{1,0:T(8,128)(2,1)S(1)} %fusion.75.k0_ref.v0_ref, bf16[288,2048]{1,0:T(8,128)(2,1)S(1)} %fusion.75.k0_ref.v0_ref, ...), custom_call_target="tpu_custom_call" | custom-call | flops 679477248 | bytes 4718592 | tf_op jit(solution)/shard_map/pallas_call | solution.py:123
  292.6 7.1 multiply_convert_fusion.1
  307.2 7.3 fusion.57.k0_ref.v0_ref
  321.5 21.8 %shard_map.465 = (bf16[672,384]{1,0:T(8,128)(2,1)S(1)}, f32[672,384]{1,0:T(8,128)S(1)}) custom-call(s32[2]{0:T(128)S(1)} %broadcast.412.kept_ref, bf16[672,384]{1,0:T(8,128)(2,1)S(1)} %convolution_convert_fusion.14.q_ref, bf16[768,768]{1,0:T(8,128)(2,1)S(1)} %convolution_convert_fusion.7.k0_ref.v0_ref, ...), custom_call_target="tpu_custom_call" | custom-call | flops 1585446912 | bytes 4423680 | tf_op jit(solution)/shard_map/pallas_call | solution.py:123
  345.6 4.4 multiply_convert_fusion.2
  352.4 37.8 %shard_map.466 = (bf16[672,1024]{1,0:T(8,128)(2,1)S(1)}, f32[672,1024]{1,0:T(8,128)}) custom-call(s32[2]{0:T(128)S(1)} %broadcast.412.kept_ref, bf16[672,1024]{1,0:T(8,128)(2,1)S(1)} %fusion.105.q_ref, bf16[768,2048]{1,0:T(8,128)(2,1)} %fusion.57.k0_ref.v0_ref, bf16[768,2048]{1,0:T(8,128)(2,1)} %fusion.57.k0_ref.v0_ref, ...), custom_call_target="tpu_custom_call" | custom-call | flops 4227858432 | bytes 11796480 | tf_op jit(solution)/shard_map/pallas_call | solution.py:123
  395.1 19.7 %fusion.250 = (f32[672]{0:T(1024)S(1)}, f32[672,1024]{1,0:T(8,128)}) fusion(bf16[5632,1024]{1,0:T(8,128)(2,1)} %get-tuple-element.79, bf16[1024,8192]{1,0:T(8,128)(2,1)} %get-tuple-element.80, bf16[672,1024]{1,0:T(8,128)(2,1)} %copy-done.46, f32[1024]{0:T(1024)S(1)} %get-tuple-element.145, f32[672]{0:T(1024)S(1)} %add_rsqrt_fusion.2, ...), kind=kOutput, calls=%fused_computation.372 | convolution fusion | flops 11293555712 | bytes 22294400 | tf_op jit(solution)/shard_map/dot_general | solution.py:63
  434.5 47.3 %shard_map.467 = (bf16[672,384]{1,0:T(8,128)(2,1)S(1)}, f32[768,384]{1,0:T(8,128)S(1)}, f32[768,384]{1,0:T(8,128)}, f32[768,384]{1,0:T(8,128)}, f32[768,384]{1,0:T(8,128)}) custom-call(s32[2]{0:T(128)S(1)} %broadcast.412.kept_ref, bf16[672,384]{1,0:T(8,128)(2,1)S(1)} %convolution_convert_fusion.14.q_ref, ...), custom_call_target="tpu_custom_call" | custom-call | flops 3963617280 | bytes 11501568 | tf_op jit(solution)/shard_map/pallas_call | solution.py:195
  503.0 6.6 fusion.25
  517.0 18.1 %shard_map.468 = (bf16[288,1024]{1,0:T(8,128)(2,1)S(1)}, f32[288,1024]{1,0:T(8,128)S(1)}, f32[288,1024]{1,0:T(8,128)}, f32[288,1024]{1,0:T(8,128)}, f32[288,1024]{1,0:T(8,128)}) custom-call(s32[2]{0:T(128)S(1)} %copy-done.7, bf16[288,1024]{1,0:T(8,128)(2,1)S(1)} %copy-done.4, bf16[288,1024]{1,0:T(8,128)(2,1)S(1)} %fusion.142.g_ref, f32[288,1024]{1,0:T(8,128)} %copy-done.5, ...), custom_call_target="tpu_custom_call" | custom-call | flops 1698693120 | bytes 11796480 | tf_op jit(solution)/shard_map/pallas_call | solution.py:195
  543.9 7.3 convolution_convert_fusion.refs_2_
  554.4 5.1 fusion.158
  559.5 5.9 convolution_convert_fusion.1.refs_0_
  570.0 12.4 %shard_map.469.refs_4_ = bf16[5632,1024]{1,0:T(8,128)(2,1)} custom-call(bf16[288,1536]{1,0:T(8,128)(2,1)S(1)} %slice.286.x_ref, bf16[288,1024]{1,0:T(8,128)(2,1)S(1)} %add_convert_fusion.gx_ref, bf16[288,4096]{1,0:T(8,128)(2,1)} %copy-done.42, bf16[288,1024]{1,0:T(8,128)(2,1)S(1)} %add_convert_fusion.6.gh_ref), custom_call_target="tpu_custom_call" | custom-call | flops 3321888768 | bytes 14778368 | tf_op jit(solution)/shard_map/pallas_call | solution.py:301
  583.8 208.3 %shard_map.470 = (bf16[128,3072]{1,0:T(8,128)(2,1)}, bf16[128,1024]{1,0:T(8,128)(2,1)}, bf16[128,4096]{1,0:T(8,128)(2,1)}, bf16[128,512]{1,0:T(8,128)(2,1)}, bf1...) custom-call(bf16[1024,3072]{1,0:T(8,128)(2,1)} %convolution_convert_fusion.1.refs_0_, ...), custom_call_target="tpu_custom_call" | custom-call | tf_op jit(solution)/shard_map/pallas_call | solution.py:865
  800.7 7.3 multiply_add_fusion.1
  811.1 8.0 fusion.241
  (412 shorter events, 137.6 us)
Async XLA Ops:
  2.2 9.6 %slice-start = ((s8[4390912]{0:T(1024)(128)(4,1)}), s8[4194304]{0:T(1024)(128)(4,1)S(1)}, s32[]{:S(2)}) async-start(s8[4390912]{0:T(1024)(128)(4,1)} %bitcast.49), calls=%async_computation | async-start | bytes 8388608
  9.9 242.3 %collective-permute-start = (bf16[768,1536]{1,0:T(8,128)(2,1)}, bf16[768,1536]{1,0:T(8,128)(2,1)}, u32[]{:S(2)}, u32[]{:S(2)}) collective-permute-start(bf16[768,1536]{1,0:T(8,128)(2,1)} %fusion.54), channel_id=1, source_target_pairs={{0,1},{1,0},{2,3},{3,2},{4,5},{5,4},{6,7},{7,6},{8,9},{9,8},{10,11... | collective-permute-start | bytes 7077896 | tf_op jit(solution)/shard_map/ppermute | solution.py:256
  11.6 228.5 %collective-permute-start.1 = (s32[1537]{0:T(1024)S(1)}, s32[1537]{0:T(1024)S(1)}, u32[]{:S(2)}, u32[]{:S(2)}) collective-permute-start(s32[1537]{0:T(1024)S(1)} %pad_add_fusion), channel_id=1, source_target_pairs={{0,1},{1,0},{2,3},{3,2},{4,5},{5,4},{6,7},{7,6},{8,9},{9,8},{10,11... | collective-permute-start | bytes 18452 | tf_op jit(solution)/shard_map/ppermute | solution.py:256
  239.5 28.3 %copy-start.67 = (f32[1024]{0:T(1024)}, f32[1024]{0:T(1024)S(1)}, u32[]{:S(2)}) copy-start(f32[1024]{0:T(1024)S(1)} %get-tuple-element.229) | copy-start | bytes 12292
  243.1 34.1 %copy-start.6 = (s32[2]{0:T(128)}, s32[2]{0:T(128)S(1)}, u32[]{:S(2)}) copy-start(s32[2]{0:T(128)S(1)} %pad_add_fusion.1.kept_ref) | copy-start | bytes 28
  267.4 21.5 %copy-start.16 = (f32[288,1024]{1,0:T(8,128)}, f32[288,1024]{1,0:T(8,128)S(1)}, u32[]{:S(2)}) copy-start(f32[288,1024]{1,0:T(8,128)S(1)} %get-tuple-element.199) | copy-start | bytes 3538948
  271.9 5.3 collective-permute-start.2
  289.0 10.7 %slice-start.8 = ((s8[11534336]{0:T(1024)(128)(4,1)}), s8[4194304]{0:T(1024)(128)(4,1)S(1)}, s32[]{:S(2)}) async-start(s8[11534336]{0:T(1024)(128)(4,1)} %bitcast.60), calls=%async_computation.8 | async-start | bytes 8388608
  304.1 39.3 %copy-start.13 = (f32[768,384]{1,0:T(8,128)}, f32[768,384]{1,0:T(8,128)S(1)}, u32[]{:S(2)}) copy-start(f32[768,384]{1,0:T(8,128)S(1)} %get-tuple-element.189) | copy-start | bytes 3538948
  304.7 14.3 %copy-start.58 = (bf16[768,384]{1,0:T(8,128)(2,1)}, bf16[768,384]{1,0:T(8,128)(2,1)S(1)}, u32[]{:S(2)}) copy-start(bf16[768,384]{1,0:T(8,128)(2,1)S(1)} %multiply_convert_fusion.5) | copy-start | bytes 1769476
  307.1 13.5 %copy-start.8 = (bf16[768,768]{1,0:T(8,128)(2,1)}, bf16[768,768]{1,0:T(8,128)(2,1)S(1)}, u32[]{:S(2)}) copy-start(bf16[768,768]{1,0:T(8,128)(2,1)S(1)} %convolution_convert_fusion.7.k0_ref.v0_ref) | copy-start | bytes 3538948
  307.1 13.4 %collective-permute-start.3 = (bf16[768,768]{1,0:T(8,128)(2,1)S(1)}, bf16[768,768]{1,0:T(8,128)(2,1)S(1)}, u32[]{:S(2)}, u32[]{:S(2)}) collective-permute-start(bf16[768,768]{1,0:T(8,128)(2,1)S(1)} %convolution_convert_fusion.7.k0_ref.v0_ref), channel_id=1, source_target_pairs={{0,1},{1,0},{2,3},{3,2},{4,5},{5,4},{6,7},{7,6},{8,9},{9,8},{10,11... | collective-permute-start | bytes 3538952 | tf_op jit(solution)/shard_map/ppermute | solution.py:256
  314.4 38.0 %collective-permute-start.4 = (bf16[768,2048]{1,0:T(8,128)(2,1)}, bf16[768,2048]{1,0:T(8,128)(2,1)}, u32[]{:S(2)}, u32[]{:S(2)}) collective-permute-start(bf16[768,2048]{1,0:T(8,128)(2,1)} %fusion.57.k0_ref.v0_ref), channel_id=1, source_target_pairs={{0,1},{1,0},{2,3},{3,2},{4,5},{5,4},{6,7},{7,6},{8,9},{9,8},{10,11... | collective-permute-start | bytes 9437192 | tf_op jit(solution)/shard_map/ppermute | solution.py:256
  481.8 10.3 %collective-permute-start.5 = (f32[768,384]{1,0:T(8,128)}, f32[768,384]{1,0:T(8,128)S(1)}, u32[]{:S(2)}, u32[]{:S(2)}) collective-permute-start(f32[768,384]{1,0:T(8,128)} %get-tuple-element.85), channel_id=1, source_target_pairs={{0,1},{1,0},{2,3},{3,2},{4,5},{5,4},{6,7},{7,6},{8,9},{9,8},{10,11... | collective-permute-start | bytes 3538952 | tf_op jit(solution)/shard_map/ppermute | solution.py:256
  482.2 10.0 %collective-permute-start.6 = (f32[768,384]{1,0:T(8,128)}, f32[768,384]{1,0:T(8,128)S(1)}, u32[]{:S(2)}, u32[]{:S(2)}) collective-permute-start(f32[768,384]{1,0:T(8,128)} %get-tuple-element.87), channel_id=1, source_target_pairs={{0,1},{1,0},{2,3},{3,2},{4,5},{5,4},{6,7},{7,6},{8,9},{9,8},{10,11... | collective-permute-start | bytes 3538952 | tf_op jit(solution)/shard_map/ppermute | solution.py:256
  535.0 16.2 %collective-permute-start.7 = (f32[288,1024]{1,0:T(8,128)}, f32[288,1024]{1,0:T(8,128)}, u32[]{:S(2)}, u32[]{:S(2)}) collective-permute-start(f32[288,1024]{1,0:T(8,128)} %get-tuple-element.91), channel_id=1, source_target_pairs={{0,1},{1,0},{2,3},{3,2},{4,5},{5,4},{6,7},{7,6},{8,9},{9,8},{10,11... | collective-permute-start | bytes 3538952 | tf_op jit(solution)/shard_map/ppermute | solution.py:256
  535.4 17.5 %collective-permute-start.8 = (f32[288,1024]{1,0:T(8,128)}, f32[288,1024]{1,0:T(8,128)}, u32[]{:S(2)}, u32[]{:S(2)}) collective-permute-start(f32[288,1024]{1,0:T(8,128)} %get-tuple-element.93), channel_id=1, source_target_pairs={{0,1},{1,0},{2,3},{3,2},{4,5},{5,4},{6,7},{7,6},{8,9},{9,8},{10,11... | collective-permute-start | bytes 3538952 | tf_op jit(solution)/shard_map/ppermute | solution.py:256
  570.0 12.4 %copy-start.86 = (f32[48]{0:T(128)S(1)}, f32[48]{0:T(128)}, u32[]{:S(2)}) copy-start(f32[48]{0:T(128)} %pad.56.clone) | copy-start | bytes 580
  583.8 215.7 %copy-start.76 = (f32[128,3]{0,1:T(4,128)S(1)}, f32[128,3]{0,1:T(4,128)}, u32[]{:S(2)}) copy-start(f32[128,3]{0,1:T(4,128)} %param.33) | copy-start | bytes 4612
  583.8 215.7 %copy-start.78 = (f32[128,3]{0,1:T(4,128)S(1)}, f32[128,3]{0,1:T(4,128)}, u32[]{:S(2)}) copy-start(f32[128,3]{0,1:T(4,128)} %param.49) | copy-start | bytes 4612
  583.8 215.7 %copy-start.82 = (f32[128,3]{0,1:T(4,128)S(1)}, f32[128,3]{0,1:T(4,128)}, u32[]{:S(2)}) copy-start(f32[128,3]{0,1:T(4,128)} %param.39) | copy-start | bytes 4612
  583.8 215.7 %copy-start.83 = (f32[128,3]{0,1:T(4,128)S(1)}, f32[128,3]{0,1:T(4,128)}, u32[]{:S(2)}) copy-start(f32[128,3]{0,1:T(4,128)} %param.45) | copy-start | bytes 4612
  583.8 216.9 %copy-start.25 = (f32[704,1024]{1,0:T(8,128)S(1)}, f32[704,1024]{1,0:T(8,128)}, u32[]{:S(2)}) copy-start(f32[704,1024]{1,0:T(8,128)} %param.48) | copy-start | bytes 8650756
  807.9 11.1 %copy-start.27 = (f32[704,1024]{1,0:T(8,128)}, f32[704,1024]{1,0:T(8,128)S(1)}, u32[]{:S(2)}) copy-start(f32[704,1024]{1,0:T(8,128)S(1)} %get-tuple-element.161) | copy-start | bytes 8650756
  (93 other events, 345.0 us)

commit v3 on v2

--- a/solution.py
+++ b/solution.py
@@ -107,7 +107,8 @@
         merged = jnp.where(chosen, outcome / row_total, merged)
         log_totals = jnp.where(chosen, row_max + jnp.log2(row_total), log_totals)
     o_ref[...] = merged.astype(o_ref.dtype)
-    l_ref[...] = log_totals
+    if l_ref is not None:
+        l_ref[...] = log_totals
 
 
 def attend_rows(queries, kv_near, kv_far, kept, num_heads, block_rows):
@@ -321,10 +322,25 @@
 MESH = pl.DeviceIdType.MESH
 
 
+def normed_rows(source, target, rows, gain_row, chunk, twice=False):
+    def step(i, carried_through):
+        at = pl.ds(pl.multiple_of(i * chunk, 16), chunk)
+        values = normed(source[at, :]) * gain_row
+        if twice:
+            values = normed(values)
+        target[at, :] = values.astype(target.dtype)
+        return carried_through
+
+    lax.fori_loop(0, rows // chunk, step, 0)
+
+
 def gather_kernel(count, zn, *refs):
-    ins, outs = refs[:count], refs[count : 2 * count]
-    stages = refs[2 * count : 3 * count]
-    local_sem, z_send, z_recv, p_send, p_recv = refs[3 * count :]
+    ins, refs = refs[:count], refs[count:]
+    chosen_ref, table_ref, *refs = refs
+    outs, goal_ref, refs = refs[:count], refs[count], refs[count + 1 :]
+    stages, refs = refs[:count], refs[count:]
+    facts_ref, t0_ref, a_ref, near_ref, far_ref, q_ref, o_ref, h_ref, sum_ref, embed_buf, qkv_buf, up_buf, down_buf, *refs = refs
+    local_sem, z_send, z_recv, p_send, p_recv, w_sem, kv_sem = refs
     section, place = lax.axis_index("section"), lax.axis_index("dp")
     z, core = place // 2, place % 2
     near = {"section": section + 1 - 2 * (section % 2)}
@@ -397,14 +413,17 @@
         return copy(part, part, p_send, p_recv, index, (near, far, far, near, mate)[kind])
 
     own = []
-    ranked = sorted(range(count), key=lambda a: ins[a].shape[0] * ins[a].shape[1])
-    for a in ranked:
+    def offered(a):
         for upward in (True, False):
 
             @pl.when(sends_along(1, upward))
-            def _(a=a, upward=upward):
+            def _(upward=upward):
                 along(a, 1, upward).start()
 
+    for a in range(2):
+        offered(a)
+
+    settled = []
     for a in range(count):
         take = pltpu.make_async_copy(ins[a], stages[a], local_sem.at[a])
         take.start()
@@ -420,8 +439,8 @@
 
     items = [
         (a, step, upward)
+        for a in range(count)
         for step in range(1, zn)
-        for a in ranked
         for upward in (True, False)
     ]
 
@@ -456,18 +475,161 @@
             in_plane(a, step, upward, 3).wait_recv()
             in_plane(a, step, upward, 4).start()
 
-    lag = 4
-    for i in range(len(items) + 2 * lag):
+    lag = 3
+    group = 2 * (zn - 1)
+
+    def advance(i):
+        if i % group == 0 and 2 <= i // group + 1 < count:
+            offered(i // group + 1)
+        if 0 <= i - 2 * lag < len(items):
+            completed(*items[i - 2 * lag])
+        if 0 <= i - lag < len(items):
+            passed_on(*items[i - lag])
         if i < len(items):
             received(*items[i])
-        if 0 <= i - lag < len(items):
-            passed_on(*items[i - lag])
-        if 0 <= i - 2 * lag < len(items):
-            completed(*items[i - 2 * lag])
-
+
+    def settle(a):
+        take, keep, give = own[a]
+        keep.wait()
+        give.wait_recv()
+        for b, step, upward in items:
+            if b == a:
+
+                @pl.when(arrives(step, upward))
+                def _(step=step, upward=upward):
+                    in_plane(a, step, upward, 4).wait_recv()
+
+        settled.append(a)
+
+    def run_loop(length, body, steps):
+        def step(i, carried_through):
+            body(i)
+            for at, move in enumerate(steps):
+                pl.when(i == at * length // len(steps))(functools.partial(advance, move))
+            return carried_through
+
+        lax.fori_loop(0, length, step, 0)
+
+    def streamed(length, fetches, body, steps):
+        for fetch in fetches:
+            fetch(0).start()
+
+        def with_blocks(i):
+            @pl.when(i + 1 < length)
+            def _():
+                for fetch in fetches:
+                    fetch(i + 1).start()
+
+            for fetch in fetches:
+                fetch(i).wait()
+            body(i, i % 2)
+
+        run_loop(length, with_blocks, steps)
+
+    def column_fetch(a, rows, first, width, buffer, sem):
+        def fetch(i):
+            columns = pl.ds(pl.multiple_of(first + i * width, 128), width)
+            return pltpu.make_async_copy(
+                outs[a].at[rows, columns], buffer.at[i % 2], w_sem.at[sem * 2 + i % 2]
+            )
+
+        return fetch
+
+    ends = [group * (a + 1) + 2 * lag for a in range(count)]
+    last = len(items) + 2 * lag
+    SMALL, TALL, WIDE = 0, 1, 2
+    for i in range(min(ends[TALL], last)):
+        advance(i)
+    settle(SMALL)
+    settle(TALL)
+    facts = pltpu.make_async_copy(outs[SMALL].at[:, PD : PD + LANES], facts_ref, local_sem.at[SMALL])
+    facts.start()
+
+    def embed(i, slot):
+        at = pl.ds(pl.multiple_of(i * 256, 128), 256)
+        t0_ref[:, at] = matmul(chosen_ref[...], embed_buf[slot]) + table_ref[:, at]
+
+    waiting = list(range(ends[TALL], min(ends[WIDE], last)))
+    streamed(4, [column_fetch(TALL, pl.ds(0, PATCH), 0, 256, embed_buf, 0)], embed, waiting[:2])
+    facts.wait()
+    gain_rows = jnp.transpose(facts_ref[...].astype(jnp.float32))
+    normed_rows(t0_ref, a_ref, HALF, gain_rows[3:4, :], 96)
+    for i in waiting[2:]:
+        advance(i)
+    settle(WIDE)
+
+    rest = list(range(ends[WIDE], last))
+    cuts = [len(rest) * part // 80 for part in (0, 8, 12, 48, 54, 80)]
+    rest = [rest[cuts[i] : cuts[i + 1]] for i in range(5)]
+    whole_rows = pl.ds(0, D)
+
+    def keys_values(i, slot):
+        at = pl.ds(pl.multiple_of(i * 256, 128), 256)
+        near_ref[:, at] = matmul(a_ref[...], qkv_buf[slot]).astype(jnp.bfloat16)
+
+    def queries(i, slot):
+        at = pl.ds(pl.multiple_of(i * 256, 128), 256)
+        q_ref[:, at] = matmul(a_ref[SKIP:, :], qkv_buf[slot]).astype(jnp.bfloat16)
+
+    streamed(8, [column_fetch(WIDE, whole_rows, D, 256, qkv_buf, 1)], keys_values, rest[0])
+    share = pltpu.make_async_remote_copy(
+        src_ref=near_ref,
+        dst_ref=far_ref,
+        send_sem=kv_sem.at[0],
+        recv_sem=kv_sem.at[1],
+        device_id=mate,
+        device_id_type=MESH,
+    )
+    share.start()
+    streamed(4, [column_fetch(WIDE, whole_rows, 0, 256, qkv_buf, 1)], queries, rest[1])
+    share.wait()
+    block_rows = (HALF - SKIP) // 2
+
+    def attention(i):
+        lanes = pl.ds(pl.multiple_of(i // 2 * LANES, LANES), LANES)
+        values = pl.ds(pl.multiple_of(D + i // 2 * LANES, LANES), LANES)
+        rows = pl.ds(pl.multiple_of(i % 2 * block_rows, 16), block_rows)
+        attend_kernel(
+            D // HE, False, None, q_ref.at[rows, lanes], near_ref.at[:, lanes],
+            near_ref.at[:, values], far_ref.at[:, lanes], far_ref.at[:, values],
+            o_ref.at[rows, lanes], None,
+        )
+
+    run_loop(2 * D // LANES, attention, rest[2])
+
+    def merge(i, slot):
+        at = pl.ds(pl.multiple_of(i * 256, 128), 256)
+        stream = t0_ref[SKIP:, at] + matmul(o_ref[...], qkv_buf[slot])
+        sum_ref[:, at] = stream.astype(jnp.bfloat16).astype(jnp.float32)
+
+    streamed(4, [column_fetch(WIDE, whole_rows, 3 * D, 256, qkv_buf, 1)], merge, rest[3])
+
+    row_count = HALF - SKIP
+    normed_rows(sum_ref, a_ref, row_count, gain_rows[4:5, :], 96)
+
+    def down_fetch(i):
+        rows = pl.ds(pl.multiple_of(PATCH + i * 512, 16), 512)
+        return pltpu.make_async_copy(outs[TALL].at[rows, :], down_buf.at[i % 2], w_sem.at[6 + i % 2])
+
+    def feed(i, slot):
+        for part in range(2):
+            rows = pl.ds(part * block_rows, block_rows)
+            h_ref[...] = gelu_erf(matmul(a_ref[rows, :], up_buf[slot])).astype(jnp.bfloat16)
+            sum_ref[rows, :] += matmul(h_ref[...], down_buf[slot])
+
+    streamed(
+        8,
+        [column_fetch(WIDE, whole_rows, 4 * D, 512, up_buf, 2), down_fetch],
+        feed,
+        rest[4],
+    )
+    normed_rows(sum_ref, goal_ref, row_count, gain_rows[5:6, :], 96, twice=True)
+
+    for a in range(count):
+        if a not in settled:
+            settle(a)
     for take, keep, give in own:
-        keep.wait()
-        give.wait()
+        give.wait_send()
     for a, step, upward in items:
 
         @pl.when(sends_along(step, upward))
@@ -478,33 +640,52 @@
         def _(a=a, step=step, upward=upward):
             for kind in range(5):
                 in_plane(a, step, upward, kind).wait_send()
-            in_plane(a, step, upward, 4).wait_recv()
-
-
-def gather_blocks(blocks):
+
+
+def gather_and_teach(blocks, chosen, table):
     count = len(blocks)
     dp_size = lax.axis_size("dp")
     zn = dp_size // 2
     return pl.pallas_call(
         functools.partial(gather_kernel, count, zn),
-        in_specs=[pl.BlockSpec(memory_space=pl.ANY)] * count,
-        out_specs=[pl.BlockSpec(memory_space=pl.ANY)] * count,
+        in_specs=[pl.BlockSpec(memory_space=pl.ANY)] * count
+        + [pl.BlockSpec(memory_space=pltpu.VMEM)] * 2,
+        out_specs=[pl.BlockSpec(memory_space=pl.ANY)] * count
+        + [pl.BlockSpec(memory_space=pltpu.VMEM)],
         out_shape=[
             jax.ShapeDtypeStruct((member.shape[0] * dp_size, member.shape[1]), member.dtype)
             for member in blocks
-        ],
+        ]
+        + [jax.ShapeDtypeStruct((HALF - SKIP, D), jnp.bfloat16)],
         scratch_shapes=[pltpu.VMEM(member.shape, member.dtype) for member in blocks]
+        + [
+            pltpu.VMEM((D, LANES), jnp.bfloat16),
+            pltpu.VMEM((HALF, D), jnp.float32),
+            pltpu.VMEM((HALF, D), jnp.bfloat16),
+            pltpu.VMEM((HALF, 2 * D), jnp.bfloat16),
+            pltpu.VMEM((HALF, 2 * D), jnp.bfloat16),
+            pltpu.VMEM((HALF - SKIP, D), jnp.bfloat16),
+            pltpu.VMEM((HALF - SKIP, D), jnp.bfloat16),
+            pltpu.VMEM(((HALF - SKIP) // 2, 512), jnp.bfloat16),
+            pltpu.VMEM((HALF - SKIP, D), jnp.float32),
+            pltpu.VMEM((2, PATCH, 256), jnp.bfloat16),
+            pltpu.VMEM((2, D, 256), jnp.bfloat16),
+            pltpu.VMEM((2, D, 512), jnp.bfloat16),
+            pltpu.VMEM((2, 512, D), jnp.bfloat16),
+        ]
         + [
             pltpu.SemaphoreType.DMA((count,)),
             pltpu.SemaphoreType.DMA((count * (zn - 1) * 2,)),
             pltpu.SemaphoreType.DMA((count * (zn - 1) * 2,)),
             pltpu.SemaphoreType.DMA((count * ((zn - 1) * 10 + 1),)),
             pltpu.SemaphoreType.DMA((count * ((zn - 1) * 10 + 1),)),
+            pltpu.SemaphoreType.DMA((8,)),
+            pltpu.SemaphoreType.DMA((2,)),
         ],
         compiler_params=pltpu.CompilerParams(
             collective_id=0, has_side_effects=True, vmem_limit_bytes=VMEM_LIMIT
         ),
-    )(*blocks)
+    )(*blocks, chosen, table)
 
 
 def upper_rows(size):
@@ -975,22 +1156,23 @@
     pred_block = pred_weight.shape if pred_weight.shape[0] % 16 == 0 else (-1, D)
     pred_form = (PD, pred_weight.shape[1]) if pred_weight.shape[0] % 16 == 0 else (-1, D)
     blocks = (
+        small,
+        teacher_tall,
         teacher_wide,
-        teacher_tall,
+        tall_weight,
         wide_weight[:, : 4 * D + FF],
-        tall_weight,
         pred_weight.reshape(pred_block),
-        small,
         jnp.pad(pred_down, ((0, 0), (0, LANES))),
     )
-    teach_wide, teach_tall, w_wide, w_tall, w_pred, w_small, w_down = gather_blocks(
-        tuple(member.astype(jnp.bfloat16) for member in blocks)
-    )
+    table = position_table(order, D)
+    w_small, teach_tall, teach_wide, w_tall, w_wide, w_pred, w_down, goal = gather_and_teach(
+        tuple(member.astype(jnp.bfloat16) for member in blocks), chosen, table
+    )
+    goal = goal.astype(jnp.float32)
     w_pred = w_pred.reshape(PD, -1)
     w_down = w_down[:, :PD]
     pred_embed = w_small[:, :PD]
     enc_copy = w_small[:, PD : PD + 3]
-    teach_copy = w_small[:, PD + 3 : PD + 6]
     pred_copy = w_small[:, PD + 6 : PD + 10].reshape(dp_size, row_count, 4)
     pred_copy = pred_copy[:, : pred_gains.shape[0]].reshape(PD, 4)
     counts = w_small[::row_count, PD + LANES - 2 * clips_here :].astype(jnp.float32)
@@ -998,28 +1180,15 @@
     target_total = jnp.sum(L - counts)
     enc_gain = enc_copy.astype(jnp.float32)
     pred_gain = pred_copy.astype(jnp.float32)
-    teach_gain = teach_copy.astype(jnp.float32)
     enc_attn = (w_wide[:, : 3 * D], w_wide[:, 3 * D : 4 * D])
     enc_feed = (w_wide[:, 4 * D : 4 * D + FF], w_tall[PATCH:])
     pred_attn = (w_pred[:, : 3 * PD], w_pred[:, 3 * PD : 4 * PD])
     pred_feed = (w_pred[:, 4 * PD : 4 * PD + PF], w_down)
     pred_head = w_pred[:, 4 * PD + PF :]
 
-    table = position_table(order, D)
     pred_table = position_table(order, PD)
     row_ids = lax.iota(jnp.int32, HALF)
     context = (row_ids < seen_near)[:, None]
-
-    teach_stream = matmul(chosen, teach_tall[:PATCH]) + table
-    teach_stream, discarded_value = attend_fwd(
-        teach_stream, teach_gain[:, 0], teach_wide[:, : 3 * D], teach_wide[:, 3 * D : 4 * D],
-        HE, None, SKIP, 336,
-    )
-    teach_stream = teach_stream.astype(jnp.bfloat16).astype(jnp.float32)
-    teach_stream, discarded_value = feed_fwd(
-        teach_stream, teach_gain[:, 1], teach_wide[:, 4 * D :], teach_tall[PATCH:]
-    )
-    goal = normed(scaled(teach_stream, teach_gain[:, 2])).astype(jnp.bfloat16).astype(jnp.float32)
 
     enc_chosen = chosen[:SEEN]
     stream_a = matmul(enc_chosen, w_tall[:PATCH]) + table[:SEEN]

time: 835 us -> 799 us (0.957)
  matrix products: 145 us -> 106 us
    dot_general x20 -> x15, matrix products: 90.9 us -> 47.9 us  [matmul(): return jnp.dot(left, right, preferred_element_type=jnp.float32)]
    pallas_call x3 -> x2, Pallas kernels: 70.4 us -> 32.8 us  [attend_rows(): pl.pallas_call(functools.partial(attend_kernel, width // num_heads, maske...]
    pallas_call x1, Pallas kernels: 215 us -> 248 us  [gather_and_teach(): pl.pallas_call(functools.partial(gather_kernel, count, zn), in_specs=[pl....]
  transfers between devices with their start and end apart: 9 -> 8, of which waited for: 0 -> 0; matrix products, arithmetic and copies ran while one was open for 9% -> 8% of each run, Pallas kernels for 29% -> 0%
where the time goes in v3:
time: 799 us; the launch traced here: 789 us
  Pallas kernels  573 us (72%)
  matrix products  106 us (13%)
  other arithmetic  72.8 us (9%)
  local copies, waits for them, and re-layouts  28.7 us (4%)
    pallas_call x1, Pallas kernels, gather_and_teach(): pl.pallas_call(functools.partial(gather_kernel, count, zn), in_specs=[pl....  248 us
    pallas_call x1, Pallas kernels, reduce_blocks(): pl.pallas_call(functools.partial(reduce_kernel, count, zn), in_specs=[any...  215 us
    pallas_call x2, Pallas kernels, attend_rows_back(): pl.pallas_call(functools.partial(attend_back_kernel, width // num_heads,...  65.4 us
    dot_general x15, matrix products, matmul(): return jnp.dot(left, right, preferred_element_type=jnp.float32)  47.9 us
    pallas_call x2, Pallas kernels, attend_rows(): pl.pallas_call(functools.partial(attend_kernel, width // num_heads, maske...  32.8 us
    dot_general x10, matrix products, outer_rows(): lax.dot_general(left, right, (((1,), (1,)), ((), ())), preferred_element_...  30.3 us
    dot_general x9, matrix products, inner_rows(): lax.dot_general(left, right, (((0,), (0,)), ((), ())), preferred_element_...  27.6 us
  transfers between devices with their start and end apart: 8, of which 0 were waited for; matrix products, arithmetic and copies ran while one was open for 8% of the time, Pallas kernels for 0%

profile of v3, /device:TPU:0, one launch (start us, length us, event | category | flops | bytes accessed | tf_op | source)
XLA Modules:
  0.0 789.5 jit_solution(15764106997186099189)
XLA Ops:
  2.2 7.6 fusion.46
  16.6 3.9 convert_element_type.260.refs_2_
  26.5 5.5 multiply_sine_fusion
  34.1 5.6 fusion.51.refs_7_
  39.7 247.6 %shard_map.463 = (bf16[1024,512]{1,0:T(8,128)(2,1)S(1)}, bf16[5632,1024]{1,0:T(8,128)(2,1)}, bf16[1024,8192]{1,0:T(8,128)(2,1)}, bf16[5632,1024]{1,0:T(8,128)(2,...) custom-call(bf16[128,512]{1,0:T(8,128)(2,1)S(1)} %concatenate.38.ref, ...), custom_call_target="tpu_custom_call" | custom-call | tf_op jit(solution)/shard_map/pallas_call | solution.py:649
  287.3 3.5 fusion.196
  292.2 3.8 fusion.55.k0_ref.v0_ref
  298.2 4.3 multiply_sine_fusion.1
  306.4 10.8 %shard_map.464 = (bf16[288,1024]{1,0:T(8,128)(2,1)S(1)}, f32[288,1024]{1,0:T(8,128)S(1)}) custom-call(s32[2]{0:T(128)S(1)} %pad_add_fusion.1.kept_ref, bf16[288,1024]{1,0:T(8,128)(2,1)S(1)} %fusion.98.q_ref, bf16[288,2048]{1,0:T(8,128)(2,1)S(1)} %fusion.55.k0_ref.v0_ref, bf16[288,2048]{1,0:T(8,128)(2,1)S(1)} %fusion.55.k0_ref.v0_ref, ...), custom_call_target="tpu_custom_call" | custom-call | flops 679477248 | bytes 4718592 | tf_op jit(solution)/shard_map/pallas_call | solution.py:124
  317.3 3.2 convert_reduce_fusion
  320.9 7.3 multiply_convert_fusion
  343.8 22.0 %shard_map.465 = (bf16[672,384]{1,0:T(8,128)(2,1)S(1)}, f32[672,384]{1,0:T(8,128)S(1)}) custom-call(s32[2]{0:T(128)S(1)} %broadcast.338.kept_ref, bf16[672,384]{1,0:T(8,128)(2,1)S(1)} %convolution_convert_fusion.14.q_ref, bf16[768,768]{1,0:T(8,128)(2,1)} %convolution_convert_fusion.7.k0_ref.v0_ref, bf16[768,768]{1,0:T(8,128)(2,1)} %convolution_convert_fusion.7.k0_ref.v0_ref, ...), custom_call_target="tpu_custom_call" | custom-call | flops 1585446912 | bytes 4423680 | tf_op jit(solution)/shard_map/pallas_call | solution.py:124
  374.2 3.7 select_reduce_fusion
  384.9 47.3 %shard_map.466 = (bf16[672,384]{1,0:T(8,128)(2,1)S(1)}, f32[768,384]{1,0:T(8,128)S(1)}, f32[768,384]{1,0:T(8,128)}, f32[768,384]{1,0:T(8,128)}, f32[768,384]{1,0:T(8,128)}) custom-call(s32[2]{0:T(128)S(1)} %broadcast.338.kept_ref, bf16[672,384]{1,0:T(8,128)(2,1)S(1)} %convolution_convert_fusion.14.q_ref, ...), custom_call_target="tpu_custom_call" | custom-call | flops 3963617280 | bytes 11501568 | tf_op jit(solution)/shard_map/pallas_call | solution.py:196
  453.8 6.6 fusion.19
  460.4 7.0 fusion.119
  471.8 18.0 %shard_map.467 = (bf16[288,1024]{1,0:T(8,128)(2,1)S(1)}, f32[288,1024]{1,0:T(8,128)S(1)}, f32[288,1024]{1,0:T(8,128)}, f32[288,1024]{1,0:T(8,128)}, f32[288,1024]{1,0:T(8,128)}) custom-call(s32[2]{0:T(128)S(1)} %pad_add_fusion.1.kept_ref, bf16[288,1024]{1,0:T(8,128)(2,1)S(1)} %fusion.98.q_ref, bf16[288,1024]{1,0:T(8,128)(2,1)S(1)} %fusion.95.g_ref, ...), custom_call_target="tpu_custom_call" | custom-call | flops 1698693120 | bytes 11796480 | tf_op jit(solution)/shard_map/pallas_call | solution.py:196
  500.2 7.2 convolution_convert_fusion.refs_2_
  510.8 5.1 fusion.111
  515.9 5.7 convolution_convert_fusion.1.refs_0_
  524.6 12.3 %shard_map.468.refs_4_ = bf16[5632,1024]{1,0:T(8,128)(2,1)} custom-call(bf16[288,1536]{1,0:T(8,128)(2,1)S(1)} %slice.235.x_ref, bf16[288,1024]{1,0:T(8,128)(2,1)S(1)} %add_convert_fusion.gx_ref, bf16[288,4096]{1,0:T(8,128)(2,1)} %copy-done.37, bf16[288,1024]{1,0:T(8,128)(2,1)S(1)} %add_convert_fusion.6.gh_ref), custom_call_target="tpu_custom_call" | custom-call | flops 3321888768 | bytes 14778368 | tf_op jit(solution)/shard_map/pallas_call | solution.py:302
  538.3 215.1 %shard_map.469 = (bf16[128,3072]{1,0:T(8,128)(2,1)}, bf16[128,1024]{1,0:T(8,128)(2,1)}, bf16[128,4096]{1,0:T(8,128)(2,1)}, bf16[128,512]{1,0:T(8,128)(2,1)}, bf1...) custom-call(bf16[1024,3072]{1,0:T(8,128)(2,1)} %convolution_convert_fusion.1.refs_0_, ...), custom_call_target="tpu_custom_call" | custom-call | tf_op jit(solution)/shard_map/pallas_call | solution.py:1046
  762.0 7.3 multiply_add_fusion.1
  772.4 8.0 %fusion.191 = (bf16[128,8576]{1,0:T(8,128)(2,1)}, f32[128,8576]{1,0:T(8,128)S(1)}, f32[128,8576]{1,0:T(8,128)}, f32[128,8576]{1,0:T(8,128)}) fusion(f32[128,8576]{1,0:T(8,128)S(1)} %bitcast.47, f32[]{:T(128)S(6)} %min.3, bf16[128,384]{1,0:T(8,128)(2,1)S(1)} %slice.228, bf16[128,4096]{1,0:T(8,128)(2,1)S(1)} %copy-done.44, ...), kind=kLoop, calls=%fused_computation.312 | loop fusion | flops 27443200 | bytes 30736388 | tf_op jit(solution)/shard_map/convert_element_type | solution.py:1342
  (378 shorter events, 114.5 us)
Async XLA Ops:
  9.7 24.3 %collective-permute-start = (bf16[768,1536]{1,0:T(8,128)(2,1)}, bf16[768,1536]{1,0:T(8,128)(2,1)}, u32[]{:S(2)}, u32[]{:S(2)}) collective-permute-start(bf16[768,1536]{1,0:T(8,128)(2,1)} %fusion.46), channel_id=1, source_target_pairs={{0,1},{1,0},{2,3},{3,2},{4,5},{5,4},{6,7},{7,6},{8,9},{9,8},{10,11... | collective-permute-start | bytes 7077896 | tf_op jit(solution)/shard_map/ppermute | solution.py:257
  11.4 13.8 %collective-permute-start.1 = (s32[1537]{0:T(1024)S(1)}, s32[1537]{0:T(1024)S(1)}, u32[]{:S(2)}, u32[]{:S(2)}) collective-permute-start(s32[1537]{0:T(1024)S(1)} %pad_add_fusion), channel_id=1, source_target_pairs={{0,1},{1,0},{2,3},{3,2},{4,5},{5,4},{6,7},{7,6},{8,9},{9,8},{10,11... | collective-permute-start | bytes 18452 | tf_op jit(solution)/shard_map/ppermute | solution.py:257
  39.7 247.6 %copy-start.29 = (bf16[768,1536]{1,0:T(8,128)(2,1)S(1)}, bf16[768,1536]{1,0:T(8,128)(2,1)}, u32[]{:S(2)}) copy-start(bf16[768,1536]{1,0:T(8,128)(2,1)} %fusion.51.refs_7_) | copy-start | bytes 7077892
  291.9 40.8 %copy-start.71 = (f32[1024]{0:T(1024)}, f32[1024]{0:T(1024)S(1)}, u32[]{:S(2)}) copy-start(f32[1024]{0:T(1024)S(1)} %get-tuple-element.140) | copy-start | bytes 12292
  296.0 10.4 %collective-permute-start.2 = (bf16[288,2048]{1,0:T(8,128)(2,1)S(1)}, bf16[288,2048]{1,0:T(8,128)(2,1)}, u32[]{:S(2)}, u32[]{:S(2)}) collective-permute-start(bf16[288,2048]{1,0:T(8,128)(2,1)S(1)} %fusion.55.k0_ref.v0_ref), channel_id=1, source_target_pairs={{0,1},{1,0},{2,3},{3,2},{4,5},{5,4},{6,7},{7,6},{8,9},{9,8},{10,11... | collective-permute-start | bytes 3538952 | tf_op jit(solution)/shard_map/ppermute | solution.py:257
  298.2 41.9 %copy-start.74 = (pred[768]{0:T(1024)(128)(4,1)}, pred[768]{0:T(1024)(128)(4,1)S(1)}, u32[]{:S(2)}) copy-start(pred[768]{0:T(1024)(128)(4,1)S(1)} %iota_compare_fusion.12) | copy-start | bytes 2308
  303.8 31.3 %copy-start.65 = (f32[384]{0:T(512)}, f32[384]{0:T(512)S(1)}, u32[]{:S(2)}) copy-start(f32[384]{0:T(512)S(1)} %get-tuple-element.147) | copy-start | bytes 4612
  306.4 10.8 %copy-start.14 = (f32[288,1024]{1,0:T(8,128)S(1)}, f32[288,1024]{1,0:T(8,128)}, u32[]{:S(2)}) copy-start(f32[288,1024]{1,0:T(8,128)} %copy-done.13) | copy-start | bytes 3538948
  317.3 12.4 %slice-start.3 = ((s8[11534336]{0:T(1024)(128)(4,1)}), s8[4194304]{0:T(1024)(128)(4,1)S(1)}, s32[]{:S(2)}) async-start(s8[11534336]{0:T(1024)(128)(4,1)} %bitcast.53), calls=%async_computation.3 | async-start | bytes 8388608
  320.5 148.2 %copy-start.60 = (f32[288]{0:T(512)}, f32[288]{0:T(512)S(1)}, u32[]{:S(2)}) copy-start(f32[288]{0:T(512)S(1)} %broadcast_multiply_fusion.4) | copy-start | bytes 3460
  320.8 147.8 %copy-start.67 = (f32[288]{0:T(512)}, f32[288]{0:T(512)S(1)}, u32[]{:S(2)}) copy-start(f32[288]{0:T(512)S(1)} %fusion.160) | copy-start | bytes 3460
  339.1 4.7 collective-permute-start.3
  343.8 22.1 %copy-start.12 = (f32[768,384]{1,0:T(8,128)S(1)}, f32[768,384]{1,0:T(8,128)}, u32[]{:S(2)}) copy-start(f32[768,384]{1,0:T(8,128)} %copy-done.11) | copy-start | bytes 3538948
  432.2 10.3 %collective-permute-start.4 = (f32[768,384]{1,0:T(8,128)}, f32[768,384]{1,0:T(8,128)S(1)}, u32[]{:S(2)}, u32[]{:S(2)}) collective-permute-start(f32[768,384]{1,0:T(8,128)} %get-tuple-element.81), channel_id=1, source_target_pairs={{0,1},{1,0},{2,3},{3,2},{4,5},{5,4},{6,7},{7,6},{8,9},{9,8},{10,11... | collective-permute-start | bytes 3538952 | tf_op jit(solution)/shard_map/ppermute | solution.py:257
  432.4 10.3 %collective-permute-start.5 = (f32[768,384]{1,0:T(8,128)}, f32[768,384]{1,0:T(8,128)S(1)}, u32[]{:S(2)}, u32[]{:S(2)}) collective-permute-start(f32[768,384]{1,0:T(8,128)} %get-tuple-element.83), channel_id=1, source_target_pairs={{0,1},{1,0},{2,3},{3,2},{4,5},{5,4},{6,7},{7,6},{8,9},{9,8},{10,11... | collective-permute-start | bytes 3538952 | tf_op jit(solution)/shard_map/ppermute | solution.py:257
  490.7 16.7 %collective-permute-start.6 = (f32[288,1024]{1,0:T(8,128)}, f32[288,1024]{1,0:T(8,128)}, u32[]{:S(2)}, u32[]{:S(2)}) collective-permute-start(f32[288,1024]{1,0:T(8,128)} %get-tuple-element.87), channel_id=1, source_target_pairs={{0,1},{1,0},{2,3},{3,2},{4,5},{5,4},{6,7},{7,6},{8,9},{9,8},{10,11... | collective-permute-start | bytes 3538952 | tf_op jit(solution)/shard_map/ppermute | solution.py:257
  490.8 18.2 %collective-permute-start.7 = (f32[288,1024]{1,0:T(8,128)}, f32[288,1024]{1,0:T(8,128)}, u32[]{:S(2)}, u32[]{:S(2)}) collective-permute-start(f32[288,1024]{1,0:T(8,128)} %get-tuple-element.89), channel_id=1, source_target_pairs={{0,1},{1,0},{2,3},{3,2},{4,5},{5,4},{6,7},{7,6},{8,9},{9,8},{10,11... | collective-permute-start | bytes 3538952 | tf_op jit(solution)/shard_map/ppermute | solution.py:257
  524.6 12.4 %copy-start.62 = (f32[12,128]{1,0:T(8,128)S(1)}, f32[12,128]{1,0:T(8,128)}, u32[]{:S(2)}) copy-start(f32[12,128]{1,0:T(8,128)} %reshape.329) | copy-start | bytes 18436
  524.6 12.4 %copy-start.88 = (f32[48]{0:T(128)S(1)}, f32[48]{0:T(128)}, u32[]{:S(2)}) copy-start(f32[48]{0:T(128)} %pad.56.clone) | copy-start | bytes 580
  538.3 222.5 %copy-start.77 = (f32[128,3]{0,1:T(4,128)S(1)}, f32[128,3]{0,1:T(4,128)}, u32[]{:S(2)}) copy-start(f32[128,3]{0,1:T(4,128)} %param.33) | copy-start | bytes 4612
  538.3 222.5 %copy-start.79 = (f32[128,3]{0,1:T(4,128)S(1)}, f32[128,3]{0,1:T(4,128)}, u32[]{:S(2)}) copy-start(f32[128,3]{0,1:T(4,128)} %param.49) | copy-start | bytes 4612
  538.3 222.5 %copy-start.84 = (f32[128,3]{0,1:T(4,128)S(1)}, f32[128,3]{0,1:T(4,128)}, u32[]{:S(2)}) copy-start(f32[128,3]{0,1:T(4,128)} %param.39) | copy-start | bytes 4612
  538.3 222.5 %copy-start.85 = (f32[128,3]{0,1:T(4,128)S(1)}, f32[128,3]{0,1:T(4,128)}, u32[]{:S(2)}) copy-start(f32[128,3]{0,1:T(4,128)} %param.45) | copy-start | bytes 4612
  538.3 223.7 %copy-start.19 = (f32[704,1024]{1,0:T(8,128)S(1)}, f32[704,1024]{1,0:T(8,128)}, u32[]{:S(2)}) copy-start(f32[704,1024]{1,0:T(8,128)} %param.48) | copy-start | bytes 8650756
  (87 other events, 315.3 us)

commit v4 on v3

--- a/solution.py
+++ b/solution.py
@@ -247,11 +247,6 @@
     return (grad_out + grad_stream, grad_wup, branch_grad, grad_gain)
 
 
-def picked_rows(table, row_ids):
-    choice = row_ids[:, None] == lax.iota(jnp.int32, table.shape[0])[None, :]
-    return matmul(choice.astype(table.dtype), table).astype(table.dtype)
-
-
 def swapped(block):
     devices = range(lax.axis_size("dp"))
     return lax.ppermute(block, "dp", [(i, i ^ 1) for i in devices])
@@ -336,10 +331,12 @@
 
 def gather_kernel(count, zn, *refs):
     ins, refs = refs[:count], refs[count:]
-    chosen_ref, table_ref, *refs = refs
-    outs, goal_ref, refs = refs[:count], refs[count], refs[count + 1 :]
+    pixels_ref, here_ref, there_ref, order_ref, high_ref, low_ref, *refs = refs
+    outs, refs = refs[:count], refs[count:]
+    goal_ref, picked_ref, table_ref, *refs = refs
     stages, refs = refs[:count], refs[count:]
     facts_ref, t0_ref, a_ref, near_ref, far_ref, q_ref, o_ref, h_ref, sum_ref, embed_buf, qkv_buf, up_buf, down_buf, *refs = refs
+    pixel_buf, other_ref, chosen_ref, *refs = refs
     local_sem, z_send, z_recv, p_send, p_recv, w_sem, kv_sem = refs
     section, place = lax.axis_index("section"), lax.axis_index("dp")
     z, core = place // 2, place % 2
@@ -538,8 +535,76 @@
     ends = [group * (a + 1) + 2 * lag for a in range(count)]
     last = len(items) + 2 * lag
     SMALL, TALL, WIDE = 0, 1, 2
-    for i in range(min(ends[TALL], last)):
+    clips_here = pixels_ref.shape[0]
+    holds = core == section // clips_here
+    first = list(range(min(ends[TALL], last)))
+    pixel_copy = pltpu.make_async_copy(pixels_ref.at[section % clips_here], pixel_buf, kv_sem.at[2])
+    handed = pltpu.make_async_remote_copy(
+        src_ref=other_ref,
+        dst_ref=chosen_ref,
+        send_sem=kv_sem.at[3],
+        recv_sem=kv_sem.at[4],
+        device_id=mate,
+        device_id_type=MESH,
+    )
+
+    @pl.when(holds)
+    def _():
+        pixel_copy.start()
+
+    def tabulate(i):
+        rows = pl.ds(pl.multiple_of(i * 96, 16), 96)
+        order = order_ref[rows, :]
+
+        def wave(table, index):
+            choice = lax.broadcasted_iota(jnp.int32, (96, table.shape[0]), 1) == index
+            return jnp.dot(
+                choice.astype(jnp.float32), table[...],
+                precision=lax.Precision.HIGHEST, preferred_element_type=jnp.float32,
+            )
+
+        high, low = wave(high_ref, order // 32), wave(low_ref, order % 32)
+        sin_high, cos_high = high[:, : D // 2], high[:, D // 2 :]
+        sin_low, cos_low = low[:, : D // 2], low[:, D // 2 :]
+        t0_ref[rows, : D // 2] = sin_high * cos_low + cos_high * sin_low
+        t0_ref[rows, D // 2 :] = cos_high * cos_low - sin_high * sin_low
+
+    run_loop(HALF // 96, tabulate, first[:2])
+    table_ref[...] = t0_ref[:SEEN, :]
+
+    @pl.when(holds)
+    def _():
+        pixel_copy.wait()
+
+    def pick(source, target):
+        def rows_picked(i):
+            @pl.when(holds)
+            def _():
+                rows = pl.ds(pl.multiple_of(i * 96, 16), 96)
+                choice = lax.broadcasted_iota(jnp.int32, (96, L), 1) == source[rows, :]
+                target[rows, :] = matmul(choice.astype(jnp.bfloat16), pixel_buf[...]).astype(jnp.bfloat16)
+
+        return rows_picked
+
+    run_loop(HALF // 96, pick(there_ref, other_ref), first[2:5])
+
+    @pl.when(holds)
+    def _():
+        handed.start()
+
+    run_loop(HALF // 96, pick(here_ref, chosen_ref), first[5:8])
+    for i in first[8:]:
         advance(i)
+
+    @pl.when(holds)
+    def _():
+        handed.wait_send()
+
+    @pl.when(jnp.logical_not(holds))
+    def _():
+        handed.wait_recv()
+
+    picked_ref[...] = chosen_ref[:SEEN, :]
     settle(SMALL)
     settle(TALL)
     facts = pltpu.make_async_copy(outs[SMALL].at[:, PD : PD + LANES], facts_ref, local_sem.at[SMALL])
@@ -547,7 +612,7 @@
 
     def embed(i, slot):
         at = pl.ds(pl.multiple_of(i * 256, 128), 256)
-        t0_ref[:, at] = matmul(chosen_ref[...], embed_buf[slot]) + table_ref[:, at]
+        t0_ref[:, at] += matmul(chosen_ref[...], embed_buf[slot])
 
     waiting = list(range(ends[TALL], min(ends[WIDE], last)))
     streamed(4, [column_fetch(TALL, pl.ds(0, PATCH), 0, 256, embed_buf, 0)], embed, waiting[:2])
@@ -642,21 +707,26 @@
                 in_plane(a, step, upward, kind).wait_send()
 
 
-def gather_and_teach(blocks, chosen, table):
+def gather_and_teach(blocks, pixels, order_here, order_there, order):
     count = len(blocks)
     dp_size = lax.axis_size("dp")
     zn = dp_size // 2
     return pl.pallas_call(
         functools.partial(gather_kernel, count, zn),
         in_specs=[pl.BlockSpec(memory_space=pl.ANY)] * count
-        + [pl.BlockSpec(memory_space=pltpu.VMEM)] * 2,
+        + [pl.BlockSpec(memory_space=pl.ANY)]
+        + [pl.BlockSpec(memory_space=pltpu.VMEM)] * 5,
         out_specs=[pl.BlockSpec(memory_space=pl.ANY)] * count
-        + [pl.BlockSpec(memory_space=pltpu.VMEM)],
+        + [pl.BlockSpec(memory_space=pltpu.VMEM)] * 3,
         out_shape=[
             jax.ShapeDtypeStruct((member.shape[0] * dp_size, member.shape[1]), member.dtype)
             for member in blocks
         ]
-        + [jax.ShapeDtypeStruct((HALF - SKIP, D), jnp.bfloat16)],
+        + [
+            jax.ShapeDtypeStruct((HALF - SKIP, D), jnp.bfloat16),
+            jax.ShapeDtypeStruct((SEEN, PATCH), jnp.bfloat16),
+            jax.ShapeDtypeStruct((SEEN, D), jnp.float32),
+        ],
         scratch_shapes=[pltpu.VMEM(member.shape, member.dtype) for member in blocks]
         + [
             pltpu.VMEM((D, LANES), jnp.bfloat16),
@@ -672,6 +742,9 @@
             pltpu.VMEM((2, D, 256), jnp.bfloat16),
             pltpu.VMEM((2, D, 512), jnp.bfloat16),
             pltpu.VMEM((2, 512, D), jnp.bfloat16),
+            pltpu.VMEM((L, PATCH), jnp.bfloat16),
+            pltpu.VMEM((HALF, PATCH), jnp.bfloat16),
+            pltpu.VMEM((HALF, PATCH), jnp.bfloat16),
         ]
         + [
             pltpu.SemaphoreType.DMA((count,)),
@@ -680,12 +753,20 @@
             pltpu.SemaphoreType.DMA((count * ((zn - 1) * 10 + 1),)),
             pltpu.SemaphoreType.DMA((count * ((zn - 1) * 10 + 1),)),
             pltpu.SemaphoreType.DMA((8,)),
-            pltpu.SemaphoreType.DMA((2,)),
+            pltpu.SemaphoreType.DMA((5,)),
         ],
         compiler_params=pltpu.CompilerParams(
-            collective_id=0, has_side_effects=True, vmem_limit_bytes=VMEM_LIMIT
+            collective_id=0, has_side_effects=True, vmem_limit_bytes=58 * 1024 * 1024
         ),
-    )(*blocks, chosen, table)
+    )(
+        *blocks,
+        pixels,
+        order_here[:, None],
+        order_there[:, None],
+        order[:, None],
+        position_table(32 * lax.iota(jnp.int32, L // 32), D),
+        position_table(lax.iota(jnp.int32, 32), D),
+    )
 
 
 def upper_rows(size):
@@ -1129,10 +1210,6 @@
     pairs_own = order_own.reshape(HALF, 2)
     order_here = jnp.where(core == 0, pairs_own[:, 0], pairs_own[:, 1])
     order_there = jnp.where(core == 0, pairs_own[:, 1], pairs_own[:, 0])
-    pixel_rows = lax.dynamic_index_in_dim(pixels, clip, 0, keepdims=False)
-    for_here = picked_rows(pixel_rows, order_here)
-    for_there = picked_rows(pixel_rows, order_there)
-    chosen = jnp.where(holds, for_here, swapped(for_there))
     seen_near = (seen - core + 1) // 2
     seen_far = (seen + core) // 2
     kept = jnp.stack([seen_near, seen_far])
@@ -1164,9 +1241,12 @@
         pred_weight.reshape(pred_block),
         jnp.pad(pred_down, ((0, 0), (0, LANES))),
     )
-    table = position_table(order, D)
-    w_small, teach_tall, teach_wide, w_tall, w_wide, w_pred, w_down, goal = gather_and_teach(
-        tuple(member.astype(jnp.bfloat16) for member in blocks), chosen, table
+    w_small, teach_tall, teach_wide, w_tall, w_wide, w_pred, w_down, goal, enc_chosen, table = gather_and_teach(
+        tuple(member.astype(jnp.bfloat16) for member in blocks),
+        pixels,
+        order_here,
+        order_there,
+        order,
     )
     goal = goal.astype(jnp.float32)
     w_pred = w_pred.reshape(PD, -1)
@@ -1190,8 +1270,7 @@
     row_ids = lax.iota(jnp.int32, HALF)
     context = (row_ids < seen_near)[:, None]
 
-    enc_chosen = chosen[:SEEN]
-    stream_a = matmul(enc_chosen, w_tall[:PATCH]) + table[:SEEN]
+    stream_a = matmul(enc_chosen, w_tall[:PATCH]) + table
     stream_b, stored_a = attend_fwd(
         stream_a, enc_gain[:, 0], enc_attn[0], enc_attn[1], HE, kept, 0, SEEN
     )
@@ -1239,7 +1318,7 @@
         stream_a, enc_gain[:, 0], enc_attn[0], enc_attn[1], HE, kept, 0, SEEN, stored_a, grad_stream
     )
     grad_tall = tall_grad(
-        chosen[:SEEN], grad_stream.astype(jnp.bfloat16), stored_b[2], branch_grad
+        enc_chosen, grad_stream.astype(jnp.bfloat16), stored_b[2], branch_grad
     )
 
     gain_grads = jnp.concatenate(

time: 799 us -> 776 us (0.971)
  matrix products: 106 us -> 95.5 us
    dot_general x15 -> x13, matrix products: 47.9 us -> 35.1 us  [matmul(): return jnp.dot(left, right, preferred_element_type=jnp.float32)]
  transfers between devices with their start and end apart: 8 -> 7, of which waited for: 0 -> 0; matrix products, arithmetic and copies ran while one was open for 8% -> 8% of each run, Pallas kernels for 0% -> 0%
where the time goes in v4:
time: 776 us; the launch traced here: 771 us
  Pallas kernels  570 us (73%)
  matrix products  95.5 us (12%)
  other arithmetic  66.6 us (9%)
  local copies, waits for them, and re-layouts  29.7 us (4%)
    pallas_call x1, Pallas kernels, gather_and_teach(): pl.pallas_call(functools.partial(gather_kernel, count, zn), in_specs=[pl....  248 us
    pallas_call x1, Pallas kernels, reduce_blocks(): pl.pallas_call(functools.partial(reduce_kernel, count, zn), in_specs=[any...  212 us
    pallas_call x2, Pallas kernels, attend_rows_back(): pl.pallas_call(functools.partial(attend_back_kernel, width // num_heads,...  65 us
    dot_general x13, matrix products, matmul(): return jnp.dot(left, right, preferred_element_type=jnp.float32)  35.1 us
    pallas_call x2, Pallas kernels, attend_rows(): pl.pallas_call(functools.partial(attend_kernel, width // num_heads, maske...  33 us
    dot_general x10, matrix products, outer_rows(): lax.dot_general(left, right, (((1,), (1,)), ((), ())), preferred_element_...  32.7 us
    dot_general x9, matrix products, inner_rows(): lax.dot_general(left, right, (((0,), (0,)), ((), ())), preferred_element_...  27.6 us
  transfers between devices with their start and end apart: 7, of which 0 were waited for; matrix products, arithmetic and copies ran while one was open for 8% of the time, Pallas kernels for 0%

profile of v4, /device:TPU:0, one launch (start us, length us, event | category | flops | bytes accessed | tf_op | source)
XLA Modules:
  0.0 770.7 jit_solution(7693485011036413322)
XLA Ops:
  13.0 3.9 convert_element_type.267.refs_2_
  24.9 247.5 %shard_map.463 = (bf16[1024,512]{1,0:T(8,128)(2,1)}, bf16[5632,1024]{1,0:T(8,128)(2,1)}, bf16[1024,8192]{1,0:T(8,128)(2,1)}, bf16[5632,1024]{1,0:T(8,128)(2,1)},...) custom-call(bf16[128,512]{1,0:T(8,128)(2,1)} %concatenate.41.refs_0_, ...), custom_call_target="tpu_custom_call" | custom-call | tf_op jit(solution)/shard_map/pallas_call | solution.py:714
  272.4 3.7 fusion.173
  279.2 3.8 fusion.40.k0_ref.v0_ref
  287.6 2.8 multiply_sine_fusion
  292.9 10.8 %shard_map.464 = (bf16[288,1024]{1,0:T(8,128)(2,1)S(1)}, f32[288,1024]{1,0:T(8,128)S(1)}) custom-call(s32[2]{0:T(128)S(1)} %pad_add_fusion.1.kept_ref, bf16[288,1024]{1,0:T(8,128)(2,1)S(1)} %fusion.81.q_ref, bf16[288,2048]{1,0:T(8,128)(2,1)S(1)} %fusion.40.k0_ref.v0_ref, bf16[288,2048]{1,0:T(8,128)(2,1)S(1)} %fusion.40.k0_ref.v0_ref, ...), custom_call_target="tpu_custom_call" | custom-call | flops 679477248 | bytes 4718592 | tf_op jit(solution)/shard_map/pallas_call | solution.py:124
  303.7 3.0 convert_reduce_fusion
  307.1 7.5 multiply_convert_fusion
  314.6 2.8 fusion.174
  327.3 22.2 %shard_map.465 = (bf16[672,384]{1,0:T(8,128)(2,1)S(1)}, f32[672,384]{1,0:T(8,128)S(1)}) custom-call(s32[2]{0:T(128)S(1)} %broadcast.346.kept_ref, bf16[672,384]{1,0:T(8,128)(2,1)S(1)} %convolution_convert_fusion.14.q_ref, bf16[768,768]{1,0:T(8,128)(2,1)S(1)} %convolution_convert_fusion.7.k0_ref.v0_ref, ...), custom_call_target="tpu_custom_call" | custom-call | flops 1585446912 | bytes 4423680 | tf_op jit(solution)/shard_map/pallas_call | solution.py:124
  354.1 4.5 select_reduce_fusion
  367.9 46.9 %shard_map.466 = (bf16[672,384]{1,0:T(8,128)(2,1)S(1)}, f32[768,384]{1,0:T(8,128)S(1)}, f32[768,384]{1,0:T(8,128)}, f32[768,384]{1,0:T(8,128)}, f32[768,384]{1,0:T(8,128)}) custom-call(s32[2]{0:T(128)S(1)} %broadcast.346.kept_ref, bf16[672,384]{1,0:T(8,128)(2,1)S(1)} %convolution_convert_fusion.14.q_ref, ...), custom_call_target="tpu_custom_call" | custom-call | flops 3963617280 | bytes 11501568 | tf_op jit(solution)/shard_map/pallas_call | solution.py:196
  415.4 3.1 convolution_convert_fusion.3
  436.5 6.7 fusion.19
  443.2 7.0 fusion.102
  454.7 18.1 %shard_map.467 = (bf16[288,1024]{1,0:T(8,128)(2,1)S(1)}, f32[288,1024]{1,0:T(8,128)S(1)}, f32[288,1024]{1,0:T(8,128)}, f32[288,1024]{1,0:T(8,128)}, f32[288,1024]{1,0:T(8,128)}) custom-call(s32[2]{0:T(128)S(1)} %pad_add_fusion.1.kept_ref, bf16[288,1024]{1,0:T(8,128)(2,1)S(1)} %fusion.81.q_ref, bf16[288,1024]{1,0:T(8,128)(2,1)S(1)} %fusion.78.g_ref, ...), custom_call_target="tpu_custom_call" | custom-call | flops 1698693120 | bytes 11796480 | tf_op jit(solution)/shard_map/pallas_call | solution.py:196
  477.3 3.1 pad_maximum_fusion.refs_5_
  483.0 7.2 convolution_convert_fusion.refs_2_
  493.7 5.1 fusion.94
  498.8 5.7 convolution_convert_fusion.1.refs_0_
  509.3 12.5 %shard_map.468.refs_4_ = bf16[5632,1024]{1,0:T(8,128)(2,1)} custom-call(bf16[288,1536]{1,0:T(8,128)(2,1)S(1)} %copy-done.4, bf16[288,1024]{1,0:T(8,128)(2,1)S(1)} %add_convert_fusion.gx_ref, bf16[288,4096]{1,0:T(8,128)(2,1)} %copy-done.28, bf16[288,1024]{1,0:T(8,128)(2,1)S(1)} %add_convert_fusion.6.gh_ref), custom_call_target="tpu_custom_call" | custom-call | flops 3321888768 | bytes 14778368 | tf_op jit(solution)/shard_map/pallas_call | solution.py:297
  523.1 211.7 %shard_map.469 = (bf16[128,3072]{1,0:T(8,128)(2,1)}, bf16[128,1024]{1,0:T(8,128)(2,1)}, bf16[128,4096]{1,0:T(8,128)(2,1)}, bf16[128,512]{1,0:T(8,128)(2,1)}, bf1...) custom-call(bf16[1024,3072]{1,0:T(8,128)(2,1)} %convolution_convert_fusion.1.refs_0_, ...), custom_call_target="tpu_custom_call" | custom-call | tf_op jit(solution)/shard_map/pallas_call | solution.py:1127
  743.4 7.3 multiply_add_fusion.1
  753.9 7.9 %fusion.168 = (bf16[128,8576]{1,0:T(8,128)(2,1)}, f32[128,8576]{1,0:T(8,128)S(1)}, f32[128,8576]{1,0:T(8,128)}, f32[128,8576]{1,0:T(8,128)}) fusion(f32[128,8576]{1,0:T(8,128)S(1)} %bitcast.37, f32[]{:T(128)S(6)} %min.3, bf16[128,384]{1,0:T(8,128)(2,1)S(1)} %slice.219, bf16[128,4096]{1,0:T(8,128)(2,1)S(1)} %copy-done.33, ...), kind=kLoop, calls=%fused_computation.297 | loop fusion | flops 27443200 | bytes 30736388 | tf_op jit(solution)/shard_map/convert_element_type | solution.py:1421
  (398 shorter events, 109.2 us)
Async XLA Ops:
  3.3 19.6 %collective-permute-start = (s32[1537]{0:T(1024)S(1)}, s32[1537]{0:T(1024)S(1)}, u32[]{:S(2)}, u32[]{:S(2)}) collective-permute-start(s32[1537]{0:T(1024)S(1)} %pad_add_fusion), channel_id=1, source_target_pairs={{0,1},{1,0},{2,3},{3,2},{4,5},{5,4},{6,7},{7,6},{8,9},{9,8},{10,11... | collective-permute-start | bytes 18452 | tf_op jit(solution)/shard_map/ppermute | solution.py:252
  276.1 27.5 %copy-start.10 = (f32[288,1024]{1,0:T(8,128)}, f32[288,1024]{1,0:T(8,128)S(1)}, u32[]{:S(2)}) copy-start(f32[288,1024]{1,0:T(8,128)S(1)} %get-tuple-element.198) | copy-start | bytes 3538948
  278.9 28.2 %copy-start.57 = (f32[1024]{0:T(1024)}, f32[1024]{0:T(1024)S(1)}, u32[]{:S(2)}) copy-start(f32[1024]{0:T(1024)S(1)} %get-tuple-element.145) | copy-start | bytes 12292
  278.9 38.9 %copy-start.78 = (f32[1024]{0:T(1024)}, f32[1024]{0:T(1024)S(1)}, u32[]{:S(2)}) copy-start(f32[1024]{0:T(1024)S(1)} %get-tuple-element.144) | copy-start | bytes 12292
  279.1 11.3 %copy-start.38 = (bf16[288,1024]{1,0:T(8,128)(2,1)}, bf16[288,1024]{1,0:T(8,128)(2,1)S(1)}, u32[]{:S(2)}) copy-start(bf16[288,1024]{1,0:T(8,128)(2,1)S(1)} %multiply_convert_fusion.4) | copy-start | bytes 1769476
  283.0 9.8 %collective-permute-start.1 = (bf16[288,2048]{1,0:T(8,128)(2,1)S(1)}, bf16[288,2048]{1,0:T(8,128)(2,1)}, u32[]{:S(2)}, u32[]{:S(2)}) collective-permute-start(bf16[288,2048]{1,0:T(8,128)(2,1)S(1)} %fusion.40.k0_ref.v0_ref), channel_id=1, source_target_pairs={{0,1},{1,0},{2,3},{3,2},{4,5},{5,4},{6,7},{7,6},{8,9},{9,8},{10,11... | collective-permute-start | bytes 3538952 | tf_op jit(solution)/shard_map/ppermute | solution.py:252
  287.0 31.4 %copy-start.81 = (pred[768]{0:T(1024)(128)(4,1)}, pred[768]{0:T(1024)(128)(4,1)S(1)}, u32[]{:S(2)}) copy-start(pred[768]{0:T(1024)(128)(4,1)S(1)} %iota_compare_fusion.2) | copy-start | bytes 2308
  287.6 31.7 %copy-start.66 = (f32[384]{0:T(512)}, f32[384]{0:T(512)S(1)}, u32[]{:S(2)}) copy-start(f32[384]{0:T(512)S(1)} %get-tuple-element.149) | copy-start | bytes 4612
  319.7 29.8 %copy-start.40 = (bf16[768,384]{1,0:T(8,128)(2,1)}, bf16[768,384]{1,0:T(8,128)(2,1)S(1)}, u32[]{:S(2)}) copy-start(bf16[768,384]{1,0:T(8,128)(2,1)S(1)} %multiply_convert_fusion.2) | copy-start | bytes 1769476
  321.7 27.7 %copy-start.5 = (bf16[768,768]{1,0:T(8,128)(2,1)}, bf16[768,768]{1,0:T(8,128)(2,1)S(1)}, u32[]{:S(2)}) copy-start(bf16[768,768]{1,0:T(8,128)(2,1)S(1)} %convolution_convert_fusion.7.k0_ref.v0_ref) | copy-start | bytes 3538948
  321.8 5.5 collective-permute-start.2
  327.3 22.2 %copy-start.9 = (f32[768,384]{1,0:T(8,128)S(1)}, f32[768,384]{1,0:T(8,128)}, u32[]{:S(2)}) copy-start(f32[768,384]{1,0:T(8,128)} %copy-done.8) | copy-start | bytes 3538948
  327.3 22.2 %copy-start.48 = (bf16[384,4096]{1,0:T(8,128)(2,1)S(1)}, bf16[384,4096]{1,0:T(8,128)(2,1)}, u32[]{:S(2)}) copy-start(bf16[384,4096]{1,0:T(8,128)(2,1)} %get-tuple-element.78) | copy-start | bytes 9437188
  414.8 10.3 %collective-permute-start.3 = (f32[768,384]{1,0:T(8,128)}, f32[768,384]{1,0:T(8,128)S(1)}, u32[]{:S(2)}, u32[]{:S(2)}) collective-permute-start(f32[768,384]{1,0:T(8,128)} %get-tuple-element.85), channel_id=1, source_target_pairs={{0,1},{1,0},{2,3},{3,2},{4,5},{5,4},{6,7},{7,6},{8,9},{9,8},{10,11... | collective-permute-start | bytes 3538952 | tf_op jit(solution)/shard_map/ppermute | solution.py:252
  415.2 10.2 %collective-permute-start.4 = (f32[768,384]{1,0:T(8,128)}, f32[768,384]{1,0:T(8,128)S(1)}, u32[]{:S(2)}, u32[]{:S(2)}) collective-permute-start(f32[768,384]{1,0:T(8,128)} %get-tuple-element.87), channel_id=1, source_target_pairs={{0,1},{1,0},{2,3},{3,2},{4,5},{5,4},{6,7},{7,6},{8,9},{9,8},{10,11... | collective-permute-start | bytes 3538952 | tf_op jit(solution)/shard_map/ppermute | solution.py:252
  473.6 16.7 %collective-permute-start.5 = (f32[288,1024]{1,0:T(8,128)}, f32[288,1024]{1,0:T(8,128)}, u32[]{:S(2)}, u32[]{:S(2)}) collective-permute-start(f32[288,1024]{1,0:T(8,128)} %get-tuple-element.91), channel_id=1, source_target_pairs={{0,1},{1,0},{2,3},{3,2},{4,5},{5,4},{6,7},{7,6},{8,9},{9,8},{10,11... | collective-permute-start | bytes 3538952 | tf_op jit(solution)/shard_map/ppermute | solution.py:252
  473.8 18.1 %collective-permute-start.6 = (f32[288,1024]{1,0:T(8,128)}, f32[288,1024]{1,0:T(8,128)}, u32[]{:S(2)}, u32[]{:S(2)}) collective-permute-start(f32[288,1024]{1,0:T(8,128)} %get-tuple-element.93), channel_id=1, source_target_pairs={{0,1},{1,0},{2,3},{3,2},{4,5},{5,4},{6,7},{7,6},{8,9},{9,8},{10,11... | collective-permute-start | bytes 3538952 | tf_op jit(solution)/shard_map/ppermute | solution.py:252
  509.2 12.5 %copy-start.63 = (f32[12,128]{1,0:T(8,128)S(1)}, f32[12,128]{1,0:T(8,128)}, u32[]{:S(2)}) copy-start(f32[12,128]{1,0:T(8,128)} %reshape.338) | copy-start | bytes 18436
  509.3 12.5 %copy-start.98 = (f32[48]{0:T(128)S(1)}, f32[48]{0:T(128)}, u32[]{:S(2)}) copy-start(f32[48]{0:T(128)} %pad.56.clone) | copy-start | bytes 580
  523.1 219.1 %copy-start.84 = (f32[128,3]{0,1:T(4,128)S(1)}, f32[128,3]{0,1:T(4,128)}, u32[]{:S(2)}) copy-start(f32[128,3]{0,1:T(4,128)} %param.33) | copy-start | bytes 4612
  523.1 219.1 %copy-start.86 = (f32[128,3]{0,1:T(4,128)S(1)}, f32[128,3]{0,1:T(4,128)}, u32[]{:S(2)}) copy-start(f32[128,3]{0,1:T(4,128)} %param.49) | copy-start | bytes 4612
  523.1 219.1 %copy-start.94 = (f32[128,3]{0,1:T(4,128)S(1)}, f32[128,3]{0,1:T(4,128)}, u32[]{:S(2)}) copy-start(f32[128,3]{0,1:T(4,128)} %param.39) | copy-start | bytes 4612
  523.1 219.1 %copy-start.95 = (f32[128,3]{0,1:T(4,128)S(1)}, f32[128,3]{0,1:T(4,128)}, u32[]{:S(2)}) copy-start(f32[128,3]{0,1:T(4,128)} %param.45) | copy-start | bytes 4612
  523.1 220.3 %copy-start.15 = (f32[704,1024]{1,0:T(8,128)S(1)}, f32[704,1024]{1,0:T(8,128)}, u32[]{:S(2)}) copy-start(f32[704,1024]{1,0:T(8,128)} %param.48) | copy-start | bytes 8650756
  (97 other events, 350.7 us)

commit v5 on v4

--- a/solution.py
+++ b/solution.py
@@ -175,8 +175,8 @@
             probs, steps, (k0_ref, k1_ref), (dk0_ref, dk1_ref), (dv0_ref, dv1_ref)
         ):
             grad_logits = (step - attn * totals).astype(jnp.bfloat16)
-            dv_ref[...] += inner_rows(attn.astype(jnp.bfloat16), head_grads)
-            dk_ref[...] += inner_rows(grad_logits, head_queries) * scaling
+            dv_ref[...] += jnp.transpose(inner_rows(head_grads, attn.astype(jnp.bfloat16)))
+            dk_ref[...] += jnp.transpose(inner_rows(head_queries, grad_logits)) * scaling
             outcome = outcome + matmul(grad_logits, k_ref[...])
         grad_queries = jnp.where(chosen, outcome * scaling, grad_queries)
     dq_ref[...] = grad_queries.astype(dq_ref.dtype)
@@ -336,7 +336,7 @@
     goal_ref, picked_ref, table_ref, *refs = refs
     stages, refs = refs[:count], refs[count:]
     facts_ref, t0_ref, a_ref, near_ref, far_ref, q_ref, o_ref, h_ref, sum_ref, embed_buf, qkv_buf, up_buf, down_buf, *refs = refs
-    pixel_buf, other_ref, chosen_ref, *refs = refs
+    pixel_buf, other_ref, chosen_ref, wide_buf, pred_buf, *refs = refs
     local_sem, z_send, z_recv, p_send, p_recv, w_sem, kv_sem = refs
     section, place = lax.axis_index("section"), lax.axis_index("dp")
     z, core = place // 2, place % 2
@@ -346,6 +346,20 @@
     ahead = {"dp": place + 2}
     behind = {"dp": place - 2}
 
+    def landing(a):
+        rows, columns = stages[a].shape
+        if ins[a].dtype == stages[a].dtype:
+            return stages[a]
+        buffer = t0_ref if columns == D and rows > 48 else wide_buf if columns == 8 * D else pred_buf
+        return buffer.at[pl.ds(0, rows), pl.ds(0, columns)]
+
+    def fetched(a):
+        source = ins[a].at[:, pl.ds(0, stages[a].shape[1])]
+        return pltpu.make_async_copy(source, landing(a), local_sem.at[a])
+
+    for a in FIRST_IN:
+        fetched(a).start()
+
     barrier = pltpu.get_barrier_semaphore()
     line = [{"dp": (z + j) % zn * 2 + core} for j in range(1, zn)]
     for other in [near, far, mate] + line:
@@ -353,17 +367,17 @@
     pl.semaphore_wait(barrier, 3 + len(line))
 
     def block(ref, a, owner_z, quarter=None, rows=None, owner_core=core):
-        size = ins[a].shape[0]
+        size = stages[a].shape[0]
         start, length = (0, size) if rows is None else rows
         offset = pl.multiple_of((owner_z * 2 + owner_core) * size + start, 16)
         if quarter is None:
             return ref.at[pl.ds(offset, length), :]
-        width = ins[a].shape[1] // 4
+        width = stages[a].shape[1] // 4
         return ref.at[pl.ds(offset, length), pl.ds(pl.multiple_of(quarter * width, 128), width)]
 
     def own_quarter(a):
-        width = ins[a].shape[1] // 4
-        return ins[a].at[:, pl.ds(pl.multiple_of(section * width, 128), width)]
+        width = stages[a].shape[1] // 4
+        return stages[a].at[:, pl.ds(pl.multiple_of(section * width, 128), width)]
 
     def copy(src, dst, sends, recvs, index, device):
         return pltpu.make_async_remote_copy(
@@ -388,11 +402,11 @@
         return (z + (step - 1) <= zn - 1) & (z > 0)
 
     def first_half(a):
-        size = ins[a].shape[0]
+        size = stages[a].shape[0]
         return (0, (size + 31) // 32 * 16)
 
     def second_half(a):
-        size = ins[a].shape[0]
+        size = stages[a].shape[0]
         start = (size + 31) // 32 * 16
         return (start, size - start)
 
@@ -409,7 +423,6 @@
         ][kind]()
         return copy(part, part, p_send, p_recv, index, (near, far, far, near, mate)[kind])
 
-    own = []
     def offered(a):
         for upward in (True, False):
 
@@ -417,22 +430,30 @@
             def _(upward=upward):
                 along(a, 1, upward).start()
 
-    for a in range(2):
-        offered(a)
-
+    own = []
     settled = []
-    for a in range(count):
-        take = pltpu.make_async_copy(ins[a], stages[a], local_sem.at[a])
-        take.start()
-        base = count * (zn - 1) * 10
-        give = copy(ins[a], block(outs[a], a, z), p_send, p_recv, base + a, mate)
+    base = count * (zn - 1) * 10
+    for a in ARRIVAL:
+        fetched(a).wait()
+        if ins[a].dtype != stages[a].dtype:
+            source = landing(a)
+
+            def rounded(i, carried_through):
+                at = pl.ds(pl.multiple_of(i * 16, 16), 16)
+                stages[a][at, :] = source[at, :].astype(stages[a].dtype)
+                return carried_through
+
+            lax.fori_loop(0, stages[a].shape[0] // 16, rounded, 0)
+        if a in NEXT_IN:
+            fetched(NEXT_IN[a]).start()
+        keep = pltpu.make_async_copy(stages[a], block(outs[a], a, z), local_sem.at[a])
+        give = copy(stages[a], block(outs[a], a, z), p_send, p_recv, base + a, mate)
+        if a < 2:
+            offered(a)
+        keep.start()
         give.start()
-        keep = pltpu.make_async_copy(stages[a], block(outs[a], a, z), local_sem.at[a])
-        own.append((take, keep, give))
-
-    for take, keep, give in own:
-        take.wait()
-        keep.start()
+        own.append((a, keep, give))
+    own = [(keep, give) for a, keep, give in sorted(own, key=lambda entry: entry[0])]
 
     items = [
         (a, step, upward)
@@ -486,7 +507,7 @@
             received(*items[i])
 
     def settle(a):
-        take, keep, give = own[a]
+        keep, give = own[a]
         keep.wait()
         give.wait_recv()
         for b, step, upward in items:
@@ -693,7 +714,7 @@
     for a in range(count):
         if a not in settled:
             settle(a)
-    for take, keep, give in own:
+    for keep, give in own:
         give.wait_send()
     for a, step, upward in items:
 
@@ -707,7 +728,12 @@
                 in_plane(a, step, upward, kind).wait_send()
 
 
-def gather_and_teach(blocks, pixels, order_here, order_there, order):
+FIRST_IN = (0, 1, 2, 5, 6)
+ARRIVAL = (0, 1, 2, 3, 4, 5, 6)
+NEXT_IN = {1: 3, 2: 4}
+
+
+def gather_and_teach(blocks, widths, pixels, order_here, order_there, order):
     count = len(blocks)
     dp_size = lax.axis_size("dp")
     zn = dp_size // 2
@@ -719,15 +745,18 @@
         out_specs=[pl.BlockSpec(memory_space=pl.ANY)] * count
         + [pl.BlockSpec(memory_space=pltpu.VMEM)] * 3,
         out_shape=[
-            jax.ShapeDtypeStruct((member.shape[0] * dp_size, member.shape[1]), member.dtype)
-            for member in blocks
+            jax.ShapeDtypeStruct((member.shape[0] * dp_size, width), jnp.bfloat16)
+            for member, width in zip(blocks, widths)
         ]
         + [
             jax.ShapeDtypeStruct((HALF - SKIP, D), jnp.bfloat16),
             jax.ShapeDtypeStruct((SEEN, PATCH), jnp.bfloat16),
             jax.ShapeDtypeStruct((SEEN, D), jnp.float32),
         ],
-        scratch_shapes=[pltpu.VMEM(member.shape, member.dtype) for member in blocks]
+        scratch_shapes=[
+            pltpu.VMEM((member.shape[0], width), jnp.bfloat16)
+            for member, width in zip(blocks, widths)
+        ]
         + [
             pltpu.VMEM((D, LANES), jnp.bfloat16),
             pltpu.VMEM((HALF, D), jnp.float32),
@@ -745,6 +774,8 @@
             pltpu.VMEM((L, PATCH), jnp.bfloat16),
             pltpu.VMEM((HALF, PATCH), jnp.bfloat16),
             pltpu.VMEM((HALF, PATCH), jnp.bfloat16),
+            pltpu.VMEM((blocks[2].shape[0], 8 * D), jnp.float32),
+            pltpu.VMEM(blocks[5].shape, jnp.float32),
         ]
         + [
             pltpu.SemaphoreType.DMA((count,)),
@@ -1229,7 +1260,7 @@
             ),
         ],
         axis=1,
-    )
+    ).astype(jnp.bfloat16)
     pred_block = pred_weight.shape if pred_weight.shape[0] % 16 == 0 else (-1, D)
     pred_form = (PD, pred_weight.shape[1]) if pred_weight.shape[0] % 16 == 0 else (-1, D)
     blocks = (
@@ -1237,12 +1268,13 @@
         teacher_tall,
         teacher_wide,
         tall_weight,
-        wide_weight[:, : 4 * D + FF],
+        wide_weight,
         pred_weight.reshape(pred_block),
-        jnp.pad(pred_down, ((0, 0), (0, LANES))),
+        jnp.pad(pred_down.astype(jnp.bfloat16), ((0, 0), (0, LANES))),
     )
     w_small, teach_tall, teach_wide, w_tall, w_wide, w_pred, w_down, goal, enc_chosen, table = gather_and_teach(
-        tuple(member.astype(jnp.bfloat16) for member in blocks),
+        blocks,
+        [4 * D + FF if member is wide_weight else member.shape[1] for member in blocks],
         pixels,
         order_here,
         order_there,
@@ -1281,7 +1313,7 @@
     projected = padded_rows(matmul(encoded, pred_embed), 0, HALF - SEEN)
     stream_d = jnp.where(context, projected, pred_gain[:, 3][None, :]) + pred_table
     stream_e, stored_d = attend_fwd(
-        stream_d, pred_gain[:, 0], pred_attn[0], pred_attn[1], PH, None, SKIP, 336
+        stream_d, pred_gain[:, 0], pred_attn[0], pred_attn[1], PH, None, SKIP, HALF - SKIP
     )
     stream_e = stream_e.astype(jnp.bfloat16).astype(jnp.float32)
     stream_f, stored_e = feed_fwd(stream_e, pred_gain[:, 1], pred_feed[0], pred_feed[1])
@@ -1303,7 +1335,7 @@
     grad_down = inner_rows(stored_e[2], branch_grad)
     grad_stream = grad_stream.astype(jnp.bfloat16).astype(jnp.float32)
     grad_stream, grad_pin, grad_pout, grad_pg0 = attend_back(
-        stream_d, pred_gain[:, 0], pred_attn[0], pred_attn[1], PH, None, SKIP, 336, stored_d, grad_stream
+        stream_d, pred_gain[:, 0], pred_attn[0], pred_attn[1], PH, None, SKIP, HALF - SKIP, stored_d, grad_stream
     )
     grad_token = jnp.sum(jnp.where(context, 0.0, grad_stream), axis=0)
     grad_projected = jnp.where(context, grad_stream, 0.0)[:SEEN].astype(jnp.bfloat16)

time: 776 us -> 751 us (0.968)
  other arithmetic: 66.6 us -> 52 us
  Pallas kernels: 570 us -> 561 us
  transfers between devices with their start and end apart: 7 -> 7, of which waited for: 0 -> 0; matrix products, arithmetic and copies ran while one was open for 8% -> 6% of each run, Pallas kernels for 0% -> 0%
where the time goes in v5:
time: 751 us; the launch traced here: 747 us
  Pallas kernels  561 us (75%)
  matrix products  95 us (13%)
  other arithmetic  52 us (7%)
  local copies, waits for them, and re-layouts  29.1 us (4%)
    pallas_call x1, Pallas kernels, gather_and_teach(): pl.pallas_call(functools.partial(gather_kernel, count, zn), in_specs=[pl....  248 us
    pallas_call x1, Pallas kernels, reduce_blocks(): pl.pallas_call(functools.partial(reduce_kernel, count, zn), in_specs=[any...  211 us
    pallas_call x2, Pallas kernels, attend_rows_back(): pl.pallas_call(functools.partial(attend_back_kernel, width // num_heads,...  58.5 us
    dot_general x13, matrix products, matmul(): return jnp.dot(left, right, preferred_element_type=jnp.float32)  34.5 us
    dot_general x10, matrix products, outer_rows(): lax.dot_general(left, right, (((1,), (1,)), ((), ())), preferred_element_...  33.7 us
    pallas_call x2, Pallas kernels, attend_rows(): pl.pallas_call(functools.partial(attend_kernel, width // num_heads, maske...  31.8 us
    dot_general x9, matrix products, inner_rows(): lax.dot_general(left, right, (((0,), (0,)), ((), ())), preferred_element_...  26.8 us
  transfers between devices with their start and end apart: 7, of which 0 were waited for; matrix products, arithmetic and copies ran while one was open for 6% of the time, Pallas kernels for 0%

profile of v5, /device:TPU:0, one launch (start us, length us, event | category | flops | bytes accessed | tf_op | source)
XLA Modules:
  0.0 747.0 jit_solution(12615940147522064946)
XLA Ops:
  12.4 247.6 %shard_map.463 = (bf16[1024,512]{1,0:T(8,128)(2,1)}, bf16[5632,1024]{1,0:T(8,128)(2,1)}, bf16[1024,8192]{1,0:T(8,128)(2,1)}, bf16[5632,1024]{1,0:T(8,128)(2,1)},...) custom-call(bf16[128,512]{1,0:T(8,128)(2,1)} %concatenate.41.refs_0_, ...), custom_call_target="tpu_custom_call" | custom-call | tf_op jit(solution)/shard_map/pallas_call | solution.py:740
  260.0 3.7 fusion.173
  266.7 3.8 fusion.40.k0_ref.v0_ref
  275.4 2.8 multiply_sine_fusion
  280.7 10.8 %shard_map.464 = (bf16[288,1024]{1,0:T(8,128)(2,1)S(1)}, f32[288,1024]{1,0:T(8,128)S(1)}) custom-call(s32[2]{0:T(128)S(1)} %pad_add_fusion.1.kept_ref, bf16[288,1024]{1,0:T(8,128)(2,1)S(1)} %fusion.81.q_ref, bf16[288,2048]{1,0:T(8,128)(2,1)S(1)} %fusion.40.k0_ref.v0_ref, bf16[288,2048]{1,0:T(8,128)(2,1)S(1)} %fusion.40.k0_ref.v0_ref, ...), custom_call_target="tpu_custom_call" | custom-call | flops 679477248 | bytes 4718592 | tf_op jit(solution)/shard_map/pallas_call | solution.py:124
  291.5 3.0 convert_reduce_fusion
  294.9 7.2 multiply_convert_fusion
  302.1 2.8 fusion.174
  315.9 21.1 %shard_map.465 = (bf16[672,384]{1,0:T(8,128)(2,1)S(1)}, f32[672,384]{1,0:T(8,128)S(1)}) custom-call(s32[2]{0:T(128)S(1)} %broadcast.346.kept_ref, bf16[672,384]{1,0:T(8,128)(2,1)S(1)} %convolution_convert_fusion.14.q_ref, bf16[768,768]{1,0:T(8,128)(2,1)S(1)} %convolution_convert_fusion.7.k0_ref.v0_ref, ...), custom_call_target="tpu_custom_call" | custom-call | flops 1585446912 | bytes 4423680 | tf_op jit(solution)/shard_map/pallas_call | solution.py:124
  341.7 4.3 select_reduce_fusion
  350.0 2.6 fusion.113
  355.2 40.2 %shard_map.466 = (bf16[672,384]{1,0:T(8,128)(2,1)S(1)}, f32[768,384]{1,0:T(8,128)S(1)}, f32[768,384]{1,0:T(8,128)}, f32[768,384]{1,0:T(8,128)}, f32[768,384]{1,0:T(8,128)}) custom-call(s32[2]{0:T(128)S(1)} %broadcast.346.kept_ref, bf16[672,384]{1,0:T(8,128)(2,1)S(1)} %convolution_convert_fusion.14.q_ref, ...), custom_call_target="tpu_custom_call" | custom-call | flops 3963617280 | bytes 11501568 | tf_op jit(solution)/shard_map/pallas_call | solution.py:196
  395.8 3.1 convolution_convert_fusion.3
  420.0 7.4 fusion.19
  427.5 7.2 fusion.102
  438.4 18.3 %shard_map.467 = (bf16[288,1024]{1,0:T(8,128)(2,1)S(1)}, f32[288,1024]{1,0:T(8,128)S(1)}, f32[288,1024]{1,0:T(8,128)}, f32[288,1024]{1,0:T(8,128)}, f32[288,1024]{1,0:T(8,128)}) custom-call(s32[2]{0:T(128)S(1)} %pad_add_fusion.1.kept_ref, bf16[288,1024]{1,0:T(8,128)(2,1)S(1)} %fusion.81.q_ref, bf16[288,1024]{1,0:T(8,128)(2,1)S(1)} %fusion.78.g_ref, ...), custom_call_target="tpu_custom_call" | custom-call | flops 1698693120 | bytes 11796480 | tf_op jit(solution)/shard_map/pallas_call | solution.py:196
  461.7 7.3 convolution_convert_fusion.refs_2_
  470.7 5.1 fusion.94
  475.8 5.7 convolution_convert_fusion.1.refs_0_
  483.4 12.5 %shard_map.468.refs_4_ = bf16[5632,1024]{1,0:T(8,128)(2,1)} custom-call(bf16[288,1536]{1,0:T(8,128)(2,1)S(1)} %copy-done.4, bf16[288,1024]{1,0:T(8,128)(2,1)S(1)} %add_convert_fusion.gx_ref, bf16[288,4096]{1,0:T(8,128)(2,1)} %copy-done.18, bf16[288,1024]{1,0:T(8,128)(2,1)S(1)} %add_convert_fusion.6.gh_ref), custom_call_target="tpu_custom_call" | custom-call | flops 3321888768 | bytes 14778368 | tf_op jit(solution)/shard_map/pallas_call | solution.py:297
  497.3 211.0 %shard_map.469 = (bf16[128,3072]{1,0:T(8,128)(2,1)}, bf16[128,1024]{1,0:T(8,128)(2,1)}, bf16[128,4096]{1,0:T(8,128)(2,1)}, bf16[128,512]{1,0:T(8,128)(2,1)}, bf1...) custom-call(bf16[1024,3072]{1,0:T(8,128)(2,1)} %convolution_convert_fusion.1.refs_0_, ...), custom_call_target="tpu_custom_call" | custom-call | tf_op jit(solution)/shard_map/pallas_call | solution.py:1158
  719.3 7.6 %multiply_add_fusion.1 = (f32[704,1024]{1,0:T(8,128)}, f32[704,1024]{1,0:T(8,128)S(1)}, f32[704,1024]{1,0:T(8,128)}, f32[704,1024]{1,0:T(8,128)}) fusion(f32[704,1024]{1,0:T(8,128)S(1)} %copy-done.10, f32[704,1024]{1,0:T(8,128)} %refs_3_.1, f32[]{:T(128)S(6)} %min.3, bf16[704,1024]{1,0:T(8,128)(2,1)} %get-tuple-element.99, f32[704,1024]{1,0:T(8,128)} %param.36, ...), kind=kLoop, calls=%fused_computation.49 | loop fusion | flops 14417920 | bytes 24510468 | tf_op jit(solution)/shard_map/add | solution.py:1429
  730.8 7.3 fusion.168
  738.2 2.6 fusion.27
  (381 shorter events, 95.4 us)
Async XLA Ops:
  2.7 7.7 %collective-permute-start = (s32[1537]{0:T(1024)S(1)}, s32[1537]{0:T(1024)S(1)}, u32[]{:S(2)}, u32[]{:S(2)}) collective-permute-start(s32[1537]{0:T(1024)S(1)} %pad_add_fusion), channel_id=1, source_target_pairs={{0,1},{1,0},{2,3},{3,2},{4,5},{5,4},{6,7},{7,6},{8,9},{9,8},{10,11... | collective-permute-start | bytes 18452 | tf_op jit(solution)/shard_map/ppermute | solution.py:252
  263.7 27.8 %copy-start.6 = (f32[288,1024]{1,0:T(8,128)}, f32[288,1024]{1,0:T(8,128)S(1)}, u32[]{:S(2)}) copy-start(f32[288,1024]{1,0:T(8,128)S(1)} %get-tuple-element.198) | copy-start | bytes 3538948
  266.4 28.5 %copy-start.49 = (f32[1024]{0:T(1024)}, f32[1024]{0:T(1024)S(1)}, u32[]{:S(2)}) copy-start(f32[1024]{0:T(1024)S(1)} %get-tuple-element.145) | copy-start | bytes 12292
  266.4 38.9 %copy-start.71 = (f32[1024]{0:T(1024)}, f32[1024]{0:T(1024)S(1)}, u32[]{:S(2)}) copy-start(f32[1024]{0:T(1024)S(1)} %get-tuple-element.144) | copy-start | bytes 12292
  270.5 10.1 %collective-permute-start.1 = (bf16[288,2048]{1,0:T(8,128)(2,1)S(1)}, bf16[288,2048]{1,0:T(8,128)(2,1)}, u32[]{:S(2)}, u32[]{:S(2)}) collective-permute-start(bf16[288,2048]{1,0:T(8,128)(2,1)S(1)} %fusion.40.k0_ref.v0_ref), channel_id=1, source_target_pairs={{0,1},{1,0},{2,3},{3,2},{4,5},{5,4},{6,7},{7,6},{8,9},{9,8},{10,11... | collective-permute-start | bytes 3538952 | tf_op jit(solution)/shard_map/ppermute | solution.py:252
  274.8 31.0 %copy-start.74 = (pred[768]{0:T(1024)(128)(4,1)}, pred[768]{0:T(1024)(128)(4,1)S(1)}, u32[]{:S(2)}) copy-start(pred[768]{0:T(1024)(128)(4,1)S(1)} %iota_compare_fusion.2) | copy-start | bytes 2308
  275.4 31.4 %copy-start.58 = (f32[384]{0:T(512)}, f32[384]{0:T(512)S(1)}, u32[]{:S(2)}) copy-start(f32[384]{0:T(512)S(1)} %get-tuple-element.149) | copy-start | bytes 4612
  309.8 27.2 %copy-start.5 = (bf16[768,768]{1,0:T(8,128)(2,1)}, bf16[768,768]{1,0:T(8,128)(2,1)S(1)}, u32[]{:S(2)}) copy-start(bf16[768,768]{1,0:T(8,128)(2,1)S(1)} %convolution_convert_fusion.7.k0_ref.v0_ref) | copy-start | bytes 3538948
  309.8 6.1 collective-permute-start.2
  315.9 21.1 %copy-start.41 = (bf16[384,4096]{1,0:T(8,128)(2,1)S(1)}, bf16[384,4096]{1,0:T(8,128)(2,1)}, u32[]{:S(2)}) copy-start(bf16[384,4096]{1,0:T(8,128)(2,1)} %get-tuple-element.78) | copy-start | bytes 9437188
  395.4 10.7 %collective-permute-start.3 = (f32[768,384]{1,0:T(8,128)}, f32[768,384]{1,0:T(8,128)S(1)}, u32[]{:S(2)}, u32[]{:S(2)}) collective-permute-start(f32[768,384]{1,0:T(8,128)} %get-tuple-element.85), channel_id=1, source_target_pairs={{0,1},{1,0},{2,3},{3,2},{4,5},{5,4},{6,7},{7,6},{8,9},{9,8},{10,11... | collective-permute-start | bytes 3538952 | tf_op jit(solution)/shard_map/ppermute | solution.py:252
  400.6 5.8 collective-permute-start.4
  438.4 18.8 %copy-start.16 = (bf16[384,1536]{1,0:T(8,128)(2,1)S(1)}, bf16[384,1536]{1,0:T(8,128)(2,1)}, u32[]{:S(2)}) copy-start(bf16[384,1536]{1,0:T(8,128)(2,1)} %convolution_convert_fusion.4) | copy-start | bytes 3538948
  438.4 18.8 %copy-start.24 = (bf16[384,1152]{1,0:T(8,128)(2,1)S(1)}, bf16[384,1152]{1,0:T(8,128)(2,1)}, u32[]{:S(2)}) copy-start(bf16[384,1152]{1,0:T(8,128)(2,1)} %convolution_convert_fusion.5) | copy-start | bytes 2654212
  438.4 18.8 %copy-start.27 = (bf16[384,1024]{1,0:T(8,128)(2,1)S(1)}, bf16[384,1024]{1,0:T(8,128)(2,1)}, u32[]{:S(2)}) copy-start(bf16[384,1024]{1,0:T(8,128)(2,1)} %convolution_convert_fusion.8) | copy-start | bytes 2359300
  438.4 18.8 %copy-start.36 = (bf16[384,384]{1,0:T(8,128)(2,1)S(1)}, bf16[384,384]{1,0:T(8,128)(2,1)}, u32[]{:S(2)}) copy-start(bf16[384,384]{1,0:T(8,128)(2,1)} %convolution_convert_fusion.16) | copy-start | bytes 884740
  456.7 12.3 %collective-permute-start.5 = (f32[288,1024]{1,0:T(8,128)}, f32[288,1024]{1,0:T(8,128)S(1)}, u32[]{:S(2)}, u32[]{:S(2)}) collective-permute-start(f32[288,1024]{1,0:T(8,128)} %get-tuple-element.91), channel_id=1, source_target_pairs={{0,1},{1,0},{2,3},{3,2},{4,5},{5,4},{6,7},{7,6},{8,9},{9,8},{10,11... | collective-permute-start | bytes 3538952 | tf_op jit(solution)/shard_map/ppermute | solution.py:252
  457.0 12.3 %collective-permute-start.6 = (f32[288,1024]{1,0:T(8,128)}, f32[288,1024]{1,0:T(8,128)S(1)}, u32[]{:S(2)}, u32[]{:S(2)}) collective-permute-start(f32[288,1024]{1,0:T(8,128)} %get-tuple-element.93), channel_id=1, source_target_pairs={{0,1},{1,0},{2,3},{3,2},{4,5},{5,4},{6,7},{7,6},{8,9},{9,8},{10,11... | collective-permute-start | bytes 3538952 | tf_op jit(solution)/shard_map/ppermute | solution.py:252
  483.4 12.5 %copy-start.91 = (f32[48]{0:T(128)S(1)}, f32[48]{0:T(128)}, u32[]{:S(2)}) copy-start(f32[48]{0:T(128)} %pad.55.clone) | copy-start | bytes 580
  497.2 220.8 %copy-start.77 = (f32[128,3]{0,1:T(4,128)S(1)}, f32[128,3]{0,1:T(4,128)}, u32[]{:S(2)}) copy-start(f32[128,3]{0,1:T(4,128)} %param.33) | copy-start | bytes 4612
  497.2 220.8 %copy-start.79 = (f32[128,3]{0,1:T(4,128)S(1)}, f32[128,3]{0,1:T(4,128)}, u32[]{:S(2)}) copy-start(f32[128,3]{0,1:T(4,128)} %param.49) | copy-start | bytes 4612
  497.2 220.8 %copy-start.87 = (f32[128,3]{0,1:T(4,128)S(1)}, f32[128,3]{0,1:T(4,128)}, u32[]{:S(2)}) copy-start(f32[128,3]{0,1:T(4,128)} %param.39) | copy-start | bytes 4612
  497.2 220.8 %copy-start.88 = (f32[128,3]{0,1:T(4,128)S(1)}, f32[128,3]{0,1:T(4,128)}, u32[]{:S(2)}) copy-start(f32[128,3]{0,1:T(4,128)} %param.45) | copy-start | bytes 4612
  497.2 222.0 %copy-start.10 = (f32[704,1024]{1,0:T(8,128)S(1)}, f32[704,1024]{1,0:T(8,128)}, u32[]{:S(2)}) copy-start(f32[704,1024]{1,0:T(8,128)} %refs_1_.1) | copy-start | bytes 8650756
  (91 other events, 383.6 us)

commit v6 on v5

--- a/solution.py
+++ b/solution.py
@@ -396,19 +396,36 @@
         index = (a * (zn - 1) + step - 1) * 2 + (0 if upward else 1)
         return copy(src, block(outs[a], a, source_z, section), z_send, z_recv, index, device)
 
+    def beside(a, step, upward):
+        device = ahead if upward else behind
+        source_z = z - (step - 1) if upward else z + (step - 1)
+        rows = (0, line_rows(a))
+        quarter = (far["section"] + 1 - 2 * (far["section"] % 2)) % 4
+        target = block(outs[a], a, source_z, quarter, rows)
+        width = stages[a].shape[1] // 4
+        src = (
+            stages[a].at[pl.ds(0, rows[1]), pl.ds(pl.multiple_of(quarter * width, 128), width)]
+            if step == 1
+            else target
+        )
+        index = (a * (zn - 1) + step - 1) * 2 + (0 if upward else 1) + count * (zn - 1) * 2
+        return copy(src, target, z_send, z_recv, index, device)
+
     def sends_along(step, upward):
         if upward:
             return (z - (step - 1) >= 0) & (z < zn - 1)
         return (z + (step - 1) <= zn - 1) & (z > 0)
 
+    def line_rows(a):
+        return stages[a].shape[0] // 16 // 3 * 16
+
     def first_half(a):
-        size = stages[a].shape[0]
-        return (0, (size + 31) // 32 * 16)
+        start = line_rows(a)
+        return (start, (stages[a].shape[0] - start + 31) // 32 * 16)
 
     def second_half(a):
-        size = stages[a].shape[0]
-        start = (size + 31) // 32 * 16
-        return (start, size - start)
+        start = sum(first_half(a))
+        return (start, stages[a].shape[0] - start)
 
     def in_plane(a, step, upward, kind):
         owner_z = z - step if upward else z + step
@@ -429,6 +446,8 @@
             @pl.when(sends_along(1, upward))
             def _(upward=upward):
                 along(a, 1, upward).start()
+                if line_rows(a):
+                    beside(a, 1, upward).start()
 
     own = []
     settled = []
@@ -479,6 +498,18 @@
                 along(a, step + 1, upward).start()
 
     def passed_on(a, step, upward):
+        if line_rows(a):
+
+            @pl.when(arrives(step, upward))
+            def _():
+                beside(a, step, upward).wait_recv()
+
+            if step < zn - 1:
+
+                @pl.when(arrives(step, upward) & sends_along(step + 1, upward))
+                def _():
+                    beside(a, step + 1, upward).start()
+
         @pl.when(arrives(step, upward))
         def _():
             in_plane(a, step, upward, 0).wait_recv()
@@ -497,7 +528,7 @@
     group = 2 * (zn - 1)
 
     def advance(i):
-        if i % group == 0 and 2 <= i // group + 1 < count:
+        if i % group == group // 2 and 2 <= i // group + 1 < count:
             offered(i // group + 1)
         if 0 <= i - 2 * lag < len(items):
             completed(*items[i - 2 * lag])
@@ -645,7 +676,7 @@
     settle(WIDE)
 
     rest = list(range(ends[WIDE], last))
-    cuts = [len(rest) * part // 80 for part in (0, 8, 12, 48, 54, 80)]
+    cuts = [len(rest) * part // 80 for part in (0, 6, 9, 42, 48, 80)]
     rest = [rest[cuts[i] : cuts[i + 1]] for i in range(5)]
     whole_rows = pl.ds(0, D)
 
@@ -721,6 +752,8 @@
         @pl.when(sends_along(step, upward))
         def _(a=a, step=step, upward=upward):
             along(a, step, upward).wait_send()
+            if line_rows(a):
+                beside(a, step, upward).wait_send()
 
         @pl.when(arrives(step, upward))
         def _(a=a, step=step, upward=upward):
@@ -779,8 +812,8 @@
         ]
         + [
             pltpu.SemaphoreType.DMA((count,)),
-            pltpu.SemaphoreType.DMA((count * (zn - 1) * 2,)),
-            pltpu.SemaphoreType.DMA((count * (zn - 1) * 2,)),
+            pltpu.SemaphoreType.DMA((count * (zn - 1) * 4,)),
+            pltpu.SemaphoreType.DMA((count * (zn - 1) * 4,)),
             pltpu.SemaphoreType.DMA((count * ((zn - 1) * 10 + 1),)),
             pltpu.SemaphoreType.DMA((count * ((zn - 1) * 10 + 1),)),
             pltpu.SemaphoreType.DMA((8,)),
@@ -1332,14 +1365,14 @@
     grad_stream, grad_pup, branch_grad, grad_pg1 = feed_back(
         stream_e, pred_gain[:, 1], pred_feed[0], pred_feed[1], stored_e, grad_stream
     )
-    grad_down = inner_rows(stored_e[2], branch_grad)
+    grad_down = inner_rows(stored_e[2], jnp.pad(branch_grad, ((0, 0), (0, LANES))))
     grad_stream = grad_stream.astype(jnp.bfloat16).astype(jnp.float32)
     grad_stream, grad_pin, grad_pout, grad_pg0 = attend_back(
         stream_d, pred_gain[:, 0], pred_attn[0], pred_attn[1], PH, None, SKIP, HALF - SKIP, stored_d, grad_stream
     )
     grad_token = jnp.sum(jnp.where(context, 0.0, grad_stream), axis=0)
     grad_projected = jnp.where(context, grad_stream, 0.0)[:SEEN].astype(jnp.bfloat16)
-    grad_embed = inner_rows(encoded, grad_projected)
+    grad_embed = inner_rows(encoded, jnp.pad(grad_projected, ((0, 0), (0, LANES))))
     grad_encoded = outer_rows(grad_projected, pred_embed).astype(jnp.bfloat16).astype(jnp.float32)
     grad_stream, grad_eg2 = scaled_back(stream_c, enc_gain[:, 2], grad_encoded)
     grad_stream, grad_eup, branch_grad, grad_eg1 = feed_back(
@@ -1370,10 +1403,10 @@
             grad_ein,
             grad_eout,
             grad_eup,
-            jnp.pad(grad_embed, ((0, 0), (0, LANES))),
+            grad_embed,
             grad_tall,
             jnp.concatenate(shortened([grad_pin, grad_pout, grad_pup, grad_head]), axis=1).reshape(pred_form),
-            jnp.pad(grad_down, ((0, 0), (0, LANES))),
+            grad_down,
         )
     )
     *summed, tally = reduce_blocks(

time: 751 us -> 735 us (0.979)
  Pallas kernels: 561 us -> 545 us
    pallas_call x1, Pallas kernels: 248 us -> 235 us  [gather_and_teach(): pl.pallas_call(functools.partial(gather_kernel, count, zn), in_specs=[pl....]
where the time goes in v6:
time: 735 us; the launch traced here: 731 us
  Pallas kernels  545 us (74%)
  matrix products  96.4 us (13%)
  other arithmetic  52.9 us (7%)
  local copies, waits for them, and re-layouts  27.8 us (4%)
    pallas_call x1, Pallas kernels, gather_and_teach(): pl.pallas_call(functools.partial(gather_kernel, count, zn), in_specs=[pl....  235 us
    pallas_call x1, Pallas kernels, reduce_blocks(): pl.pallas_call(functools.partial(reduce_kernel, count, zn), in_specs=[any...  208 us
    pallas_call x2, Pallas kernels, attend_rows_back(): pl.pallas_call(functools.partial(attend_back_kernel, width // num_heads,...  58.2 us
    dot_general x13, matrix products, matmul(): return jnp.dot(left, right, preferred_element_type=jnp.float32)  34.7 us
    dot_general x10, matrix products, outer_rows(): lax.dot_general(left, right, (((1,), (1,)), ((), ())), preferred_element_...  33.1 us
    pallas_call x2, Pallas kernels, attend_rows(): pl.pallas_call(functools.partial(attend_kernel, width // num_heads, maske...  31.6 us
    dot_general x9, matrix products, inner_rows(): lax.dot_general(left, right, (((0,), (0,)), ((), ())), preferred_element_...  28.6 us
  transfers between devices with their start and end apart: 7, of which 0 were waited for; matrix products, arithmetic and copies ran while one was open for 6% of the time, Pallas kernels for 0%

profile of v6, /device:TPU:0, one launch (start us, length us, event | category | flops | bytes accessed | tf_op | source)
XLA Modules:
  0.0 730.6 jit_solution(14616050868827150900)
XLA Ops:
  12.4 234.7 %shard_map.463 = (bf16[1024,512]{1,0:T(8,128)(2,1)}, bf16[5632,1024]{1,0:T(8,128)(2,1)}, bf16[1024,8192]{1,0:T(8,128)(2,1)}, bf16[5632,1024]{1,0:T(8,128)(2,1)},...) custom-call(bf16[128,512]{1,0:T(8,128)(2,1)} %concatenate.41.refs_0_, ...), custom_call_target="tpu_custom_call" | custom-call | tf_op jit(solution)/shard_map/pallas_call | solution.py:773
  247.0 3.7 fusion.175
  253.8 3.8 fusion.40.k0_ref.v0_ref
  261.7 2.8 multiply_sine_fusion
  267.0 10.8 %shard_map.464 = (bf16[288,1024]{1,0:T(8,128)(2,1)S(1)}, f32[288,1024]{1,0:T(8,128)S(1)}) custom-call(s32[2]{0:T(128)S(1)} %pad_add_fusion.1.kept_ref, bf16[288,1024]{1,0:T(8,128)(2,1)S(1)} %fusion.81.q_ref, bf16[288,2048]{1,0:T(8,128)(2,1)S(1)} %fusion.40.k0_ref.v0_ref, bf16[288,2048]{1,0:T(8,128)(2,1)S(1)} %fusion.40.k0_ref.v0_ref, ...), custom_call_target="tpu_custom_call" | custom-call | flops 679477248 | bytes 4718592 | tf_op jit(solution)/shard_map/pallas_call | solution.py:124
  277.8 3.0 convert_reduce_fusion
  281.2 6.9 multiply_convert_fusion
  288.2 2.8 fusion.176
  302.1 20.8 %shard_map.465 = (bf16[672,384]{1,0:T(8,128)(2,1)S(1)}, f32[672,384]{1,0:T(8,128)S(1)}) custom-call(s32[2]{0:T(128)S(1)} %broadcast.346.kept_ref, bf16[672,384]{1,0:T(8,128)(2,1)S(1)} %convolution_convert_fusion.14.q_ref, bf16[768,768]{1,0:T(8,128)(2,1)S(1)} %convolution_convert_fusion.7.k0_ref.v0_ref, ...), custom_call_target="tpu_custom_call" | custom-call | flops 1585446912 | bytes 4423680 | tf_op jit(solution)/shard_map/pallas_call | solution.py:124
  327.6 4.7 select_reduce_fusion
  336.8 2.6 fusion.113
  342.0 39.8 %shard_map.466 = (bf16[672,384]{1,0:T(8,128)(2,1)S(1)}, f32[768,384]{1,0:T(8,128)S(1)}, f32[768,384]{1,0:T(8,128)}, f32[768,384]{1,0:T(8,128)}, f32[768,384]{1,0:T(8,128)}) custom-call(s32[2]{0:T(128)S(1)} %broadcast.346.kept_ref, bf16[672,384]{1,0:T(8,128)(2,1)S(1)} %convolution_convert_fusion.14.q_ref, ...), custom_call_target="tpu_custom_call" | custom-call | flops 3963617280 | bytes 11501568 | tf_op jit(solution)/shard_map/pallas_call | solution.py:196
  382.4 3.2 convolution_convert_fusion.9
  404.6 8.7 %fusion.19 = bf16[288,4096]{1,0:T(8,128)(2,1)} fusion(bf16[288,1024]{1,0:T(8,128)(2,1)S(1)} %add_convert_fusion.6.gh_ref, bf16[5632,1024]{1,0:T(8,128)(2,1)} %get-tuple-element.73, f32[288,4096]{1,0:T(8,128)} %get-tuple-element.202), kind=kOutput, calls=%fused_computation.18 | convolution fusion | flops 2430074880 | bytes 16056320 | tf_op jit(solution)/shard_map/dot_general | solution.py:73
  414.8 4.7 fusion.102
  423.3 18.4 %shard_map.467 = (bf16[288,1024]{1,0:T(8,128)(2,1)S(1)}, f32[288,1024]{1,0:T(8,128)S(1)}, f32[288,1024]{1,0:T(8,128)}, f32[288,1024]{1,0:T(8,128)}, f32[288,1024]{1,0:T(8,128)}) custom-call(s32[2]{0:T(128)S(1)} %pad_add_fusion.1.kept_ref, bf16[288,1024]{1,0:T(8,128)(2,1)S(1)} %fusion.81.q_ref, bf16[288,1024]{1,0:T(8,128)(2,1)S(1)} %fusion.78.g_ref, ...), custom_call_target="tpu_custom_call" | custom-call | flops 1698693120 | bytes 11796480 | tf_op jit(solution)/shard_map/pallas_call | solution.py:196
  448.5 7.2 convolution_convert_fusion.refs_2_
  457.4 5.1 fusion.94
  462.5 5.8 convolution_convert_fusion.1.refs_0_
  470.1 12.5 %shard_map.468.refs_4_ = bf16[5632,1024]{1,0:T(8,128)(2,1)} custom-call(bf16[288,1536]{1,0:T(8,128)(2,1)S(1)} %copy-done.4, bf16[288,1024]{1,0:T(8,128)(2,1)S(1)} %add_convert_fusion.gx_ref, bf16[288,4096]{1,0:T(8,128)(2,1)} %copy-done.18, bf16[288,1024]{1,0:T(8,128)(2,1)S(1)} %add_convert_fusion.6.gh_ref), custom_call_target="tpu_custom_call" | custom-call | flops 3321888768 | bytes 14778368 | tf_op jit(solution)/shard_map/pallas_call | solution.py:297
  484.0 207.9 %shard_map.469 = (bf16[128,3072]{1,0:T(8,128)(2,1)}, bf16[128,1024]{1,0:T(8,128)(2,1)}, bf16[128,4096]{1,0:T(8,128)(2,1)}, bf16[128,512]{1,0:T(8,128)(2,1)}, bf1...) custom-call(bf16[1024,3072]{1,0:T(8,128)(2,1)} %convolution_convert_fusion.1.refs_0_, ...), custom_call_target="tpu_custom_call" | custom-call | tf_op jit(solution)/shard_map/pallas_call | solution.py:1191
  702.9 7.6 %multiply_add_fusion.1 = (f32[704,1024]{1,0:T(8,128)}, f32[704,1024]{1,0:T(8,128)S(1)}, f32[704,1024]{1,0:T(8,128)}, f32[704,1024]{1,0:T(8,128)}) fusion(f32[704,1024]{1,0:T(8,128)S(1)} %copy-done.10, f32[704,1024]{1,0:T(8,128)} %refs_3_.1, f32[]{:T(128)S(6)} %min.3, bf16[704,1024]{1,0:T(8,128)(2,1)} %get-tuple-element.99, f32[704,1024]{1,0:T(8,128)} %param.36, ...), kind=kLoop, calls=%fused_computation.50 | loop fusion | flops 14417920 | bytes 24510468 | tf_op jit(solution)/shard_map/add | solution.py:1462
  714.4 7.3 fusion.170
  721.8 2.6 fusion.27
  (376 shorter events, 96.7 us)
Async XLA Ops:
  2.7 7.7 %collective-permute-start = (s32[1537]{0:T(1024)S(1)}, s32[1537]{0:T(1024)S(1)}, u32[]{:S(2)}, u32[]{:S(2)}) collective-permute-start(s32[1537]{0:T(1024)S(1)} %pad_add_fusion), channel_id=1, source_target_pairs={{0,1},{1,0},{2,3},{3,2},{4,5},{5,4},{6,7},{7,6},{8,9},{9,8},{10,11... | collective-permute-start | bytes 18452 | tf_op jit(solution)/shard_map/ppermute | solution.py:252
  250.7 27.1 %copy-start.6 = (f32[288,1024]{1,0:T(8,128)}, f32[288,1024]{1,0:T(8,128)S(1)}, u32[]{:S(2)}) copy-start(f32[288,1024]{1,0:T(8,128)S(1)} %get-tuple-element.198) | copy-start | bytes 3538948
  253.5 27.7 %copy-start.48 = (f32[1024]{0:T(1024)}, f32[1024]{0:T(1024)S(1)}, u32[]{:S(2)}) copy-start(f32[1024]{0:T(1024)S(1)} %get-tuple-element.145) | copy-start | bytes 12292
  253.5 37.8 %copy-start.69 = (f32[1024]{0:T(1024)}, f32[1024]{0:T(1024)S(1)}, u32[]{:S(2)}) copy-start(f32[1024]{0:T(1024)S(1)} %get-tuple-element.144) | copy-start | bytes 12292
  257.6 9.3 %collective-permute-start.1 = (bf16[288,2048]{1,0:T(8,128)(2,1)S(1)}, bf16[288,2048]{1,0:T(8,128)(2,1)}, u32[]{:S(2)}, u32[]{:S(2)}) collective-permute-start(bf16[288,2048]{1,0:T(8,128)(2,1)S(1)} %fusion.40.k0_ref.v0_ref), channel_id=1, source_target_pairs={{0,1},{1,0},{2,3},{3,2},{4,5},{5,4},{6,7},{7,6},{8,9},{9,8},{10,11... | collective-permute-start | bytes 3538952 | tf_op jit(solution)/shard_map/ppermute | solution.py:252
  261.1 30.8 %copy-start.71 = (pred[768]{0:T(1024)(128)(4,1)}, pred[768]{0:T(1024)(128)(4,1)S(1)}, u32[]{:S(2)}) copy-start(pred[768]{0:T(1024)(128)(4,1)S(1)} %iota_compare_fusion.2) | copy-start | bytes 2308
  261.7 31.1 %copy-start.57 = (f32[384]{0:T(512)}, f32[384]{0:T(512)S(1)}, u32[]{:S(2)}) copy-start(f32[384]{0:T(512)S(1)} %get-tuple-element.149) | copy-start | bytes 4612
  295.8 27.2 %copy-start.5 = (bf16[768,768]{1,0:T(8,128)(2,1)}, bf16[768,768]{1,0:T(8,128)(2,1)S(1)}, u32[]{:S(2)}) copy-start(bf16[768,768]{1,0:T(8,128)(2,1)S(1)} %convolution_convert_fusion.7.k0_ref.v0_ref) | copy-start | bytes 3538948
  295.8 6.3 collective-permute-start.2
  302.1 20.9 %copy-start.40 = (bf16[384,4096]{1,0:T(8,128)(2,1)S(1)}, bf16[384,4096]{1,0:T(8,128)(2,1)}, u32[]{:S(2)}) copy-start(bf16[384,4096]{1,0:T(8,128)(2,1)} %get-tuple-element.78) | copy-start | bytes 9437188
  381.8 9.9 %collective-permute-start.3 = (f32[768,384]{1,0:T(8,128)}, f32[768,384]{1,0:T(8,128)S(1)}, u32[]{:S(2)}, u32[]{:S(2)}) collective-permute-start(f32[768,384]{1,0:T(8,128)} %get-tuple-element.85), channel_id=1, source_target_pairs={{0,1},{1,0},{2,3},{3,2},{4,5},{5,4},{6,7},{7,6},{8,9},{9,8},{10,11... | collective-permute-start | bytes 3538952 | tf_op jit(solution)/shard_map/ppermute | solution.py:252
  382.1 9.7 %collective-permute-start.4 = (f32[768,384]{1,0:T(8,128)}, f32[768,384]{1,0:T(8,128)S(1)}, u32[]{:S(2)}, u32[]{:S(2)}) collective-permute-start(f32[768,384]{1,0:T(8,128)} %get-tuple-element.87), channel_id=1, source_target_pairs={{0,1},{1,0},{2,3},{3,2},{4,5},{5,4},{6,7},{7,6},{8,9},{9,8},{10,11... | collective-permute-start | bytes 3538952 | tf_op jit(solution)/shard_map/ppermute | solution.py:252
  423.2 19.0 %copy-start.16 = (bf16[384,1536]{1,0:T(8,128)(2,1)S(1)}, bf16[384,1536]{1,0:T(8,128)(2,1)}, u32[]{:S(2)}) copy-start(bf16[384,1536]{1,0:T(8,128)(2,1)} %convolution_convert_fusion.4) | copy-start | bytes 3538948
  423.2 18.9 %copy-start.24 = (bf16[384,1152]{1,0:T(8,128)(2,1)S(1)}, bf16[384,1152]{1,0:T(8,128)(2,1)}, u32[]{:S(2)}) copy-start(bf16[384,1152]{1,0:T(8,128)(2,1)} %convolution_convert_fusion.5) | copy-start | bytes 2654212
  423.3 18.9 %copy-start.27 = (bf16[384,1024]{1,0:T(8,128)(2,1)S(1)}, bf16[384,1024]{1,0:T(8,128)(2,1)}, u32[]{:S(2)}) copy-start(bf16[384,1024]{1,0:T(8,128)(2,1)} %convolution_convert_fusion.9) | copy-start | bytes 2359300
  423.3 18.9 %copy-start.36 = (bf16[384,384]{1,0:T(8,128)(2,1)S(1)}, bf16[384,384]{1,0:T(8,128)(2,1)}, u32[]{:S(2)}) copy-start(bf16[384,384]{1,0:T(8,128)(2,1)} %convolution_convert_fusion.16) | copy-start | bytes 884740
  441.7 14.1 %collective-permute-start.5 = (f32[288,1024]{1,0:T(8,128)}, f32[288,1024]{1,0:T(8,128)S(1)}, u32[]{:S(2)}, u32[]{:S(2)}) collective-permute-start(f32[288,1024]{1,0:T(8,128)} %get-tuple-element.91), channel_id=1, source_target_pairs={{0,1},{1,0},{2,3},{3,2},{4,5},{5,4},{6,7},{7,6},{8,9},{9,8},{10,11... | collective-permute-start | bytes 3538952 | tf_op jit(solution)/shard_map/ppermute | solution.py:252
  441.9 14.1 %collective-permute-start.6 = (f32[288,1024]{1,0:T(8,128)}, f32[288,1024]{1,0:T(8,128)S(1)}, u32[]{:S(2)}, u32[]{:S(2)}) collective-permute-start(f32[288,1024]{1,0:T(8,128)} %get-tuple-element.93), channel_id=1, source_target_pairs={{0,1},{1,0},{2,3},{3,2},{4,5},{5,4},{6,7},{7,6},{8,9},{9,8},{10,11... | collective-permute-start | bytes 3538952 | tf_op jit(solution)/shard_map/ppermute | solution.py:252
  470.1 12.5 %copy-start.87 = (f32[48]{0:T(128)S(1)}, f32[48]{0:T(128)}, u32[]{:S(2)}) copy-start(f32[48]{0:T(128)} %pad.53.clone) | copy-start | bytes 580
  483.9 217.7 %copy-start.74 = (f32[128,3]{0,1:T(4,128)S(1)}, f32[128,3]{0,1:T(4,128)}, u32[]{:S(2)}) copy-start(f32[128,3]{0,1:T(4,128)} %param.33) | copy-start | bytes 4612
  484.0 217.7 %copy-start.76 = (f32[128,3]{0,1:T(4,128)S(1)}, f32[128,3]{0,1:T(4,128)}, u32[]{:S(2)}) copy-start(f32[128,3]{0,1:T(4,128)} %param.49) | copy-start | bytes 4612
  484.0 217.7 %copy-start.83 = (f32[128,3]{0,1:T(4,128)S(1)}, f32[128,3]{0,1:T(4,128)}, u32[]{:S(2)}) copy-start(f32[128,3]{0,1:T(4,128)} %param.39) | copy-start | bytes 4612
  484.0 217.7 %copy-start.84 = (f32[128,3]{0,1:T(4,128)S(1)}, f32[128,3]{0,1:T(4,128)}, u32[]{:S(2)}) copy-start(f32[128,3]{0,1:T(4,128)} %param.45) | copy-start | bytes 4612
  484.0 218.9 %copy-start.10 = (f32[704,1024]{1,0:T(8,128)S(1)}, f32[704,1024]{1,0:T(8,128)}, u32[]{:S(2)}) copy-start(f32[704,1024]{1,0:T(8,128)} %refs_1_.1) | copy-start | bytes 8650756
  (88 other events, 405.2 us)
